TPU v7x, 128 devices: a whole 4x4x4 slice. The times are simulated.
128 devices in a mesh: dp: 8 (over z, core), tensor: 16 (over x, y).
Axes of the slice: x: 4, y: 4, z: 4, core: 2. Of those that a mesh axis runs over, the one named last changes fastest.
Arguments:
- hidden: bfloat16 [512, 8192], P('dp'), may hold values from -180 to 180
- weight: bfloat16 [8192, 114688], P(None, ('dp', 'tensor')), may hold values from -4 to 4
- ref_logits: bfloat16 [512, 114688], P(('dp', 'tensor')), may hold values from -867 to 867
- targets: int32 [512], replicated, may hold values from 0 to 114687
- sequence: int32 [512], replicated, may hold values from 0 to 15, never falling along the last dimension, each value on 1 to 64 neighbouring positions
- response: int32 [512], replicated, may hold values 0 or 1
Outputs:
- d_hidden: bfloat16 [512, 8192], P(('dp', 'tensor'))
- loss: float32 [], replicated
Inputs may be any that keep to these rules, and one draw needn't show every extreme that they name: Sequence ids never fall along the tokens; each sequence has 1 to 64 tokens, the longest exactly 64; a sequence with an even id is the chosen response of a pair and the next id its rejected response.
All inputs are finite; a program needn't handle non-finite values.
Results may differ from a plain program's by a relative error of at most 0.012.
Values may be sent and summed in bfloat16 or wider, within the bound.
No kernel may reach another device: no remote copies, remote signals or barrier semaphores. Data moves between devices by JAX's collectives and lax.ppermute only.
A program may use at most 128 MiB of HBM per device.

v0:
```python
import jax
import jax.numpy as jnp
from jax import lax
from jax.sharding import PartitionSpec as P

SEQ_GRP = 2


BETA = 0.05
KL_WEIGHT = 0.1
LOSS_SCALE = 1024.0


def objective_parts(policy, refer, target_hit, stats, sequence, response, n_seq):
    peak, total, cross, ref_peak, ref_total, picked, ref_picked = stats
    log_total = peak + jnp.log(total)
    ref_log_total = ref_peak + jnp.log(ref_total)
    diverge = cross / total - log_total + ref_log_total
    maskf = response.astype(jnp.float32)
    delta = maskf * (picked - log_total - (ref_picked - ref_log_total))
    member = (sequence[:, None] == jnp.arange(n_seq, dtype=jnp.int32)[None, :]).astype(jnp.float32)
    seq_sums = jnp.sum(member * delta[:, None], axis=0)
    margin = BETA * (seq_sums[0::2] - seq_sums[1::2])
    losses = jax.nn.softplus(-margin)
    pull = BETA * jax.nn.sigmoid(-margin)
    seq_grad = jnp.stack([-pull, pull], axis=1).reshape(-1)
    token_grad = jnp.sum(member * seq_grad[None, :], axis=1)
    loss = (jnp.sum(losses) + KL_WEIGHT * jnp.sum(maskf * diverge)) / policy.shape[0]
    probs = jnp.exp(policy - log_total[:, None])
    inner = token_grad[:, None] * (target_hit - probs) + KL_WEIGHT * probs * (
        policy - refer - (log_total - ref_log_total)[:, None] - diverge[:, None]
    )
    grad = LOSS_SCALE * maskf[:, None] * inner
    return (grad.astype(jnp.bfloat16), loss)


def shards(hidden, weight, ref_logits, targets, sequence, response):
    local_cols = weight.shape[1]
    start_col = lax.axis_index(("dp", "tensor")) * local_cols
    policy = jnp.dot(
        lax.all_gather(hidden, "dp", axis=0, tiled=True), weight, preferred_element_type=jnp.float32
    )
    ref_cols = lax.all_to_all(ref_logits, ("dp", "tensor"), split_axis=1, concat_axis=0, tiled=True)
    refer = ref_cols.astype(jnp.float32)
    columns = jnp.arange(local_cols, dtype=jnp.int32)
    target_hit = ((targets - start_col)[:, None] == columns[None, :]).astype(jnp.float32)
    picked = jnp.sum(target_hit * policy, axis=1)
    ref_picked = jnp.sum(target_hit * refer, axis=1)
    peak, ref_peak = lax.pmax((jnp.max(policy, axis=1), jnp.max(refer, axis=1)), ("dp", "tensor"))
    scaled = jnp.exp(policy - peak[:, None])
    total, cross, ref_total, picked, ref_picked = lax.psum(
        (
            jnp.sum(scaled, axis=1),
            jnp.sum(scaled * (policy - refer), axis=1),
            jnp.sum(jnp.exp(refer - ref_peak[:, None]), axis=1),
            picked,
            ref_picked,
        ),
        ("dp", "tensor"),
    )
    stats = (peak, total, cross, ref_peak, ref_total, picked, ref_picked)
    n_seq = SEQ_GRP * lax.axis_size("dp")
    grad, loss = objective_parts(policy, refer, target_hit, stats, sequence, response, n_seq)
    d_hidden = lax.psum_scatter(
        lax.dot_general(grad, weight, (((1,), (1,)), ((), ())), preferred_element_type=jnp.float32),
        ("dp", "tensor"),
        scatter_dimension=0,
        tiled=True,
    )
    return (d_hidden.astype(jnp.bfloat16), loss)


def solution(mesh):
    in_specs = (P("dp", None), P(None, ("dp", "tensor")), P(("dp", "tensor"), None), P(), P(), P())
    out_specs = (P(("dp", "tensor"), None), P())
    return jax.shard_map(shards, mesh=mesh, in_specs=in_specs, out_specs=out_specs, check_vma=False)
```

profile of v0, /device:TPU:1, one launch (start us, length us, event | category | flops | bytes accessed | tf_op | source)
XLA Modules:
  0.0 373.6 jit_solution(14030158223293985244)
XLA Ops:
  7.2 0.0 copy-start.2
  7.2 0.0 all-gather.2.cloned.1.call-start
  7.2 0.7 all-gather.2.cloned.1.call-update
  7.9 11.5 %all-to-all-start = ((bf16[4,128,896]{2,0,1:T(4,128)(2,1)}), bf16[4,128,896]{2,0,1:T(4,128)(2,1)S(1)}, u32[]{:S(2)}, u32[]{:S(2)}) async-start(bf16[4,128,896]{2,0,1:T(4,128)(2,1)} %bitcast.14), calls=%async_computation | async-start | bytes 1835008 | tf_op jit(solution)/shard_map/all_to_all | solution.py:43
  19.4 0.0 copy-done.2
  19.5 0.1 eq.41
  19.6 17.1 %all-to-all-done = bf16[4,128,896]{2,0,1:T(4,128)(2,1)S(1)} async-done(((bf16[4,128,896]{2,0,1:T(4,128)(2,1)}), bf16[4,128,896]{2,0,1:T(4,128)(2,1)S(1)}, u32[]{:S(2)}, u32[]{:S(2)}) %all-to-all-start) | async-done | bytes 917536 | tf_op jit(solution)/shard_map/all_to_all | solution.py:43
  36.7 0.4 bitcast_reduce_fusion
  37.2 0.1 reshape.38
  37.3 1.5 bitcast_convert_fusion
  38.8 1.9 reshape.39
  40.7 29.5 %all-gather.2.cloned.1.call-done = bf16[512,8192]{1,0:T(8,128)(2,1)} async-done(((bf16[64,8192]{1,0:T(8,128)(2,1)}), bf16[512,8192]{1,0:T(8,128)(2,1)}) %all-gather.2.cloned.1.call-update) | async-done | bytes 8388624 | tf_op jit(solution)/shard_map/all_gather | solution.py:41
  70.2 14.8 %fusion.13 = (f32[512]{0:T(512)S(1)}, f32[512,896]{1,0:T(8,128)}) fusion(bf16[512,8192]{1,0:T(8,128)(2,1)} %all-gather.2.cloned.1.call-done, bf16[8192,896]{1,0:T(8,128)(2,1)} %param.7), kind=kOutput, calls=%fused_computation.39 | convolution fusion | flops 7516651008 | bytes 24905728 | tf_op jit(solution)/shard_map/dot_general | solution.py:40
  85.0 63.9 %all-reduce.2 = (f32[512]{0:T(512)S(1)}, f32[512]{0:T(512)S(1)}) all-reduce(f32[512]{0:T(512)S(1)} %get-tuple-element.23, f32[512]{0:T(512)S(1)} %reshape.38), channel_id=1, replica_groups=mesh['dp'=8,'tensor'=16] {'dp','tensor'}, use_global_device_ids=true, to_apply=%region_3.0 | all-reduce | flops 1024 | bytes 8192 | tf_op jit(solution)/shard_map/pmax | solution.py:49
  148.9 0.1 sub.79
  149.0 2.2 select_reduce_fusion
  151.2 0.1 reduce_sum.88
  151.3 0.1 reduce_sum.90
  151.4 0.0 copy-start
  151.4 0.0 copy-start.1
  151.4 2.3 multiply_reduce_fusion
  153.7 63.4 %all-reduce.1 = (f32[512]{0:T(512)S(1)}, f32[512]{0:T(512)S(1)}, f32[512]{0:T(512)S(1)}, f32[512]{0:T(512)S(1)}, f32[512]{0:T(512)S(1)}) all-reduce(f32[512]{0:T(512)S(1)} %get-tuple-element.3, f32[512]{0:T(512)S(1)} %get-tuple-element.2, f32[512]{0:T(512)S(1)} %reduce_sum.90, ...), channel_id=1, replica_groups=mesh['dp'=8,'tensor'=16] {'dp','tensor'}, use_global_device_ids=true, to_apply=%region_5.0 | all-reduce | flops 2560 | bytes 20480 | tf_op jit(solution)/shard_map/psum | solution.py:51
  217.1 0.0 copy-done
  217.1 0.6 multiply_reduce_fusion.1
  217.7 0.0 copy-done.1
  217.7 0.1 select_reduce_fusion.3
  217.9 0.1 slice.7
  218.0 0.1 slice.6
  218.1 0.6 negate_bitcast_fusion
  218.7 0.1 copy.15
  218.8 0.1 mul.92
  218.9 0.1 select_reduce_fusion.2
  219.0 17.0 %fusion.1 = f32[512,8192]{1,0:T(8,128)} fusion(bf16[8192,896]{1,0:T(8,128)(2,1)} %param.7, f32[512,896]{1,0:T(8,128)} %get-tuple-element.24, f32[512]{0:T(512)S(1)} %get-tuple-element.15, f32[512]{0:T(512)S(1)} %get-tuple-element.20, f32[512]{0:T(512)S(1)} %get-tuple-element.16, f32[512]{0:T(512)S(1)} %select_reduce_fusion.2, ...), kind=kOutput, calls=%fused_computation.9 | convolution fusion | flops 7522156544 | bytes 35139584 | tf_op jit(solution)/shard_map/dot_general | solution.py:65
  235.9 126.8 %all-reduce.4 = bf16[512,8192]{1,0:T(8,128)(2,1)} all-reduce(f32[512,8192]{1,0:T(8,128)} %fusion.1), channel_id=2, replica_groups=mesh['dp'=8,'tensor'=16] {'dp','tensor'}, use_global_device_ids=true, to_apply=%region_16.17.clone | all-reduce | flops 4194304 | bytes 25165824
  364.0 1.6 dynamic-slice_convert_fusion
  (3 shorter events, 0.0 us)
Async XLA Ops:
  7.2 12.3 %copy-start.2 = (s32[512]{0:T(512)S(1)}, s32[512]{0:T(512)}, u32[]{:S(2)}) copy-start(s32[512]{0:T(512)} %param.9) | copy-start | bytes 6148
  7.2 63.1 %all-gather.2.cloned.1.call-start = ((), (), s32[]{:S(2)}) async-start(), calls=%async_computation.1 | async-start | bytes 9437184 | tf_op jit(solution)/shard_map/all_gather | solution.py:41
  7.9 28.8 %all-to-all-start = ((bf16[4,128,896]{2,0,1:T(4,128)(2,1)}), bf16[4,128,896]{2,0,1:T(4,128)(2,1)S(1)}, u32[]{:S(2)}, u32[]{:S(2)}) async-start(bf16[4,128,896]{2,0,1:T(4,128)(2,1)} %bitcast.14), calls=%async_computation | async-start | bytes 1835008 | tf_op jit(solution)/shard_map/all_to_all | solution.py:43
  151.4 65.7 %copy-start = (s32[512]{0:T(512)S(1)}, s32[512]{0:T(512)}, u32[]{:S(2)}) copy-start(s32[512]{0:T(512)} %param.11) | copy-start | bytes 6148
  151.4 66.4 %copy-start.1 = (s32[512]{0:T(512)S(1)}, s32[512]{0:T(512)}, u32[]{:S(2)}) copy-start(s32[512]{0:T(512)} %param.10) | copy-start | bytes 6148
Sparse Core Ops, SparseCore 0:
  9.7 60.4 all-gather.1
where the time goes:
time: 375 us; the launch traced here: 374 us
  blocking collectives  254 us (68%)
  waiting for transfers between devices  47.3 us (13%)
  matrix products  31.7 us (8%)
  between operations  16.6 us (4%)
  starting transfers between devices  11.5 us (3%)
  other arithmetic  7.94 us (2%)
  local copies, waits for them, and re-layouts  4.41 us (1%)
    unnamed x1, blocking collectives  127 us
    pmax x1, blocking collectives, shards(): lax.pmax((jnp.max(policy, axis=1), jnp.max(refer, axis=1)), ('dp', 'tenso...  63.9 us
    psum x1, blocking collectives, shards(): lax.psum((jnp.sum(scaled, axis=1), jnp.sum(scaled * (policy - refer), axi...  63.4 us
    all_gather x1, waiting for transfers between devices, shards(): lax.all_gather(hidden, 'dp', axis=0, tiled=True)  29.5 us
    all_to_all x1, waiting for transfers between devices, shards(): lax.all_to_all(ref_logits, ('dp', 'tensor'), split_axis=1, concat_axis=0,...  17.1 us
    dot_general x1, matrix products, shards(): lax.dot_general(grad, weight, (((1,), (1,)), ((), ())), preferred_element...  17 us
    dot_general x1, matrix products, shards(): jnp.dot(lax.all_gather(hidden, 'dp', axis=0, tiled=True), weight, preferr...  14.8 us
    all_to_all x1, starting transfers between devices, shards(): lax.all_to_all(ref_logits, ('dp', 'tensor'), split_axis=1, concat_axis=0,...  11.5 us
  transfers between devices with their start and end apart: 2, of which 2 were waited for; matrix products, arithmetic and copies ran while one was open for 1% of the time, Pallas kernels for 0%

commit v1 on v0

v1 whole, which is shorter than its diff:
```python
import functools

import jax
import jax.numpy as jnp
from jax import lax
from jax.experimental import pallas as pl
from jax.experimental.pallas import tpu as pltpu
from jax.sharding import PartitionSpec as P

BETA = 0.05
KL_WEIGHT = 0.1
LOSS_SCALE = 1024.0
BF16 = jnp.bfloat16
F32 = jnp.float32

RING = 4
CORES = 2
CHIPS = RING * RING


def swap_tensor(value, offset):
    return lax.ppermute(value, "tensor", [(i, i ^ offset) for i in range(CHIPS)])


def swap_z(value, offset):
    return lax.ppermute(value, "dp", [(i, i ^ (offset * CORES)) for i in range(RING * CORES)])


def swap_core(value):
    return lax.ppermute(value, "dp", [(i, i ^ 1) for i in range(RING * CORES)])


def any_spec():
    return pl.BlockSpec(memory_space=pl.ANY)


def params(mib):
    return pltpu.CompilerParams(vmem_limit_bytes=mib * 1024 * 1024)


def place_of(first, second):
    b, e = first >> 1, second >> 1
    return ((first & 1) ^ b) + 2 * b + 4 * ((second & 1) ^ e) + 8 * e


def where_am_i():
    dp, t = lax.axis_index("dp"), lax.axis_index("tensor")
    return dp & 1, t >> 2, t & 3, dp >> 1


def logits_body(*refs):
    (mine, theirs), near, gathered, weight, policy_ref = refs[:2], refs[2:6], refs[6:14], refs[14], refs[15]
    states, pieces, slabs, sems = refs[16:]
    rows = mine.shape[0]
    half = near[0].shape[1]
    depth = half // RING
    width = half // CHIPS
    core, x, y, z = where_am_i()

    def rows_of(dz, side):
        start = (z ^ dz) * (2 * rows) + (core ^ side) * rows
        return pl.ds(pl.multiple_of(start, rows), rows)

    loads = [
        pltpu.make_async_copy(ref, pieces.at[i // 2, pl.ds(8 * (i % 2), 8)], sems.at[i]) for i, ref in enumerate(gathered)
    ]
    slices = []
    for k in range(2 * RING):
        far = k // RING
        here = pl.ds(k * depth, depth)
        there = pl.ds(pl.multiple_of((core ^ far) * half + (k % RING) * depth, depth), depth)
        within = pl.ds((k % RING) * depth, depth)
        moves = [
            (mine.at[:, there], states.at[rows_of(0, 0), here]),
            (theirs.at[:, there], states.at[rows_of(0, 1), here]),
        ]
        for dz, block in ((1, near[2 * far]), (3, near[2 * far + 1])):
            for side in range(CORES):
                moves.append((block.at[pl.ds(side * rows, rows), within], states.at[rows_of(dz, side ^ far), here]))
        moves.append((weight.at[there], slabs.at[k]))
        slices.append([pltpu.make_async_copy(a, b, sems.at[8 + 7 * k + i]) for i, (a, b) in enumerate(moves)])
    for copy in loads[:4] + slices[0] + loads[4:]:
        copy.start()
    for k in range(1, 2 * RING):
        for copy in slices[k]:
            copy.start()
    for far in range(2):
        for copy in loads[4 * far : 4 * far + 4]:
            copy.wait()
        for k in range(RING):
            for j in range(RING):
                at = pl.ds(far * half + (k * RING + j) * width, width)
                states[rows_of(2, far), at] = pieces[2 * far, place_of(y ^ j, x ^ k)]
                states[rows_of(2, 1 - far), at] = pieces[2 * far + 1, place_of(x ^ k, y ^ j)]
        for k in range(far * RING, (far + 1) * RING):
            for copy in slices[k]:
                copy.wait()
            product = jnp.dot(states[:, k * depth : (k + 1) * depth], slabs[k], preferred_element_type=F32)
            policy_ref[...] = product if k == 0 else policy_ref[...] + product


def policy_logits(mine, theirs, near, gathered, weight):
    rows, half = mine.shape[0], near[0].shape[1]
    tokens = rows * CORES * RING
    cols = weight.shape[1]
    width = half // CHIPS
    return pl.pallas_call(
        logits_body,
        out_shape=jax.ShapeDtypeStruct((tokens, cols), F32),
        in_specs=[any_spec()] * 15,
        out_specs=pl.BlockSpec(memory_space=pltpu.VMEM),
        scratch_shapes=[
            pltpu.VMEM((tokens, 2 * half), BF16),
            pltpu.VMEM((4, CHIPS, rows, width), BF16),
            pltpu.VMEM((2 * RING, half // RING, cols), BF16),
            pltpu.SemaphoreType.DMA((8 + 7 * 2 * RING,)),
        ],
        compiler_params=params(52),
        cost_estimate=pl.CostEstimate(
            flops=4 * tokens * half * cols, bytes_accessed=4 * half * (cols + tokens) + 4 * tokens * cols, transcendentals=0
        ),
        name="policy_logits",
    )(mine, theirs, *near, *gathered, weight)


def stats_body(targets_ref, policy_ref, refer_ref, stats_ref):
    rows, cols = policy_ref.shape
    core, x, y, z = where_am_i()
    start_col = (((z * CORES + core) * RING + x) * RING + y) * cols
    local = targets_ref[...].reshape(1, rows) - start_col
    local = jnp.where((local >= 0) & (local < cols), local, -1).astype(F32)
    local = jnp.broadcast_to(local, (128, rows)).T[:, 0:1].astype(jnp.int32)
    policy = policy_ref[...]
    refer = refer_ref[...].astype(F32)
    hit = lax.broadcasted_iota(jnp.int32, (rows, cols), 1) == local
    peak = jnp.max(policy, axis=1, keepdims=True)
    scaled = jnp.exp(policy - peak)
    total = jnp.sum(scaled, axis=1, keepdims=True)
    cross = jnp.sum(scaled * (policy - refer), axis=1, keepdims=True)
    ref_peak = jnp.max(refer, axis=1, keepdims=True)
    ref_total = jnp.sum(jnp.exp(refer - ref_peak), axis=1, keepdims=True)
    picked = jnp.sum(jnp.where(hit, policy, 0.0), axis=1, keepdims=True)
    ref_picked = jnp.sum(jnp.where(hit, refer, 0.0), axis=1, keepdims=True)
    lane = lax.broadcasted_iota(jnp.int32, (rows, 128), 1)
    table = jnp.zeros((rows, 128), F32)
    for k, value in enumerate((peak, total, cross, ref_peak, ref_total, picked, ref_picked)):
        table = jnp.where(lane == k, value, table)
    stats_ref[...] = table.T[:8]


def row_stats(targets, policy, refer):
    tokens, cols = policy.shape
    step = 128
    return pl.pallas_call(
        stats_body,
        grid=(tokens // step,),
        out_shape=jax.ShapeDtypeStruct((8, tokens), F32),
        in_specs=[
            pl.BlockSpec((step,), lambda i: (i,)),
            pl.BlockSpec((step, cols), lambda i: (i, 0)),
            pl.BlockSpec((step, cols), lambda i: (i, 0)),
        ],
        out_specs=pl.BlockSpec((8, step), lambda i: (0, i)),
        compiler_params=params(24),
        cost_estimate=pl.CostEstimate(flops=20 * tokens * cols, bytes_accessed=6 * tokens * cols, transcendentals=2 * tokens * cols),
        name="row_stats",
    )(targets, policy, refer)


def merge(stats):
    table = jnp.stack(stats)
    peak = jnp.max(table[:, 0], axis=0)
    share = jnp.exp(table[:, 0] - peak)
    total = jnp.sum(share * table[:, 1], axis=0)
    cross = jnp.sum(share * table[:, 2], axis=0)
    ref_peak = jnp.max(table[:, 3], axis=0)
    ref_total = jnp.sum(jnp.exp(table[:, 3] - ref_peak) * table[:, 4], axis=0)
    picked = jnp.sum(table[:, 5], axis=0)
    ref_picked = jnp.sum(table[:, 6], axis=0)
    return jnp.stack([peak, total, cross, ref_peak, ref_total, picked, ref_picked, jnp.zeros_like(peak)])


def grad_body(n_seq, stats_ref, targets_ref, sequence_ref, response_ref, policy_ref, refer_ref, by_x_ref, by_y_ref, loss_ref):
    tokens, cols = policy_ref.shape
    core_here, x, y, z = where_am_i()
    start_col = (((z * CORES + core_here) * RING + x) * RING + y) * cols
    stats = stats_ref[...]
    peak, total, cross, ref_peak, ref_total, picked, ref_picked = [stats[k : k + 1] for k in range(7)]
    targets, sequence, response = [ref[...].reshape(1, tokens) for ref in (targets_ref, sequence_ref, response_ref)]
    log_total = peak + jnp.log(total)
    ref_log_total = ref_peak + jnp.log(ref_total)
    mean_gap = cross / total
    diverge = mean_gap - log_total + ref_log_total
    mask = response.astype(F32)
    delta = mask * ((picked - log_total) - (ref_picked - ref_log_total))
    ids = lax.broadcasted_iota(jnp.int32, (n_seq, tokens), 0)
    member = (ids == sequence).astype(F32)
    pair = lax.broadcasted_iota(jnp.int32, (n_seq // 2, tokens), 0)
    side = jnp.where(pair == sequence >> 1, jnp.where((sequence & 1) == 0, 1.0, -1.0), 0.0)
    margin = BETA * jnp.sum(side * delta, axis=1, keepdims=True)
    pull = BETA * jax.nn.sigmoid(-margin)
    token_grad = -jnp.sum(side * pull, axis=0, keepdims=True)
    losses = jnp.maximum(-margin, 0.0) + jnp.log1p(jnp.exp(-jnp.abs(margin)))
    objective = jnp.sum(losses) + KL_WEIGHT * jnp.sum(mask * diverge)
    loss_ref[...] = jnp.full(loss_ref.shape, objective / tokens, F32)

    lift = LOSS_SCALE * mask
    local = targets - start_col
    local = jnp.where((local >= 0) & (local < cols), local, -1).astype(F32)
    rows8 = lax.broadcasted_iota(jnp.int32, (128, tokens), 0)
    packed = jnp.zeros((128, tokens), F32)
    for k, value in enumerate((log_total, mean_gap, lift * token_grad, lift * KL_WEIGHT, local)):
        packed = jnp.where(rows8 == k, value, packed)
    packed = packed.T

    step = 128
    pieces = []
    for i in range(tokens // step):
        span = slice(i * step, (i + 1) * step)
        per_row = packed[span]
        policy = policy_ref[span, :]
        refer = refer_ref[span, :].astype(F32)
        column = lax.broadcasted_iota(jnp.int32, (step, cols), 1)
        hit = (column == per_row[:, 4:5].astype(jnp.int32)).astype(F32)
        probs = jnp.exp(policy - per_row[:, 0:1])
        grad = per_row[:, 2:3] * (hit - probs) + per_row[:, 3:4] * probs * ((policy - refer) - per_row[:, 1:2])
        pieces.append(grad.astype(BF16))
    grad = jnp.concatenate(pieces, axis=0)

    row = lax.broadcasted_iota(jnp.int32, (tokens, tokens), 0)
    token = lax.broadcasted_iota(jnp.int32, (tokens, tokens), 1)
    outer, inner, dz, core, t = row >> 7, (row >> 5) & 3, (row >> 3) & 3, (row >> 2) & 1, row & 3
    base = (z ^ dz) * 128 + core * 64 + t
    for ref, source in (
        (by_x_ref, base + (x ^ outer) * 16 + (y ^ inner) * 4),
        (by_y_ref, base + (x ^ inner) * 16 + (y ^ outer) * 4),
    ):
        pick = (token == source).astype(F32).astype(BF16)
        ref[...] = jnp.dot(pick, grad, preferred_element_type=F32).astype(BF16)


def logit_grads(stats, targets, sequence, response, policy, refer, n_seq):
    tokens, cols = policy.shape
    vmem = pl.BlockSpec(memory_space=pltpu.VMEM)
    return pl.pallas_call(
        functools.partial(grad_body, n_seq),
        out_shape=(
            jax.ShapeDtypeStruct((tokens, cols), BF16),
            jax.ShapeDtypeStruct((tokens, cols), BF16),
            jax.ShapeDtypeStruct((8, 128), F32),
        ),
        in_specs=[vmem] * 6,
        out_specs=(vmem, vmem, vmem),
        compiler_params=params(24),
        cost_estimate=pl.CostEstimate(flops=2 * tokens * tokens * cols, bytes_accessed=10 * tokens * cols, transcendentals=tokens * cols),
        name="logit_grads",
    )(stats, targets, sequence, response, policy, refer)


PARTS = ((True, 1), (True, 3), (False, 1), (False, 3))
SENDS = {1: (1, 2), 3: (3, 2)}
KEEPS = {1: (0, 3), 3: (0, 1)}


def hidden_body(own_x, other_x, own_y, other_y, own_weight, other_weight, *refs):
    outs, (grads, slabs, sems) = refs[:8], refs[8:]
    tokens, cols = own_x.shape
    core = lax.axis_index("dp") & 1
    half = own_weight.shape[0] // CORES
    depth = half // 4
    step = depth // 2
    loads = [
        pltpu.make_async_copy(ref, grads.at[i // 2, :, pl.ds((i % 2) * cols, cols)], sems.at[i])
        for i, ref in enumerate((own_x, other_x, own_y, other_y))
    ]
    fetches = []
    for i in range(8):
        rows = pl.ds(pl.multiple_of(core * half + i * step, step), step)
        fetches.append(
            [
                pltpu.make_async_copy(ref.at[rows], slabs.at[i, :, pl.ds(n * cols, cols)], sems.at[4 + 2 * i + n])
                for n, ref in enumerate((own_weight, other_weight))
            ]
        )
    for copy in loads[:2] + sum(fetches[:4], []) + loads[2:] + sum(fetches[4:], []):
        copy.start()
    quarter = tokens // RING
    for i in range(8):
        part = i // 2
        if i % 4 == 0:
            loads[i // 2].wait()
            loads[i // 2 + 1].wait()
        for copy in fetches[i]:
            copy.wait()
        product = lax.dot_general(
            grads[i // 4], slabs[i], (((1,), (1,)), ((), ())), preferred_element_type=F32
        ).astype(BF16)
        first = PARTS[part][1]
        for ref, order in ((outs[2 * part], SENDS[first]), (outs[2 * part + 1], KEEPS[first])):
            for k, source in enumerate(order):
                ref[k * quarter : (k + 1) * quarter, (i % 2) * step : (i % 2 + 1) * step] = product[
                    source * quarter : (source + 1) * quarter
                ]


def hidden_parts(grads, weight, other_weight):
    tokens, cols = grads[0].shape
    depth = weight.shape[0] // CORES // 4
    vmem = pl.BlockSpec(memory_space=pltpu.VMEM)
    return pl.pallas_call(
        hidden_body,
        out_shape=(jax.ShapeDtypeStruct((tokens // 2, depth), BF16),) * 8,
        in_specs=[any_spec()] * 6,
        out_specs=(vmem,) * 8,
        scratch_shapes=[
            pltpu.VMEM((2, tokens, CORES * cols), BF16),
            pltpu.VMEM((8, depth // 2, CORES * cols), BF16),
            pltpu.SemaphoreType.DMA((20,)),
        ],
        compiler_params=params(52),
        cost_estimate=pl.CostEstimate(
            flops=16 * tokens * depth * cols, bytes_accessed=16 * cols * (tokens + depth) + 8 * tokens * depth, transcendentals=0
        ),
        name="hidden_parts",
    )(*grads, weight, other_weight)


def add(*terms):
    total = terms[0].astype(F32)
    for term in terms[1:]:
        total = total + term.astype(F32)
    return total


def shards(hidden, weight, ref_logits, targets, sequence, response):
    rows, width = hidden.shape
    cols = weight.shape[1]
    half = width // CORES
    piece = half // CHIPS
    dp, t = lax.axis_index("dp"), lax.axis_index("tensor")
    z, core = dp // CORES, dp % CORES
    x, y = t // RING, t % RING

    theirs = swap_core(hidden)
    sent_weight, theirs = lax.optimization_barrier((weight, theirs))
    other_weight = swap_core(sent_weight)
    across = jnp.concatenate(
        [lax.dynamic_slice_in_dim(a, core * half + t * piece, piece, axis=1) for a in (hidden, theirs)], axis=0
    )
    across = swap_z(across, 2)
    sent, across = lax.optimization_barrier(((hidden, theirs), across))
    pair = jnp.concatenate([lax.dynamic_slice_in_dim(a, core * half, half, axis=1) for a in sent], axis=0)
    near = [swap_z(pair, 1), swap_z(pair, 3)]
    by_x, by_y = across[None, :rows], across[None, rows:]
    for step_x, step_y in ((1, 4), (3, 12), (4, 1)):
        by_x, by_y = (
            jnp.concatenate([by_x, swap_tensor(by_x, step_x)], axis=0),
            jnp.concatenate([by_y, swap_tensor(by_y, step_y)], axis=0),
        )
    gathered = [by_x, swap_tensor(by_x, 12), by_y, swap_tensor(by_y, 3)]
    near += [swap_core(a) for a in near]

    ref_logits, gathered = lax.optimization_barrier((ref_logits, gathered))
    refer = lax.all_to_all(
        ref_logits.reshape(ref_logits.shape[0], -1, cols), ("dp", "tensor"), split_axis=1, concat_axis=0
    )

    swapped = [swap_core(a) for a in gathered]
    policy = policy_logits(hidden, theirs, near, gathered + swapped, weight)
    refer, policy = lax.optimization_barrier((refer, policy))
    refer = refer.reshape(policy.shape)
    stats = row_stats(targets, policy, refer)

    for send, steps in (
        (swap_tensor, (1, 2, 3)),
        (swap_tensor, (4, 8, 12)),
        (swap_z, (1, 2, 3)),
    ):
        stats = merge([stats] + [send(stats, o) for o in steps])
    stats = merge([stats, swap_core(stats)])

    grad_x, grad_y, loss = logit_grads(stats, targets, sequence, response, policy, refer, 2 * RING * CORES)
    grads = (grad_x, swap_core(grad_x), grad_y, swap_core(grad_y))

    sums = {4: [], 1: []}
    products = hidden_parts(grads, weight, other_weight)
    for part, (along_x, first) in enumerate(PARTS):
        send, keep = products[2 * part], products[2 * part + 1]
        axis = RING if along_x else 1
        got = swap_tensor(send, axis * first)
        n = keep.shape[0] // 2
        more = swap_tensor(add(keep[n:], got[n:]).astype(BF16), axis * (RING - first))
        sums[axis].append(add(keep[:n], got[:n], more).astype(BF16))
    ends = []
    for axis, cross in ((4, 1), (1, 4)):
        block = jnp.concatenate(sums[axis], axis=1)
        block = block.reshape(RING, block.shape[0] // RING, -1)
        ends.append(add(block[0], *[swap_tensor(block[k], cross * k) for k in (2, 1, 3)]).astype(BF16))
    ends = jnp.concatenate(ends, axis=1).reshape(RING, CORES * RING, half)
    d_half = add(ends[0], *[swap_z(ends[k], k) for k in (2, 1, 3)]).astype(BF16).reshape(CORES, RING, half)
    own_rows = lax.dynamic_index_in_dim(d_half, core, 0, keepdims=False)
    got_rows = swap_core(lax.dynamic_index_in_dim(d_half, 1 - core, 0, keepdims=False))
    d_hidden = jnp.where(
        core == 0, jnp.concatenate([own_rows, got_rows], axis=1), jnp.concatenate([got_rows, own_rows], axis=1)
    )
    return d_hidden, loss[0, 0]


def solution(mesh):
    in_specs = (P("dp", None), P(None, ("dp", "tensor")), P(("dp", "tensor"), None), P(), P(), P())
    out_specs = (P(("dp", "tensor"), None), P())
    return jax.shard_map(shards, mesh=mesh, in_specs=in_specs, out_specs=out_specs, check_vma=False)
```

time: 375 us -> 180 us (0.48)
  blocking collectives: 254 us -> 0 us
  starting transfers between devices: 11.5 us -> 75.6 us
  matrix products: 31.7 us -> 0 us
  Pallas kernels: 0 us -> 30 us
  waiting for transfers between devices: 47.3 us -> 63.1 us
  between operations: 16.6 us -> 1.08 us
    unnamed x1 -> x0, blocking collectives: 127 us -> none
    ppermute x0 -> x49, starting transfers between devices: none -> 68.4 us  [the longest x28 35.4 us: swap_tensor(): lax.ppermute(value, 'tensor', [(i, i ^ offset) for i in range(CHIPS)])]
    pmax x1 -> x0, blocking collectives: 63.9 us -> none  [shards(): lax.pmax((jnp.max(policy, axis=1), jnp.max(refer, axis=1)), ('dp', 'tenso...]
    psum x1 -> x0, blocking collectives: 63.4 us -> none  [shards(): lax.psum((jnp.sum(scaled, axis=1), jnp.sum(scaled * (policy - refer), axi...]
    ppermute x0 -> x49, waiting for transfers between devices: none -> 60 us  [the longest x28 29.3 us: swap_tensor(): lax.ppermute(value, 'tensor', [(i, i ^ offset) for i in range(CHIPS)])]
    dot_general x2 -> x0, matrix products: 31.7 us -> none  [the longest x1 17 us: shards(): lax.dot_general(grad, weight, (((1,), (1,)), ((), ())), preferred_element...]
    pallas_call x0 -> x4, Pallas kernels: none -> 30 us  [the longest x1 13.1 us: policy_logits(): pl.pallas_call(logits_body, out_shape=jax.ShapeDtypeStruct((tokens, cols)...]
    all_gather x1 -> x0, waiting for transfers between devices: 29.5 us -> none  [shards(): lax.all_gather(hidden, 'dp', axis=0, tiled=True)]
  transfers between devices with their start and end apart: 2 -> 50, of which waited for: 2 -> 29; matrix products, arithmetic and copies ran while one was open for 1% -> 4% of each run, Pallas kernels for 0% -> 10%
where the time goes in v1:
time: 180 us
  starting transfers between devices  75.6 us (42%)
  waiting for transfers between devices  63.1 us (35%)
  Pallas kernels  30 us (17%)
  local copies, waits for them, and re-layouts  5.89 us (3%)
  other arithmetic  4.3 us (2%)
    ppermute x28, starting transfers between devices, swap_tensor(): lax.ppermute(value, 'tensor', [(i, i ^ offset) for i in range(CHIPS)])  35.4 us
    ppermute x28, waiting for transfers between devices, swap_tensor(): lax.ppermute(value, 'tensor', [(i, i ^ offset) for i in range(CHIPS)])  29.3 us
    ppermute x9, waiting for transfers between devices, swap_z(): lax.ppermute(value, 'dp', [(i, i ^ offset * CORES) for i in range(RING *...  22.6 us
    ppermute x12, starting transfers between devices, swap_core(): return lax.ppermute(value, 'dp', [(i, i ^ 1) for i in range(RING * CORES)])  20 us
    pallas_call x1, Pallas kernels, policy_logits(): pl.pallas_call(logits_body, out_shape=jax.ShapeDtypeStruct((tokens, cols)...  13.1 us
    ppermute x9, starting transfers between devices, swap_z(): lax.ppermute(value, 'dp', [(i, i ^ offset * CORES) for i in range(RING *...  13 us
    pallas_call x1, Pallas kernels, hidden_parts(): pl.pallas_call(hidden_body, out_shape=(jax.ShapeDtypeStruct((tokens // 2,...  12.3 us
    ppermute x12, waiting for transfers between devices, swap_core(): return lax.ppermute(value, 'dp', [(i, i ^ 1) for i in range(RING * CORES)])  8.13 us
  transfers between devices with their start and end apart: 50, of which 29 were waited for; matrix products, arithmetic and copies ran while one was open for 4% of the time, Pallas kernels for 10%

profile of v1, /device:TPU:1, one launch (start us, length us, event | category | flops | bytes accessed | tf_op | source)
XLA Modules:
  0.0 180.0 jit_solution(1460540547052789355)
XLA Ops:
  0.6 1.5 collective-permute-start
  2.1 2.5 %collective-permute-done.refs_1_ = bf16[64,8192]{1,0:T(8,128)(2,1)S(1)} collective-permute-done((bf16[64,8192]{1,0:T(8,128)(2,1)}, bf16[64,8192]{1,0:T(8,128)(2,1)S(1)}, u32[]{:S(2)}, u32[]{:S(2)}) %collective-permute-start) | collective-permute-done | bytes 1048608 | tf_op jit(solution)/shard_map/ppermute | solution.py:30
  5.8 3.8 %collective-permute-start.1 = (bf16[128,256]{1,0:T(8,128)(2,1)S(1)}, bf16[128,256]{1,0:T(8,128)(2,1)S(1)}, u32[]{:S(2)}, u32[]{:S(2)}) collective-permute-start(bf16[128,256]{1,0:T(8,128)(2,1)S(1)} %pad_maximum_fusion.8), channel_id=1, source_target_pairs={{0,64},{16,80},{32,96},{48,112},{64,0},{80,16},{96,32},{112,48},{1... | collective-permute-start | bytes 196616 | tf_op jit(solution)/shard_map/ppermute | solution.py:26
  9.5 2.4 %collective-permute-done.1 = bf16[128,256]{1,0:T(8,128)(2,1)S(1)} collective-permute-done((bf16[128,256]{1,0:T(8,128)(2,1)S(1)}, bf16[128,256]{1,0:T(8,128)(2,1)S(1)}, u32[]{:S(2)}, u32[]{:S(2)}) %collective-permute-start.1) | collective-permute-done | bytes 65568 | tf_op jit(solution)/shard_map/ppermute | solution.py:26
  13.2 2.9 %collective-permute-start.11 = (bf16[128,4096]{1,0:T(8,128)(2,1)S(1)}, bf16[128,4096]{1,0:T(8,128)(2,1)}, u32[]{:S(2)}, u32[]{:S(2)}) collective-permute-start(bf16[128,4096]{1,0:T(8,128)(2,1)S(1)} %pad_maximum_fusion), channel_id=1, source_target_pairs={{0,96},{16,112},{32,64},{48,80},{64,32},{80,48},{96,0},{112,16},{1... | collective-permute-start | bytes 3145736 | tf_op jit(solution)/shard_map/ppermute | solution.py:26
  16.0 1.4 collective-permute-start.2
  17.4 1.2 collective-permute-start.6
  19.3 2.8 %collective-permute-start.3 = (bf16[2,64,256]{2,1,0:T(8,128)(2,1)S(1)}, bf16[2,64,256]{2,1,0:T(8,128)(2,1)S(1)}, u32[]{:S(2)}, u32[]{:S(2)}) collective-permute-start(bf16[2,64,256]{2,1,0:T(8,128)(2,1)S(1)} %pad_maximum_fusion.9), channel_id=1, source_target_pairs={{0,3},{1,2},{2,1},{3,0},{4,7},{5,6},{6,5},{7,4},{8,11},{9,10},{10,... | collective-permute-start | bytes 196616 | tf_op jit(solution)/shard_map/ppermute | solution.py:22
  22.1 2.6 %collective-permute-start.7 = (bf16[2,64,256]{2,1,0:T(8,128)(2,1)S(1)}, bf16[2,64,256]{2,1,0:T(8,128)(2,1)S(1)}, u32[]{:S(2)}, u32[]{:S(2)}) collective-permute-start(bf16[2,64,256]{2,1,0:T(8,128)(2,1)S(1)} %pad_maximum_fusion.10), channel_id=1, source_target_pairs={{0,12},{1,13},{2,14},{3,15},{4,8},{5,9},{6,10},{7,11},{8,4},{9,5},... | collective-permute-start | bytes 196616 | tf_op jit(solution)/shard_map/ppermute | solution.py:22
  25.5 13.2 %collective-permute-done.11.refs_3_ = bf16[128,4096]{1,0:T(8,128)(2,1)} collective-permute-done((bf16[128,4096]{1,0:T(8,128)(2,1)S(1)}, bf16[128,4096]{1,0:T(8,128)(2,1)}, u32[]{:S(2)}, u32[]{:S(2)}) %collective-permute-start.11) | collective-permute-done | bytes 1048608 | tf_op jit(solution)/shard_map/ppermute | solution.py:26
  38.7 1.6 collective-permute-start.13
  40.3 1.5 collective-permute-start.12
  41.7 1.4 collective-permute-start.8
  43.2 2.6 %collective-permute-start.5 = (bf16[8,64,256]{2,1,0:T(8,128)(2,1)S(1)}, bf16[8,64,256]{2,1,0:T(8,128)(2,1)S(1)}, u32[]{:S(2)}, u32[]{:S(2)}) collective-permute-start(bf16[8,64,256]{2,1,0:T(8,128)(2,1)S(1)} %pad_maximum_fusion.1.refs_6_), channel_id=1, source_target_pairs={{0,12},{1,13},{2,14},{3,15},{4,8},{5,9},{6,10},{7,11},{8,4},{9,5},... | collective-permute-start | bytes 786440 | tf_op jit(solution)/shard_map/ppermute | solution.py:22
  45.7 1.2 collective-permute-done.8
  47.0 2.8 %collective-permute-start.9 = (bf16[8,64,256]{2,1,0:T(8,128)(2,1)S(1)}, bf16[8,64,256]{2,1,0:T(8,128)(2,1)S(1)}, u32[]{:S(2)}, u32[]{:S(2)}) collective-permute-start(bf16[8,64,256]{2,1,0:T(8,128)(2,1)S(1)} %pad_maximum_fusion.2.refs_8_), channel_id=1, source_target_pairs={{0,3},{1,2},{2,1},{3,0},{4,7},{5,6},{6,5},{7,4},{8,11},{9,10},{10,... | collective-permute-start | bytes 786440 | tf_op jit(solution)/shard_map/ppermute | solution.py:22
  49.8 2.3 %collective-permute-done.5.refs_7_ = bf16[8,64,256]{2,1,0:T(8,128)(2,1)S(1)} collective-permute-done((bf16[8,64,256]{2,1,0:T(8,128)(2,1)S(1)}, bf16[8,64,256]{2,1,0:T(8,128)(2,1)S(1)}, u32[]{:S(2)}, u32[]{:S(2)}) %collective-permute-start.5) | collective-permute-done | bytes 262176 | tf_op jit(solution)/shard_map/ppermute | solution.py:22
  52.1 3.4 %collective-permute-done.9.refs_9_ = bf16[8,64,256]{2,1,0:T(8,128)(2,1)S(1)} collective-permute-done((bf16[8,64,256]{2,1,0:T(8,128)(2,1)S(1)}, bf16[8,64,256]{2,1,0:T(8,128)(2,1)S(1)}, u32[]{:S(2)}, u32[]{:S(2)}) %collective-permute-start.9) | collective-permute-done | bytes 262176 | tf_op jit(solution)/shard_map/ppermute | solution.py:22
  55.5 1.6 collective-permute-start.14
  59.0 7.2 %all-to-all-start = ((bf16[1,4,128,896]{3,1,0,2:T(4,128)(2,1)}), bf16[1,4,128,896]{3,1,0,2:T(4,128)(2,1)}, u32[]{:S(2)}, u32[]{:S(2)}) async-start(bf16[1,4,128,896]{3,1,0,2:T(4,128)(2,1)} %bitcast.2), calls=%async_computation | async-start | bytes 1835008 | tf_op jit(solution)/shard_map/all_to_all | solution.py:364
  66.9 13.1 %policy_logits.1.policy_ref = f32[512,896]{1,0:T(8,128)} custom-call(bf16[64,8192]{1,0:T(8,128)(2,1)} %refs_0_.1, bf16[64,8192]{1,0:T(8,128)(2,1)} %copy-done.11, bf16[128,4096]{1,0:T(8,128)(2,1)} %collective-permute-done.10.refs_2_, bf16[128,4096]{1,0:T(8,128)(2,1)} %collective-permute-done.11.refs_3_, bf16[128,4096]{1,0:T(8,128)(2,1)} %collective-permute-done.12.refs_4_, ...), custom_call_target="tpu_custom_call" | custom-call | flops 7516192768 | bytes 24903680 | tf_op jit(solution)/shard_map/policy_logits/pallas_call | solution.py:107
  80.0 3.1 %all-to-all-done = bf16[1,4,128,896]{3,1,0,2:T(4,128)(2,1)} async-done(((bf16[1,4,128,896]{3,1,0,2:T(4,128)(2,1)}), bf16[1,4,128,896]{3,1,0,2:T(4,128)(2,1)}, u32[]{:S(2)}, u32[]{:S(2)}) %all-to-all-start) | async-done | bytes 917536 | tf_op jit(solution)/shard_map/all_to_all | solution.py:364
  83.2 1.6 reshape.46.refer_ref
  84.9 2.1 %row_stats.1 = f32[8,512]{1,0:T(8,128)S(1)} custom-call(s32[512]{0:T(512)S(1)} %copy-done.3, f32[512,896]{1,0:T(8,128)S(1)} %copy-done, bf16[512,896]{1,0:T(8,128)(2,1)S(1)} %reshape.46.refer_ref), custom_call_target="tpu_custom_call" | custom-call | flops 9175040 | bytes 2752512 | tf_op jit(solution)/shard_map/row_stats/pallas_call | solution.py:154
  87.0 1.9 %collective-permute-start.20 = (f32[8,512]{1,0:T(8,128)S(1)}, f32[8,512]{1,0:T(8,128)S(1)}, u32[]{:S(2)}, u32[]{:S(2)}) collective-permute-start(f32[8,512]{1,0:T(8,128)S(1)} %row_stats.1), channel_id=1, source_target_pairs={{0,3},{1,2},{2,1},{3,0},{4,7},{5,6},{6,5},{7,4},{8,11},{9,10},{10,... | collective-permute-start | bytes 49160 | tf_op jit(solution)/shard_map/ppermute | solution.py:22
  90.8 2.1 %collective-permute-done.19 = f32[8,512]{1,0:T(8,128)S(1)} collective-permute-done((f32[8,512]{1,0:T(8,128)S(1)}, f32[8,512]{1,0:T(8,128)S(1)}, u32[]{:S(2)}, u32[]{:S(2)}) %collective-permute-start.19) | collective-permute-done | bytes 16416 | tf_op jit(solution)/shard_map/ppermute | solution.py:22
  93.9 1.5 collective-permute-start.22
  98.2 2.9 %collective-permute-start.26 = (f32[8,512]{1,0:T(8,128)S(1)}, f32[8,512]{1,0:T(8,128)S(1)}, u32[]{:S(2)}, u32[]{:S(2)}) collective-permute-start(f32[8,512]{1,0:T(8,128)S(1)} %stack.175), channel_id=1, source_target_pairs={{0,96},{16,112},{32,64},{48,80},{64,32},{80,48},{96,0},{112,16},{1... | collective-permute-start | bytes 49160 | tf_op jit(solution)/shard_map/ppermute | solution.py:26
  102.2 3.0 %collective-permute-done.25 = f32[8,512]{1,0:T(8,128)S(1)} collective-permute-done((f32[8,512]{1,0:T(8,128)S(1)}, f32[8,512]{1,0:T(8,128)S(1)}, u32[]{:S(2)}, u32[]{:S(2)}) %collective-permute-start.25) | collective-permute-done | bytes 16416 | tf_op jit(solution)/shard_map/ppermute | solution.py:26
  105.4 4.7 %collective-permute-start.27 = (f32[8,512]{1,0:T(8,128)S(1)}, f32[8,512]{1,0:T(8,128)S(1)}, u32[]{:S(2)}, u32[]{:S(2)}) collective-permute-start(f32[8,512]{1,0:T(8,128)S(1)} %stack.188), channel_id=1, source_target_pairs={{0,16},{16,0},{32,48},{48,32},{64,80},{80,64},{96,112},{112,96},{1... | collective-permute-start | bytes 49160 | tf_op jit(solution)/shard_map/ppermute | solution.py:30
  111.1 2.5 %logit_grads.1 = (bf16[512,896]{1,0:T(8,128)(2,1)S(1)}, bf16[512,896]{1,0:T(8,128)(2,1)S(1)}, f32[8,128]{1,0:T(8,128)S(1)}) custom-call(f32[8,512]{1,0:T(8,128)S(1)} %stack.199.stats_ref, s32[512]{0:T(512)S(1)} %copy-done.3, s32[512]{0:T(512)S(1)} %copy-done.4, s32[512]{0:T(512)S(1)} %copy-done.5, f32[512,896]{1,0:T(8,128)S(1)} %copy-done, ...), custom_call_target="tpu_custom_call" | custom-call | flops 469762048 | bytes 4587520 | tf_op jit(solution)/shard_map/logit_grads/pallas_call | solution.py:245
  114.4 2.0 %collective-permute-done.28.other_x = bf16[512,896]{1,0:T(8,128)(2,1)S(1)} collective-permute-done((bf16[512,896]{1,0:T(8,128)(2,1)S(1)}, bf16[512,896]{1,0:T(8,128)(2,1)S(1)}, u32[]{:S(2)}, u32[]{:S(2)}) %collective-permute-start.28) | collective-permute-done | bytes 917536 | tf_op jit(solution)/shard_map/ppermute | solution.py:30
  116.4 1.3 collective-permute-done.29.other_y
  118.6 12.3 %hidden_parts.1 = (bf16[256,1024]{1,0:T(8,128)(2,1)S(1)}, bf16[256,1024]{1,0:T(8,128)(2,1)S(1)}, bf16[256,1024]{1,0:T(8,128)(2,1)S(1)}, bf16[256,1024]{1,0:T(8,1...) custom-call(bf16[512,896]{1,0:T(8,128)(2,1)} %copy-done.1, ...), custom_call_target="tpu_custom_call" | custom-call | flops 7516192768 | bytes 26214400 | tf_op jit(solution)/shard_map/hidden_parts/pallas_call | solution.py:310
  131.1 2.0 %collective-permute-start.33 = (bf16[256,1024]{1,0:T(8,128)(2,1)S(1)}, bf16[256,1024]{1,0:T(8,128)(2,1)S(1)}, u32[]{:S(2)}, u32[]{:S(2)}) collective-permute-start(bf16[256,1024]{1,0:T(8,128)(2,1)S(1)} %get-tuple-element.42), channel_id=1, source_target_pairs={{0,12},{1,13},{2,14},{3,15},{4,8},{5,9},{6,10},{7,11},{8,4},{9,5},... | collective-permute-start | bytes 1572872 | tf_op jit(solution)/shard_map/ppermute | solution.py:22
  133.1 2.0 %collective-permute-start.40 = (bf16[256,1024]{1,0:T(8,128)(2,1)}, bf16[256,1024]{1,0:T(8,128)(2,1)S(1)}, u32[]{:S(2)}, u32[]{:S(2)}) collective-permute-start(bf16[256,1024]{1,0:T(8,128)(2,1)} %get-tuple-element.46), channel_id=1, source_target_pairs={{0,3},{1,2},{2,1},{3,0},{4,7},{5,6},{6,5},{7,4},{8,11},{9,10},{10,... | collective-permute-start | bytes 1572872 | tf_op jit(solution)/shard_map/ppermute | solution.py:22
  135.1 9.1 %collective-permute-done.31 = bf16[256,1024]{1,0:T(8,128)(2,1)S(1)} collective-permute-done((bf16[256,1024]{1,0:T(8,128)(2,1)S(1)}, bf16[256,1024]{1,0:T(8,128)(2,1)S(1)}, u32[]{:S(2)}, u32[]{:S(2)}) %collective-permute-start.31) | collective-permute-done | bytes 524320 | tf_op jit(solution)/shard_map/ppermute | solution.py:22
  144.3 1.2 collective-permute-start.32
  149.6 2.6 %collective-permute-done.32 = bf16[128,1024]{1,0:T(8,128)(2,1)S(1)} collective-permute-done((bf16[128,1024]{1,0:T(8,128)(2,1)S(1)}, bf16[128,1024]{1,0:T(8,128)(2,1)S(1)}, u32[]{:S(2)}, u32[]{:S(2)}) %collective-permute-start.32) | collective-permute-done | bytes 262176 | tf_op jit(solution)/shard_map/ppermute | solution.py:22
  153.1 1.8 %collective-permute-start.35 = (bf16[32,2048]{1,0:T(8,128)(2,1)S(1)}, bf16[32,2048]{1,0:T(8,128)(2,1)S(1)}, u32[]{:S(2)}, u32[]{:S(2)}) collective-permute-start(bf16[32,2048]{1,0:T(8,128)(2,1)S(1)} %get-tuple-element.80), channel_id=1, source_target_pairs={{0,2},{1,3},{2,0},{3,1},{4,6},{5,7},{6,4},{7,5},{8,10},{9,11},{10,... | collective-permute-start | bytes 393224 | tf_op jit(solution)/shard_map/ppermute | solution.py:22
  155.0 1.2 collective-permute-start.37
  156.5 1.7 collective-permute-start.42
  160.2 1.4 collective-permute-done.37
  162.2 1.4 collective-permute-done.44
  164.9 1.9 %collective-permute-start.45 = (bf16[8,4096]{1,0:T(8,128)(2,1)S(1)}, bf16[8,4096]{1,0:T(8,128)(2,1)S(1)}, u32[]{:S(2)}, u32[]{:S(2)}) collective-permute-start(bf16[8,4096]{1,0:T(8,128)(2,1)S(1)} %get-tuple-element.86), channel_id=1, source_target_pairs={{0,64},{16,80},{32,96},{48,112},{64,0},{80,16},{96,32},{112,48},{1... | collective-permute-start | bytes 196616 | tf_op jit(solution)/shard_map/ppermute | solution.py:26
  167.6 2.0 %collective-permute-done.45 = bf16[8,4096]{1,0:T(8,128)(2,1)S(1)} collective-permute-done((bf16[8,4096]{1,0:T(8,128)(2,1)S(1)}, bf16[8,4096]{1,0:T(8,128)(2,1)S(1)}, u32[]{:S(2)}, u32[]{:S(2)}) %collective-permute-start.45) | collective-permute-done | bytes 65568 | tf_op jit(solution)/shard_map/ppermute | solution.py:26
  169.6 1.6 collective-permute-done.47
  171.2 7.2 %collective-permute-start.48 = (bf16[4,4096]{1,0:T(4,128)(2,1)S(1)}, bf16[4,4096]{1,0:T(4,128)(2,1)S(1)}, u32[]{:S(2)}, u32[]{:S(2)}) collective-permute-start(bf16[4,4096]{1,0:T(4,128)(2,1)S(1)} %get-tuple-element.90), channel_id=1, source_target_pairs={{0,16},{16,0},{32,48},{48,32},{64,80},{80,64},{96,112},{112,96},{1... | collective-permute-start | bytes 98312 | tf_op jit(solution)/shard_map/ppermute | solution.py:30
  (133 shorter events, 27.8 us)
Async XLA Ops:
  0.6 4.0 %collective-permute-start = (bf16[64,8192]{1,0:T(8,128)(2,1)}, bf16[64,8192]{1,0:T(8,128)(2,1)S(1)}, u32[]{:S(2)}, u32[]{:S(2)}) collective-permute-start(bf16[64,8192]{1,0:T(8,128)(2,1)} %refs_0_.1), channel_id=1, source_target_pairs={{0,16},{16,0},{32,48},{48,32},{64,80},{80,64},{96,112},{112,96},{1... | collective-permute-start | bytes 3145736 | tf_op jit(solution)/shard_map/ppermute | solution.py:30
  4.6 113.1 %collective-permute-start.30 = (bf16[8192,896]{1,0:T(8,128)(2,1)}, bf16[8192,896]{1,0:T(8,128)(2,1)}, u32[]{:S(2)}, u32[]{:S(2)}) collective-permute-start(bf16[8192,896]{1,0:T(8,128)(2,1)} %own_weight.1), channel_id=1, source_target_pairs={{0,16},{16,0},{32,48},{48,32},{64,80},{80,64},{96,112},{112,96},{1... | collective-permute-start | bytes 44040200 | tf_op jit(solution)/shard_map/ppermute | solution.py:30
  5.8 6.1 %collective-permute-start.1 = (bf16[128,256]{1,0:T(8,128)(2,1)S(1)}, bf16[128,256]{1,0:T(8,128)(2,1)S(1)}, u32[]{:S(2)}, u32[]{:S(2)}) collective-permute-start(bf16[128,256]{1,0:T(8,128)(2,1)S(1)} %pad_maximum_fusion.8), channel_id=1, source_target_pairs={{0,64},{16,80},{32,96},{48,112},{64,0},{80,16},{96,32},{112,48},{1... | collective-permute-start | bytes 196616 | tf_op jit(solution)/shard_map/ppermute | solution.py:26
  13.2 25.5 %collective-permute-start.11 = (bf16[128,4096]{1,0:T(8,128)(2,1)S(1)}, bf16[128,4096]{1,0:T(8,128)(2,1)}, u32[]{:S(2)}, u32[]{:S(2)}) collective-permute-start(bf16[128,4096]{1,0:T(8,128)(2,1)S(1)} %pad_maximum_fusion), channel_id=1, source_target_pairs={{0,96},{16,112},{32,64},{48,80},{64,32},{80,48},{96,0},{112,16},{1... | collective-permute-start | bytes 3145736 | tf_op jit(solution)/shard_map/ppermute | solution.py:26
  16.0 24.2 %collective-permute-start.10 = (bf16[128,4096]{1,0:T(8,128)(2,1)S(1)}, bf16[128,4096]{1,0:T(8,128)(2,1)}, u32[]{:S(2)}, u32[]{:S(2)}) collective-permute-start(bf16[128,4096]{1,0:T(8,128)(2,1)S(1)} %pad_maximum_fusion), channel_id=1, source_target_pairs={{0,32},{16,48},{32,0},{48,16},{64,96},{80,112},{96,64},{112,80},{1... | collective-permute-start | bytes 3145736 | tf_op jit(solution)/shard_map/ppermute | solution.py:26
  16.0 3.2 %collective-permute-start.2 = (bf16[1,64,256]{2,1,0:T(8,128)(2,1)S(1)}, bf16[1,64,256]{2,1,0:T(8,128)(2,1)S(1)}, u32[]{:S(2)}, u32[]{:S(2)}) collective-permute-start(bf16[1,64,256]{2,1,0:T(8,128)(2,1)S(1)} %get-tuple-element.113), channel_id=1, source_target_pairs={{0,1},{1,0},{2,3},{3,2},{4,5},{5,4},{6,7},{7,6},{8,9},{9,8},{10,11... | collective-permute-start | bytes 98312 | tf_op jit(solution)/shard_map/ppermute | solution.py:22
  17.4 4.7 %collective-permute-start.6 = (bf16[1,64,256]{2,1,0:T(8,128)(2,1)S(1)}, bf16[1,64,256]{2,1,0:T(8,128)(2,1)S(1)}, u32[]{:S(2)}, u32[]{:S(2)}) collective-permute-start(bf16[1,64,256]{2,1,0:T(8,128)(2,1)S(1)} %get-tuple-element.112), channel_id=1, source_target_pairs={{0,4},{1,5},{2,6},{3,7},{4,0},{5,1},{6,2},{7,3},{8,12},{9,13},{10,... | collective-permute-start | bytes 98312 | tf_op jit(solution)/shard_map/ppermute | solution.py:22
  19.3 5.4 %collective-permute-start.3 = (bf16[2,64,256]{2,1,0:T(8,128)(2,1)S(1)}, bf16[2,64,256]{2,1,0:T(8,128)(2,1)S(1)}, u32[]{:S(2)}, u32[]{:S(2)}) collective-permute-start(bf16[2,64,256]{2,1,0:T(8,128)(2,1)S(1)} %pad_maximum_fusion.9), channel_id=1, source_target_pairs={{0,3},{1,2},{2,1},{3,0},{4,7},{5,6},{6,5},{7,4},{8,11},{9,10},{10,... | collective-permute-start | bytes 196616 | tf_op jit(solution)/shard_map/ppermute | solution.py:22
  22.1 19.6 %collective-permute-start.7 = (bf16[2,64,256]{2,1,0:T(8,128)(2,1)S(1)}, bf16[2,64,256]{2,1,0:T(8,128)(2,1)S(1)}, u32[]{:S(2)}, u32[]{:S(2)}) collective-permute-start(bf16[2,64,256]{2,1,0:T(8,128)(2,1)S(1)} %pad_maximum_fusion.10), channel_id=1, source_target_pairs={{0,12},{1,13},{2,14},{3,15},{4,8},{5,9},{6,10},{7,11},{8,4},{9,5},... | collective-permute-start | bytes 196616 | tf_op jit(solution)/shard_map/ppermute | solution.py:22
  24.7 18.4 %collective-permute-start.4 = (bf16[4,64,256]{2,1,0:T(8,128)(2,1)S(1)}, bf16[4,64,256]{2,1,0:T(8,128)(2,1)S(1)}, u32[]{:S(2)}, u32[]{:S(2)}) collective-permute-start(bf16[4,64,256]{2,1,0:T(8,128)(2,1)S(1)} %pad_maximum_fusion.5), channel_id=1, source_target_pairs={{0,4},{1,5},{2,6},{3,7},{4,0},{5,1},{6,2},{7,3},{8,12},{9,13},{10,... | collective-permute-start | bytes 393224 | tf_op jit(solution)/shard_map/ppermute | solution.py:22
  38.7 27.5 %collective-permute-start.13 = (bf16[128,4096]{1,0:T(8,128)(2,1)}, bf16[128,4096]{1,0:T(8,128)(2,1)}, u32[]{:S(2)}, u32[]{:S(2)}) collective-permute-start(bf16[128,4096]{1,0:T(8,128)(2,1)} %collective-permute-done.11.refs_3_), channel_id=1, source_target_pairs={{0,16},{16,0},{32,48},{48,32},{64,80},{80,64},{96,112},{112,96},{1... | collective-permute-start | bytes 3145736 | tf_op jit(solution)/shard_map/ppermute | solution.py:30
  40.3 26.0 %collective-permute-start.12 = (bf16[128,4096]{1,0:T(8,128)(2,1)}, bf16[128,4096]{1,0:T(8,128)(2,1)}, u32[]{:S(2)}, u32[]{:S(2)}) collective-permute-start(bf16[128,4096]{1,0:T(8,128)(2,1)} %collective-permute-done.10.refs_2_), channel_id=1, source_target_pairs={{0,16},{16,0},{32,48},{48,32},{64,80},{80,64},{96,112},{112,96},{1... | collective-permute-start | bytes 3145736 | tf_op jit(solution)/shard_map/ppermute | solution.py:30
  41.7 5.2 %collective-permute-start.8 = (bf16[4,64,256]{2,1,0:T(8,128)(2,1)S(1)}, bf16[4,64,256]{2,1,0:T(8,128)(2,1)S(1)}, u32[]{:S(2)}, u32[]{:S(2)}) collective-permute-start(bf16[4,64,256]{2,1,0:T(8,128)(2,1)S(1)} %pad_maximum_fusion.6), channel_id=1, source_target_pairs={{0,1},{1,0},{2,3},{3,2},{4,5},{5,4},{6,7},{7,6},{8,9},{9,8},{10,11... | collective-permute-start | bytes 393224 | tf_op jit(solution)/shard_map/ppermute | solution.py:22
  43.2 8.9 %collective-permute-start.5 = (bf16[8,64,256]{2,1,0:T(8,128)(2,1)S(1)}, bf16[8,64,256]{2,1,0:T(8,128)(2,1)S(1)}, u32[]{:S(2)}, u32[]{:S(2)}) collective-permute-start(bf16[8,64,256]{2,1,0:T(8,128)(2,1)S(1)} %pad_maximum_fusion.1.refs_6_), channel_id=1, source_target_pairs={{0,12},{1,13},{2,14},{3,15},{4,8},{5,9},{6,10},{7,11},{8,4},{9,5},... | collective-permute-start | bytes 786440 | tf_op jit(solution)/shard_map/ppermute | solution.py:22
  47.0 8.5 %collective-permute-start.9 = (bf16[8,64,256]{2,1,0:T(8,128)(2,1)S(1)}, bf16[8,64,256]{2,1,0:T(8,128)(2,1)S(1)}, u32[]{:S(2)}, u32[]{:S(2)}) collective-permute-start(bf16[8,64,256]{2,1,0:T(8,128)(2,1)S(1)} %pad_maximum_fusion.2.refs_8_), channel_id=1, source_target_pairs={{0,3},{1,2},{2,1},{3,0},{4,7},{5,6},{6,5},{7,4},{8,11},{9,10},{10,... | collective-permute-start | bytes 786440 | tf_op jit(solution)/shard_map/ppermute | solution.py:22
  55.5 2.8 %collective-permute-start.14 = (bf16[8,64,256]{2,1,0:T(8,128)(2,1)S(1)}, bf16[8,64,256]{2,1,0:T(8,128)(2,1)S(1)}, u32[]{:S(2)}, u32[]{:S(2)}) collective-permute-start(bf16[8,64,256]{2,1,0:T(8,128)(2,1)S(1)} %pad_maximum_fusion.1.refs_6_), channel_id=1, source_target_pairs={{0,16},{16,0},{32,48},{48,32},{64,80},{80,64},{96,112},{112,96},{1... | collective-permute-start | bytes 786440 | tf_op jit(solution)/shard_map/ppermute | solution.py:30
  58.2 8.0 %collective-permute-start.16 = (bf16[8,64,256]{2,1,0:T(8,128)(2,1)S(1)}, bf16[8,64,256]{2,1,0:T(8,128)(2,1)S(1)}, u32[]{:S(2)}, u32[]{:S(2)}) collective-permute-start(bf16[8,64,256]{2,1,0:T(8,128)(2,1)S(1)} %pad_maximum_fusion.2.refs_8_), channel_id=1, source_target_pairs={{0,16},{16,0},{32,48},{48,32},{64,80},{80,64},{96,112},{112,96},{1... | collective-permute-start | bytes 786440 | tf_op jit(solution)/shard_map/ppermute | solution.py:30
  58.6 7.6 %collective-permute-start.17 = (bf16[8,64,256]{2,1,0:T(8,128)(2,1)S(1)}, bf16[8,64,256]{2,1,0:T(8,128)(2,1)S(1)}, u32[]{:S(2)}, u32[]{:S(2)}) collective-permute-start(bf16[8,64,256]{2,1,0:T(8,128)(2,1)S(1)} %collective-permute-done.9.refs_9_), channel_id=1, source_target_pairs={{0,16},{16,0},{32,48},{48,32},{64,80},{80,64},{96,112},{112,96},{1... | collective-permute-start | bytes 786440 | tf_op jit(solution)/shard_map/ppermute | solution.py:30
  59.0 24.2 %all-to-all-start = ((bf16[1,4,128,896]{3,1,0,2:T(4,128)(2,1)}), bf16[1,4,128,896]{3,1,0,2:T(4,128)(2,1)}, u32[]{:S(2)}, u32[]{:S(2)}) async-start(bf16[1,4,128,896]{3,1,0,2:T(4,128)(2,1)} %bitcast.2), calls=%async_computation | async-start | bytes 1835008 | tf_op jit(solution)/shard_map/all_to_all | solution.py:364
  87.0 3.9 %collective-permute-start.20 = (f32[8,512]{1,0:T(8,128)S(1)}, f32[8,512]{1,0:T(8,128)S(1)}, u32[]{:S(2)}, u32[]{:S(2)}) collective-permute-start(f32[8,512]{1,0:T(8,128)S(1)} %row_stats.1), channel_id=1, source_target_pairs={{0,3},{1,2},{2,1},{3,0},{4,7},{5,6},{6,5},{7,4},{8,11},{9,10},{10,... | collective-permute-start | bytes 49160 | tf_op jit(solution)/shard_map/ppermute | solution.py:22
  88.8 4.1 %collective-permute-start.19 = (f32[8,512]{1,0:T(8,128)S(1)}, f32[8,512]{1,0:T(8,128)S(1)}, u32[]{:S(2)}, u32[]{:S(2)}) collective-permute-start(f32[8,512]{1,0:T(8,128)S(1)} %row_stats.1), channel_id=1, source_target_pairs={{0,2},{1,3},{2,0},{3,1},{4,6},{5,7},{6,4},{7,5},{8,10},{9,11},{10,... | collective-permute-start | bytes 49160 | tf_op jit(solution)/shard_map/ppermute | solution.py:22
  89.3 3.6 %collective-permute-start.18 = (f32[8,512]{1,0:T(8,128)S(1)}, f32[8,512]{1,0:T(8,128)S(1)}, u32[]{:S(2)}, u32[]{:S(2)}) collective-permute-start(f32[8,512]{1,0:T(8,128)S(1)} %row_stats.1), channel_id=1, source_target_pairs={{0,1},{1,0},{2,3},{3,2},{4,5},{5,4},{6,7},{7,6},{8,9},{9,8},{10,11... | collective-permute-start | bytes 49160 | tf_op jit(solution)/shard_map/ppermute | solution.py:22
  93.1 3.9 %collective-permute-start.23 = (f32[8,512]{1,0:T(8,128)S(1)}, f32[8,512]{1,0:T(8,128)S(1)}, u32[]{:S(2)}, u32[]{:S(2)}) collective-permute-start(f32[8,512]{1,0:T(8,128)S(1)} %stack.162), channel_id=1, source_target_pairs={{0,12},{1,13},{2,14},{3,15},{4,8},{5,9},{6,10},{7,11},{8,4},{9,5},... | collective-permute-start | bytes 49160 | tf_op jit(solution)/shard_map/ppermute | solution.py:22
  93.9 4.1 %collective-permute-start.22 = (f32[8,512]{1,0:T(8,128)S(1)}, f32[8,512]{1,0:T(8,128)S(1)}, u32[]{:S(2)}, u32[]{:S(2)}) collective-permute-start(f32[8,512]{1,0:T(8,128)S(1)} %stack.162), channel_id=1, source_target_pairs={{0,8},{1,9},{2,10},{3,11},{4,12},{5,13},{6,14},{7,15},{8,0},{9,1},... | collective-permute-start | bytes 49160 | tf_op jit(solution)/shard_map/ppermute | solution.py:22
  98.2 4.0 %collective-permute-start.26 = (f32[8,512]{1,0:T(8,128)S(1)}, f32[8,512]{1,0:T(8,128)S(1)}, u32[]{:S(2)}, u32[]{:S(2)}) collective-permute-start(f32[8,512]{1,0:T(8,128)S(1)} %stack.175), channel_id=1, source_target_pairs={{0,96},{16,112},{32,64},{48,80},{64,32},{80,48},{96,0},{112,16},{1... | collective-permute-start | bytes 49160 | tf_op jit(solution)/shard_map/ppermute | solution.py:26
  101.1 4.1 %collective-permute-start.25 = (f32[8,512]{1,0:T(8,128)S(1)}, f32[8,512]{1,0:T(8,128)S(1)}, u32[]{:S(2)}, u32[]{:S(2)}) collective-permute-start(f32[8,512]{1,0:T(8,128)S(1)} %stack.175), channel_id=1, source_target_pairs={{0,64},{16,80},{32,96},{48,112},{64,0},{80,16},{96,32},{112,48},{1... | collective-permute-start | bytes 49160 | tf_op jit(solution)/shard_map/ppermute | solution.py:26
  101.2 4.0 %collective-permute-start.24 = (f32[8,512]{1,0:T(8,128)S(1)}, f32[8,512]{1,0:T(8,128)S(1)}, u32[]{:S(2)}, u32[]{:S(2)}) collective-permute-start(f32[8,512]{1,0:T(8,128)S(1)} %stack.175), channel_id=1, source_target_pairs={{0,32},{16,48},{32,0},{48,16},{64,96},{80,112},{96,64},{112,80},{1... | collective-permute-start | bytes 49160 | tf_op jit(solution)/shard_map/ppermute | solution.py:26
  105.4 5.6 %collective-permute-start.27 = (f32[8,512]{1,0:T(8,128)S(1)}, f32[8,512]{1,0:T(8,128)S(1)}, u32[]{:S(2)}, u32[]{:S(2)}) collective-permute-start(f32[8,512]{1,0:T(8,128)S(1)} %stack.188), channel_id=1, source_target_pairs={{0,16},{16,0},{32,48},{48,32},{64,80},{80,64},{96,112},{112,96},{1... | collective-permute-start | bytes 49160 | tf_op jit(solution)/shard_map/ppermute | solution.py:30
  113.6 2.8 %collective-permute-start.28 = (bf16[512,896]{1,0:T(8,128)(2,1)S(1)}, bf16[512,896]{1,0:T(8,128)(2,1)S(1)}, u32[]{:S(2)}, u32[]{:S(2)}) collective-permute-start(bf16[512,896]{1,0:T(8,128)(2,1)S(1)} %get-tuple-element.36.own_x), channel_id=1, source_target_pairs={{0,16},{16,0},{32,48},{48,32},{64,80},{80,64},{96,112},{112,96},{1... | collective-permute-start | bytes 2752520 | tf_op jit(solution)/shard_map/ppermute | solution.py:30
  114.3 3.4 %collective-permute-start.29 = (bf16[512,896]{1,0:T(8,128)(2,1)S(1)}, bf16[512,896]{1,0:T(8,128)(2,1)S(1)}, u32[]{:S(2)}, u32[]{:S(2)}) collective-permute-start(bf16[512,896]{1,0:T(8,128)(2,1)S(1)} %get-tuple-element.37.own_y), channel_id=1, source_target_pairs={{0,16},{16,0},{32,48},{48,32},{64,80},{80,64},{96,112},{112,96},{1... | collective-permute-start | bytes 2752520 | tf_op jit(solution)/shard_map/ppermute | solution.py:30
  131.0 13.2 %collective-permute-start.31 = (bf16[256,1024]{1,0:T(8,128)(2,1)S(1)}, bf16[256,1024]{1,0:T(8,128)(2,1)S(1)}, u32[]{:S(2)}, u32[]{:S(2)}) collective-permute-start(bf16[256,1024]{1,0:T(8,128)(2,1)S(1)} %get-tuple-element.40), channel_id=1, source_target_pairs={{0,4},{1,5},{2,6},{3,7},{4,0},{5,1},{6,2},{7,3},{8,12},{9,13},{10,... | collective-permute-start | bytes 1572872 | tf_op jit(solution)/shard_map/ppermute | solution.py:22
  131.1 14.4 %collective-permute-start.33 = (bf16[256,1024]{1,0:T(8,128)(2,1)S(1)}, bf16[256,1024]{1,0:T(8,128)(2,1)S(1)}, u32[]{:S(2)}, u32[]{:S(2)}) collective-permute-start(bf16[256,1024]{1,0:T(8,128)(2,1)S(1)} %get-tuple-element.42), channel_id=1, source_target_pairs={{0,12},{1,13},{2,14},{3,15},{4,8},{5,9},{6,10},{7,11},{8,4},{9,5},... | collective-permute-start | bytes 1572872 | tf_op jit(solution)/shard_map/ppermute | solution.py:22
  133.1 13.8 %collective-permute-start.38 = (bf16[256,1024]{1,0:T(8,128)(2,1)}, bf16[256,1024]{1,0:T(8,128)(2,1)S(1)}, u32[]{:S(2)}, u32[]{:S(2)}) collective-permute-start(bf16[256,1024]{1,0:T(8,128)(2,1)} %get-tuple-element.44), channel_id=1, source_target_pairs={{0,1},{1,0},{2,3},{3,2},{4,5},{5,4},{6,7},{7,6},{8,9},{9,8},{10,11... | collective-permute-start | bytes 1572872 | tf_op jit(solution)/shard_map/ppermute | solution.py:22
  133.1 16.0 %collective-permute-start.40 = (bf16[256,1024]{1,0:T(8,128)(2,1)}, bf16[256,1024]{1,0:T(8,128)(2,1)S(1)}, u32[]{:S(2)}, u32[]{:S(2)}) collective-permute-start(bf16[256,1024]{1,0:T(8,128)(2,1)} %get-tuple-element.46), channel_id=1, source_target_pairs={{0,3},{1,2},{2,1},{3,0},{4,7},{5,6},{6,5},{7,4},{8,11},{9,10},{10,... | collective-permute-start | bytes 1572872 | tf_op jit(solution)/shard_map/ppermute | solution.py:22
  144.3 7.9 %collective-permute-start.32 = (bf16[128,1024]{1,0:T(8,128)(2,1)S(1)}, bf16[128,1024]{1,0:T(8,128)(2,1)S(1)}, u32[]{:S(2)}, u32[]{:S(2)}) collective-permute-start(bf16[128,1024]{1,0:T(8,128)(2,1)S(1)} %add_convert_fusion.7), channel_id=1, source_target_pairs={{0,12},{1,13},{2,14},{3,15},{4,8},{5,9},{6,10},{7,11},{8,4},{9,5},... | collective-permute-start | bytes 786440 | tf_op jit(solution)/shard_map/ppermute | solution.py:22
  146.5 6.4 %collective-permute-start.34 = (bf16[128,1024]{1,0:T(8,128)(2,1)S(1)}, bf16[128,1024]{1,0:T(8,128)(2,1)S(1)}, u32[]{:S(2)}, u32[]{:S(2)}) collective-permute-start(bf16[128,1024]{1,0:T(8,128)(2,1)S(1)} %add_convert_fusion.5), channel_id=1, source_target_pairs={{0,4},{1,5},{2,6},{3,7},{4,0},{5,1},{6,2},{7,3},{8,12},{9,13},{10,... | collective-permute-start | bytes 786440 | tf_op jit(solution)/shard_map/ppermute | solution.py:22
  148.0 8.2 %collective-permute-start.39 = (bf16[128,1024]{1,0:T(8,128)(2,1)S(1)}, bf16[128,1024]{1,0:T(8,128)(2,1)S(1)}, u32[]{:S(2)}, u32[]{:S(2)}) collective-permute-start(bf16[128,1024]{1,0:T(8,128)(2,1)S(1)} %add_convert_fusion.3), channel_id=1, source_target_pairs={{0,3},{1,2},{2,1},{3,0},{4,7},{5,6},{6,5},{7,4},{8,11},{9,10},{10,... | collective-permute-start | bytes 786440 | tf_op jit(solution)/shard_map/ppermute | solution.py:22
  149.2 7.1 %collective-permute-start.41 = (bf16[128,1024]{1,0:T(8,128)(2,1)S(1)}, bf16[128,1024]{1,0:T(8,128)(2,1)S(1)}, u32[]{:S(2)}, u32[]{:S(2)}) collective-permute-start(bf16[128,1024]{1,0:T(8,128)(2,1)S(1)} %add_convert_fusion.1), channel_id=1, source_target_pairs={{0,1},{1,0},{2,3},{3,2},{4,5},{5,4},{6,7},{7,6},{8,9},{9,8},{10,11... | collective-permute-start | bytes 786440 | tf_op jit(solution)/shard_map/ppermute | solution.py:22
  153.1 6.9 %collective-permute-start.35 = (bf16[32,2048]{1,0:T(8,128)(2,1)S(1)}, bf16[32,2048]{1,0:T(8,128)(2,1)S(1)}, u32[]{:S(2)}, u32[]{:S(2)}) collective-permute-start(bf16[32,2048]{1,0:T(8,128)(2,1)S(1)} %get-tuple-element.80), channel_id=1, source_target_pairs={{0,2},{1,3},{2,0},{3,1},{4,6},{5,7},{6,4},{7,5},{8,10},{9,11},{10,... | collective-permute-start | bytes 393224 | tf_op jit(solution)/shard_map/ppermute | solution.py:22
  155.0 6.7 %collective-permute-start.37 = (bf16[32,2048]{1,0:T(8,128)(2,1)S(1)}, bf16[32,2048]{1,0:T(8,128)(2,1)S(1)}, u32[]{:S(2)}, u32[]{:S(2)}) collective-permute-start(bf16[32,2048]{1,0:T(8,128)(2,1)S(1)} %get-tuple-element.81), channel_id=1, source_target_pairs={{0,3},{1,2},{2,1},{3,0},{4,7},{5,6},{6,5},{7,4},{8,11},{9,10},{10,... | collective-permute-start | bytes 393224 | tf_op jit(solution)/shard_map/ppermute | solution.py:22
  156.2 5.5 %collective-permute-start.36 = (bf16[32,2048]{1,0:T(8,128)(2,1)S(1)}, bf16[32,2048]{1,0:T(8,128)(2,1)S(1)}, u32[]{:S(2)}, u32[]{:S(2)}) collective-permute-start(bf16[32,2048]{1,0:T(8,128)(2,1)S(1)} %get-tuple-element.82), channel_id=1, source_target_pairs={{0,1},{1,0},{2,3},{3,2},{4,5},{5,4},{6,7},{7,6},{8,9},{9,8},{10,11... | collective-permute-start | bytes 393224 | tf_op jit(solution)/shard_map/ppermute | solution.py:22
  156.5 5.7 %collective-permute-start.42 = (bf16[32,2048]{1,0:T(8,128)(2,1)S(1)}, bf16[32,2048]{1,0:T(8,128)(2,1)S(1)}, u32[]{:S(2)}, u32[]{:S(2)}) collective-permute-start(bf16[32,2048]{1,0:T(8,128)(2,1)S(1)} %get-tuple-element.83), channel_id=1, source_target_pairs={{0,8},{1,9},{2,10},{3,11},{4,12},{5,13},{6,14},{7,15},{8,0},{9,1},... | collective-permute-start | bytes 393224 | tf_op jit(solution)/shard_map/ppermute | solution.py:22
  158.2 5.4 %collective-permute-start.44 = (bf16[32,2048]{1,0:T(8,128)(2,1)S(1)}, bf16[32,2048]{1,0:T(8,128)(2,1)S(1)}, u32[]{:S(2)}, u32[]{:S(2)}) collective-permute-start(bf16[32,2048]{1,0:T(8,128)(2,1)S(1)} %get-tuple-element.84), channel_id=1, source_target_pairs={{0,12},{1,13},{2,14},{3,15},{4,8},{5,9},{6,10},{7,11},{8,4},{9,5},... | collective-permute-start | bytes 393224 | tf_op jit(solution)/shard_map/ppermute | solution.py:22
  160.0 4.8 %collective-permute-start.43 = (bf16[32,2048]{1,0:T(8,128)(2,1)S(1)}, bf16[32,2048]{1,0:T(8,128)(2,1)S(1)}, u32[]{:S(2)}, u32[]{:S(2)}) collective-permute-start(bf16[32,2048]{1,0:T(8,128)(2,1)S(1)} %get-tuple-element.85), channel_id=1, source_target_pairs={{0,4},{1,5},{2,6},{3,7},{4,0},{5,1},{6,2},{7,3},{8,12},{9,13},{10,... | collective-permute-start | bytes 393224 | tf_op jit(solution)/shard_map/ppermute | solution.py:22
  164.9 4.7 %collective-permute-start.45 = (bf16[8,4096]{1,0:T(8,128)(2,1)S(1)}, bf16[8,4096]{1,0:T(8,128)(2,1)S(1)}, u32[]{:S(2)}, u32[]{:S(2)}) collective-permute-start(bf16[8,4096]{1,0:T(8,128)(2,1)S(1)} %get-tuple-element.86), channel_id=1, source_target_pairs={{0,64},{16,80},{32,96},{48,112},{64,0},{80,16},{96,32},{112,48},{1... | collective-permute-start | bytes 196616 | tf_op jit(solution)/shard_map/ppermute | solution.py:26
  166.8 4.3 %collective-permute-start.47 = (bf16[8,4096]{1,0:T(8,128)(2,1)S(1)}, bf16[8,4096]{1,0:T(8,128)(2,1)S(1)}, u32[]{:S(2)}, u32[]{:S(2)}) collective-permute-start(bf16[8,4096]{1,0:T(8,128)(2,1)S(1)} %get-tuple-element.87), channel_id=1, source_target_pairs={{0,96},{16,112},{32,64},{48,80},{64,32},{80,48},{96,0},{112,16},{1... | collective-permute-start | bytes 196616 | tf_op jit(solution)/shard_map/ppermute | solution.py:26
  167.0 4.1 %collective-permute-start.46 = (bf16[8,4096]{1,0:T(8,128)(2,1)S(1)}, bf16[8,4096]{1,0:T(8,128)(2,1)S(1)}, u32[]{:S(2)}, u32[]{:S(2)}) collective-permute-start(bf16[8,4096]{1,0:T(8,128)(2,1)S(1)} %get-tuple-element.88), channel_id=1, source_target_pairs={{0,32},{16,48},{32,0},{48,16},{64,96},{80,112},{96,64},{112,80},{1... | collective-permute-start | bytes 196616 | tf_op jit(solution)/shard_map/ppermute | solution.py:26
  171.2 8.1 %collective-permute-start.48 = (bf16[4,4096]{1,0:T(4,128)(2,1)S(1)}, bf16[4,4096]{1,0:T(4,128)(2,1)S(1)}, u32[]{:S(2)}, u32[]{:S(2)}) collective-permute-start(bf16[4,4096]{1,0:T(4,128)(2,1)S(1)} %get-tuple-element.90), channel_id=1, source_target_pairs={{0,16},{16,0},{32,48},{48,32},{64,80},{80,64},{96,112},{112,96},{1... | collective-permute-start | bytes 98312 | tf_op jit(solution)/shard_map/ppermute | solution.py:30
  (15 other events, 134.8 us)

commit v2 on v1

--- a/solution.py
+++ b/solution.py
@@ -51,76 +51,73 @@
 def logits_body(*refs):
     (mine, theirs), near, gathered, weight, policy_ref = refs[:2], refs[2:6], refs[6:14], refs[14], refs[15]
     states, pieces, slabs, sems = refs[16:]
-    rows = mine.shape[0]
-    half = near[0].shape[1]
-    depth = half // RING
-    width = half // CHIPS
+    rows, width = mine.shape
+    depth = width // (2 * RING)
+    span = width // CHIPS
     core, x, y, z = where_am_i()
 
-    def rows_of(dz, side):
-        start = (z ^ dz) * (2 * rows) + (core ^ side) * rows
-        return pl.ds(pl.multiple_of(start, rows), rows)
+    def rows_of(dz, side, start=0, size=rows):
+        start = (z ^ dz) * (2 * rows) + (core ^ side) * rows + start
+        return pl.ds(pl.multiple_of(start, size), size)
 
     loads = [
         pltpu.make_async_copy(ref, pieces.at[i // 2, pl.ds(8 * (i % 2), 8)], sems.at[i]) for i, ref in enumerate(gathered)
     ]
+    blocks = [(0, 0, mine), (0, 1, theirs), (1, 0, near[0]), (3, 0, near[1]), (1, 1, near[2]), (3, 1, near[3])]
     slices = []
     for k in range(2 * RING):
-        far = k // RING
         here = pl.ds(k * depth, depth)
-        there = pl.ds(pl.multiple_of((core ^ far) * half + (k % RING) * depth, depth), depth)
-        within = pl.ds((k % RING) * depth, depth)
-        moves = [
-            (mine.at[:, there], states.at[rows_of(0, 0), here]),
-            (theirs.at[:, there], states.at[rows_of(0, 1), here]),
-        ]
-        for dz, block in ((1, near[2 * far]), (3, near[2 * far + 1])):
-            for side in range(CORES):
-                moves.append((block.at[pl.ds(side * rows, rows), within], states.at[rows_of(dz, side ^ far), here]))
-        moves.append((weight.at[there], slabs.at[k]))
+        moves = [(block.at[:, here], states.at[rows_of(dz, side), here]) for dz, side, block in blocks]
+        moves.append((weight.at[here], slabs.at[k]))
         slices.append([pltpu.make_async_copy(a, b, sems.at[8 + 7 * k + i]) for i, (a, b) in enumerate(moves)])
-    for copy in loads[:4] + slices[0] + loads[4:]:
+    for copy in loads + slices[0]:
         copy.start()
     for k in range(1, 2 * RING):
         for copy in slices[k]:
             copy.start()
-    for far in range(2):
-        for copy in loads[4 * far : 4 * far + 4]:
+    for copy in loads:
+        copy.wait()
+    for i in range(CHIPS):
+        dx, dy = x ^ (i // RING), y ^ (i % RING)
+        at = pl.ds(i * span, span)
+        for side in range(CORES):
+            states[rows_of(2, side, 0, rows // 2), at] = pieces[2 * side, place_of(dy, dx)]
+            states[rows_of(2, side, rows // 2, rows // 2), at] = pieces[2 * side + 1, place_of(dx, dy)]
+    for k in range(2 * RING):
+        for copy in slices[k]:
             copy.wait()
-        for k in range(RING):
-            for j in range(RING):
-                at = pl.ds(far * half + (k * RING + j) * width, width)
-                states[rows_of(2, far), at] = pieces[2 * far, place_of(y ^ j, x ^ k)]
-                states[rows_of(2, 1 - far), at] = pieces[2 * far + 1, place_of(x ^ k, y ^ j)]
-        for k in range(far * RING, (far + 1) * RING):
-            for copy in slices[k]:
-                copy.wait()
-            product = jnp.dot(states[:, k * depth : (k + 1) * depth], slabs[k], preferred_element_type=F32)
-            policy_ref[...] = product if k == 0 else policy_ref[...] + product
+        product = jnp.dot(states[:, k * depth : (k + 1) * depth], slabs[k], preferred_element_type=F32)
+        policy_ref[...] = product if k == 0 else policy_ref[...] + product
 
 
 def policy_logits(mine, theirs, near, gathered, weight):
-    rows, half = mine.shape[0], near[0].shape[1]
+    rows, width = mine.shape
     tokens = rows * CORES * RING
     cols = weight.shape[1]
-    width = half // CHIPS
     return pl.pallas_call(
         logits_body,
         out_shape=jax.ShapeDtypeStruct((tokens, cols), F32),
         in_specs=[any_spec()] * 15,
         out_specs=pl.BlockSpec(memory_space=pltpu.VMEM),
         scratch_shapes=[
-            pltpu.VMEM((tokens, 2 * half), BF16),
-            pltpu.VMEM((4, CHIPS, rows, width), BF16),
-            pltpu.VMEM((2 * RING, half // RING, cols), BF16),
+            pltpu.VMEM((tokens, width), BF16),
+            pltpu.VMEM((4, CHIPS, rows // 2, width // CHIPS), BF16),
+            pltpu.VMEM((2 * RING, width // (2 * RING), cols), BF16),
             pltpu.SemaphoreType.DMA((8 + 7 * 2 * RING,)),
         ],
         compiler_params=params(52),
         cost_estimate=pl.CostEstimate(
-            flops=4 * tokens * half * cols, bytes_accessed=4 * half * (cols + tokens) + 4 * tokens * cols, transcendentals=0
+            flops=2 * tokens * width * cols, bytes_accessed=2 * width * (cols + tokens) + 4 * tokens * cols, transcendentals=0
         ),
         name="policy_logits",
     )(mine, theirs, *near, *gathered, weight)
+
+
+def in_token_order(refer):
+    shape = (refer.shape[0], refer.shape[0])
+    row, source = lax.broadcasted_iota(jnp.int32, shape, 0), lax.broadcasted_iota(jnp.int32, shape, 1)
+    wanted = ((row >> 2) & 15) * 8 + (row >> 6) * 4 + (row & 3)
+    return jnp.dot((source == wanted).astype(F32).astype(BF16), refer, preferred_element_type=F32)
 
 
 def stats_body(targets_ref, policy_ref, refer_ref, stats_ref):
@@ -131,7 +128,7 @@
     local = jnp.where((local >= 0) & (local < cols), local, -1).astype(F32)
     local = jnp.broadcast_to(local, (128, rows)).T[:, 0:1].astype(jnp.int32)
     policy = policy_ref[...]
-    refer = refer_ref[...].astype(F32)
+    refer = in_token_order(refer_ref[...])
     hit = lax.broadcasted_iota(jnp.int32, (rows, cols), 1) == local
     peak = jnp.max(policy, axis=1, keepdims=True)
     scaled = jnp.exp(policy - peak)
@@ -180,7 +177,7 @@
     return jnp.stack([peak, total, cross, ref_peak, ref_total, picked, ref_picked, jnp.zeros_like(peak)])
 
 
-def grad_body(n_seq, stats_ref, targets_ref, sequence_ref, response_ref, policy_ref, refer_ref, by_x_ref, by_y_ref, loss_ref):
+def grad_body(n_seq, stats_ref, targets_ref, sequence_ref, response_ref, policy_ref, refer_ref, grad_ref, loss_ref):
     tokens, cols = policy_ref.shape
     core_here, x, y, z = where_am_i()
     start_col = (((z * CORES + core_here) * RING + x) * RING + y) * cols
@@ -219,7 +216,7 @@
         span = slice(i * step, (i + 1) * step)
         per_row = packed[span]
         policy = policy_ref[span, :]
-        refer = refer_ref[span, :].astype(F32)
+        refer = in_token_order(refer_ref[span, :])
         column = lax.broadcasted_iota(jnp.int32, (step, cols), 1)
         hit = (column == per_row[:, 4:5].astype(jnp.int32)).astype(F32)
         probs = jnp.exp(policy - per_row[:, 0:1])
@@ -229,14 +226,10 @@
 
     row = lax.broadcasted_iota(jnp.int32, (tokens, tokens), 0)
     token = lax.broadcasted_iota(jnp.int32, (tokens, tokens), 1)
-    outer, inner, dz, core, t = row >> 7, (row >> 5) & 3, (row >> 3) & 3, (row >> 2) & 1, row & 3
-    base = (z ^ dz) * 128 + core * 64 + t
-    for ref, source in (
-        (by_x_ref, base + (x ^ outer) * 16 + (y ^ inner) * 4),
-        (by_y_ref, base + (x ^ inner) * 16 + (y ^ outer) * 4),
-    ):
-        pick = (token == source).astype(F32).astype(BF16)
-        ref[...] = jnp.dot(pick, grad, preferred_element_type=F32).astype(BF16)
+    dx, dy, dz, core, t = row >> 7, (row >> 5) & 3, (row >> 3) & 3, (row >> 2) & 1, row & 3
+    source = (z ^ dz) * 128 + core * 64 + (x ^ dx) * 16 + (y ^ dy) * 4 + t
+    pick = (token == source).astype(F32).astype(BF16)
+    grad_ref[...] = jnp.dot(pick, grad, preferred_element_type=F32).astype(BF16)
 
 
 def logit_grads(stats, targets, sequence, response, policy, refer, n_seq):
@@ -246,11 +239,10 @@
         functools.partial(grad_body, n_seq),
         out_shape=(
             jax.ShapeDtypeStruct((tokens, cols), BF16),
-            jax.ShapeDtypeStruct((tokens, cols), BF16),
             jax.ShapeDtypeStruct((8, 128), F32),
         ),
         in_specs=[vmem] * 6,
-        out_specs=(vmem, vmem, vmem),
+        out_specs=(vmem, vmem),
         compiler_params=params(24),
         cost_estimate=pl.CostEstimate(flops=2 * tokens * tokens * cols, bytes_accessed=10 * tokens * cols, transcendentals=tokens * cols),
         name="logit_grads",
@@ -262,67 +254,73 @@
 KEEPS = {1: (0, 3), 3: (0, 1)}
 
 
-def hidden_body(own_x, other_x, own_y, other_y, own_weight, other_weight, *refs):
-    outs, (grads, slabs, sems) = refs[:8], refs[8:]
-    tokens, cols = own_x.shape
+def hidden_body(own_grad, other_grad, own_weight, other_weight, *refs):
+    outs, (grads, slabs, results, sems) = refs[:8], refs[8:]
+    tokens, cols = own_grad.shape
     core = lax.axis_index("dp") & 1
     half = own_weight.shape[0] // CORES
     depth = half // 4
     step = depth // 2
     loads = [
-        pltpu.make_async_copy(ref, grads.at[i // 2, :, pl.ds((i % 2) * cols, cols)], sems.at[i])
-        for i, ref in enumerate((own_x, other_x, own_y, other_y))
+        pltpu.make_async_copy(ref, grads.at[:, pl.ds(i * cols, cols)], sems.at[i])
+        for i, ref in enumerate((own_grad, other_grad))
     ]
     fetches = []
     for i in range(8):
         rows = pl.ds(pl.multiple_of(core * half + i * step, step), step)
         fetches.append(
             [
-                pltpu.make_async_copy(ref.at[rows], slabs.at[i, :, pl.ds(n * cols, cols)], sems.at[4 + 2 * i + n])
+                pltpu.make_async_copy(ref.at[rows], slabs.at[i, :, pl.ds(n * cols, cols)], sems.at[2 + 2 * i + n])
                 for n, ref in enumerate((own_weight, other_weight))
             ]
         )
-    for copy in loads[:2] + sum(fetches[:4], []) + loads[2:] + sum(fetches[4:], []):
+    stores = [pltpu.make_async_copy(results.at[i], outs[i], sems.at[18 + i]) for i in range(8)]
+    for copy in loads + sum(fetches, []):
         copy.start()
-    quarter = tokens // RING
+    for copy in loads:
+        copy.wait()
+    unit = tokens // CHIPS
     for i in range(8):
         part = i // 2
-        if i % 4 == 0:
-            loads[i // 2].wait()
-            loads[i // 2 + 1].wait()
+        along_x, first = PARTS[part]
         for copy in fetches[i]:
             copy.wait()
-        product = lax.dot_general(
-            grads[i // 4], slabs[i], (((1,), (1,)), ((), ())), preferred_element_type=F32
-        ).astype(BF16)
-        first = PARTS[part][1]
-        for ref, order in ((outs[2 * part], SENDS[first]), (outs[2 * part + 1], KEEPS[first])):
-            for k, source in enumerate(order):
-                ref[k * quarter : (k + 1) * quarter, (i % 2) * step : (i % 2 + 1) * step] = product[
-                    source * quarter : (source + 1) * quarter
-                ]
-
-
-def hidden_parts(grads, weight, other_weight):
-    tokens, cols = grads[0].shape
+        product = lax.dot_general(grads[...], slabs[i], (((1,), (1,)), ((), ())), preferred_element_type=F32).astype(BF16)
+        for n, order in ((2 * part, SENDS[first]), (2 * part + 1, KEEPS[first])):
+            for k, outer in enumerate(order):
+                for inner in range(RING):
+                    source = (outer * RING + inner) if along_x else (inner * RING + outer)
+                    there = (k * RING + inner) * unit
+                    results[n, there : there + unit, (i % 2) * step : (i % 2 + 1) * step] = product[
+                        source * unit : (source + 1) * unit
+                    ]
+        if i % 2 == 1:
+            stores[2 * part].start()
+            stores[2 * part + 1].start()
+    for copy in stores:
+        copy.wait()
+
+
+def hidden_parts(own_grad, other_grad, weight, other_weight):
+    tokens, cols = own_grad.shape
     depth = weight.shape[0] // CORES // 4
-    vmem = pl.BlockSpec(memory_space=pltpu.VMEM)
     return pl.pallas_call(
         hidden_body,
         out_shape=(jax.ShapeDtypeStruct((tokens // 2, depth), BF16),) * 8,
-        in_specs=[any_spec()] * 6,
-        out_specs=(vmem,) * 8,
+        in_specs=[any_spec()] * 4,
+        out_specs=(any_spec(),) * 8,
         scratch_shapes=[
-            pltpu.VMEM((2, tokens, CORES * cols), BF16),
+            pltpu.VMEM((tokens, CORES * cols), BF16),
             pltpu.VMEM((8, depth // 2, CORES * cols), BF16),
-            pltpu.SemaphoreType.DMA((20,)),
+            pltpu.VMEM((8, tokens // 2, depth), BF16),
+            pltpu.SemaphoreType.DMA((26,)),
         ],
-        compiler_params=params(52),
+        compiler_params=params(50),
         cost_estimate=pl.CostEstimate(
             flops=16 * tokens * depth * cols, bytes_accessed=16 * cols * (tokens + depth) + 8 * tokens * depth, transcendentals=0
         ),
         name="hidden_parts",
-    )(*grads, weight, other_weight)
+    )(own_grad, other_grad, weight, other_weight)
 
 
 def add(*terms):
@@ -336,37 +334,49 @@
     rows, width = hidden.shape
     cols = weight.shape[1]
     half = width // CORES
-    piece = half // CHIPS
     dp, t = lax.axis_index("dp"), lax.axis_index("tensor")
     z, core = dp // CORES, dp % CORES
     x, y = t // RING, t % RING
 
+    piece = width // CHIPS
+    across = swap_z(lax.dynamic_slice_in_dim(hidden, t * piece, piece, axis=1), 2)
+    sent, across = lax.optimization_barrier((hidden, across))
+    near = [swap_z(sent, 1), swap_z(sent, 3)]
+    other_weight = swap_core(weight)
     theirs = swap_core(hidden)
-    sent_weight, theirs = lax.optimization_barrier((weight, theirs))
-    other_weight = swap_core(sent_weight)
-    across = jnp.concatenate(
-        [lax.dynamic_slice_in_dim(a, core * half + t * piece, piece, axis=1) for a in (hidden, theirs)], axis=0
+    ref_logits = ref_logits.reshape(RING, RING, CORES, CHIPS, cols)
+    ref_own, ref_other = [
+        lax.dynamic_index_in_dim(ref_logits, c, 2, keepdims=False).transpose(1, 2, 0, 3).reshape(RING * CHIPS, RING, cols)
+        for c in (core, 1 - core)
+    ]
+    ref_other = swap_core(ref_other)
+    ref_both = jnp.where(
+        core == 0, jnp.concatenate([ref_own, ref_other], axis=1), jnp.concatenate([ref_other, ref_own], axis=1)
     )
-    across = swap_z(across, 2)
-    sent, across = lax.optimization_barrier(((hidden, theirs), across))
-    pair = jnp.concatenate([lax.dynamic_slice_in_dim(a, core * half, half, axis=1) for a in sent], axis=0)
-    near = [swap_z(pair, 1), swap_z(pair, 3)]
-    by_x, by_y = across[None, :rows], across[None, rows:]
+    by_x, by_y = across[None, : rows // 2], across[None, rows // 2 :]
     for step_x, step_y in ((1, 4), (3, 12), (4, 1)):
-        by_x, by_y = (
-            jnp.concatenate([by_x, swap_tensor(by_x, step_x)], axis=0),
-            jnp.concatenate([by_y, swap_tensor(by_y, step_y)], axis=0),
-        )
-    gathered = [by_x, swap_tensor(by_x, 12), by_y, swap_tensor(by_y, 3)]
+        by_x = jnp.concatenate([by_x, swap_tensor(by_x, step_x)], axis=0)
+        by_y = jnp.concatenate([by_y, swap_tensor(by_y, step_y)], axis=0)
+        by_x, by_y = lax.optimization_barrier((by_x, by_y))
+    by_x, by_y, other_weight = lax.optimization_barrier((by_x, by_y, other_weight))
+    swapped = [swap_core(by_x), swap_core(by_y)]
+    late = [swap_tensor(by_x, 12), swap_tensor(by_y, 3)]
+    ref_both, swapped, late = lax.optimization_barrier((ref_both, swapped, late))
+    refer = lax.all_to_all(
+        ref_both,
+        ("dp", "tensor"),
+        split_axis=0,
+        concat_axis=0,
+        tiled=True,
+        axis_index_groups=[
+            [(ring * CORES + c) * CHIPS + chip for ring in range(RING) for chip in range(CHIPS)] for c in range(CORES)
+        ],
+    )
+    near, late = lax.optimization_barrier((near, late))
     near += [swap_core(a) for a in near]
-
-    ref_logits, gathered = lax.optimization_barrier((ref_logits, gathered))
-    refer = lax.all_to_all(
-        ref_logits.reshape(ref_logits.shape[0], -1, cols), ("dp", "tensor"), split_axis=1, concat_axis=0
-    )
-
-    swapped = [swap_core(a) for a in gathered]
-    policy = policy_logits(hidden, theirs, near, gathered + swapped, weight)
+    swapped += [swap_core(a) for a in late]
+    gathered = [by_x, late[0], by_y, late[1], swapped[0], swapped[2], swapped[1], swapped[3]]
+    policy = policy_logits(hidden, theirs, near, gathered, weight)
     refer, policy = lax.optimization_barrier((refer, policy))
     refer = refer.reshape(policy.shape)
     stats = row_stats(targets, policy, refer)
@@ -379,11 +389,10 @@
         stats = merge([stats] + [send(stats, o) for o in steps])
     stats = merge([stats, swap_core(stats)])
 
-    grad_x, grad_y, loss = logit_grads(stats, targets, sequence, response, policy, refer, 2 * RING * CORES)
-    grads = (grad_x, swap_core(grad_x), grad_y, swap_core(grad_y))
+    grad, loss = logit_grads(stats, targets, sequence, response, policy, refer, 2 * RING * CORES)
 
     sums = {4: [], 1: []}
-    products = hidden_parts(grads, weight, other_weight)
+    products = hidden_parts(grad, swap_core(grad), weight, other_weight)
     for part, (along_x, first) in enumerate(PARTS):
         send, keep = products[2 * part], products[2 * part + 1]
         axis = RING if along_x else 1

time: 180 us -> 163 us (0.906)
  waiting for transfers between devices: 63.1 us -> 46.6 us
    ppermute x9, waiting for transfers between devices: 22.6 us -> 8.22 us  [swap_z(): lax.ppermute(value, 'dp', [(i, i ^ offset * CORES) for i in range(RING *...]
    ppermute x12, waiting for transfers between devices: 8.13 us -> 4.11 us  [swap_core(): return lax.ppermute(value, 'dp', [(i, i ^ 1) for i in range(RING * CORES)])]
    ppermute x28, waiting for transfers between devices: 29.3 us -> 32.2 us  [swap_tensor(): lax.ppermute(value, 'tensor', [(i, i ^ offset) for i in range(CHIPS)])]
    unnamed x26 -> x19, local copies, waits for them, and re-layouts: 1.63 us -> 4.43 us
    ppermute x28, starting transfers between devices: 35.4 us -> 33.1 us  [swap_tensor(): lax.ppermute(value, 'tensor', [(i, i ^ offset) for i in range(CHIPS)])]
    ppermute x12, starting transfers between devices: 20 us -> 22.1 us  [swap_core(): return lax.ppermute(value, 'dp', [(i, i ^ 1) for i in range(RING * CORES)])]
    all_to_all x1, starting transfers between devices: 7.21 us -> 5.22 us  [shards(): lax.all_to_all(ref_both, ('dp', 'tensor'), split_axis=0, concat_axis=0, t...]
    convert_element_type x4, other arithmetic: 2.16 us -> 0.26 us  [shards(): add(keep[n:], got[n:]).astype(BF16)]
  transfers between devices with their start and end apart: 50 -> 50, of which waited for: 29 -> 25; matrix products, arithmetic and copies ran while one was open for 4% -> 4% of each run, Pallas kernels for 10% -> 8%
where the time goes in v2:
time: 163 us
  starting transfers between devices  74.7 us (46%)
  waiting for transfers between devices  46.6 us (29%)
  Pallas kernels  29.9 us (18%)
  local copies, waits for them, and re-layouts  6.81 us (4%)
  other arithmetic  4.04 us (2%)
    ppermute x28, starting transfers between devices, swap_tensor(): lax.ppermute(value, 'tensor', [(i, i ^ offset) for i in range(CHIPS)])  33.1 us
    ppermute x28, waiting for transfers between devices, swap_tensor(): lax.ppermute(value, 'tensor', [(i, i ^ offset) for i in range(CHIPS)])  32.2 us
    ppermute x12, starting transfers between devices, swap_core(): return lax.ppermute(value, 'dp', [(i, i ^ 1) for i in range(RING * CORES)])  22.1 us
    ppermute x9, starting transfers between devices, swap_z(): lax.ppermute(value, 'dp', [(i, i ^ offset * CORES) for i in range(RING *...  14.2 us
    pallas_call x1, Pallas kernels, policy_logits(): pl.pallas_call(logits_body, out_shape=jax.ShapeDtypeStruct((tokens, cols)...  13.1 us
    pallas_call x1, Pallas kernels, hidden_parts(): pl.pallas_call(hidden_body, out_shape=(jax.ShapeDtypeStruct((tokens // 2,...  12.5 us
    ppermute x9, waiting for transfers between devices, swap_z(): lax.ppermute(value, 'dp', [(i, i ^ offset * CORES) for i in range(RING *...  8.22 us
    all_to_all x1, starting transfers between devices, shards(): lax.all_to_all(ref_both, ('dp', 'tensor'), split_axis=0, concat_axis=0, t...  5.22 us
  transfers between devices with their start and end apart: 50, of which 25 were waited for; matrix products, arithmetic and copies ran while one was open for 4% of the time, Pallas kernels for 8%

profile of v2, /device:TPU:1, one launch (start us, length us, event | category | flops | bytes accessed | tf_op | source)
XLA Modules:
  0.0 163.1 jit_solution(8374530001341536256)
XLA Ops:
  0.6 1.5 collective-permute-start.8
  3.0 3.7 %collective-permute-start.1 = (bf16[64,512]{1,0:T(8,128)(2,1)S(1)}, bf16[64,512]{1,0:T(8,128)(2,1)S(1)}, u32[]{:S(2)}, u32[]{:S(2)}) collective-permute-start(bf16[64,512]{1,0:T(8,128)(2,1)S(1)} %constant_dynamic-slice_fusion), channel_id=1, source_target_pairs={{0,64},{16,80},{32,96},{48,112},{64,0},{80,16},{96,32},{112,48},{1... | collective-permute-start | bytes 196616 | tf_op jit(solution)/shard_map/ppermute | solution.py:26
  6.7 2.4 %collective-permute-done.1 = bf16[64,512]{1,0:T(8,128)(2,1)S(1)} collective-permute-done((bf16[64,512]{1,0:T(8,128)(2,1)S(1)}, bf16[64,512]{1,0:T(8,128)(2,1)S(1)}, u32[]{:S(2)}, u32[]{:S(2)}) %collective-permute-start.1) | collective-permute-done | bytes 65568 | tf_op jit(solution)/shard_map/ppermute | solution.py:26
  9.1 1.3 collective-permute-start.2
  10.4 1.2 collective-permute-start.3
  11.9 1.3 collective-permute-done.3
  13.2 1.9 %collective-permute-start.4 = (bf16[2,32,512]{2,1,0:T(8,128)(2,1)S(1)}, bf16[2,32,512]{2,1,0:T(8,128)(2,1)S(1)}, u32[]{:S(2)}, u32[]{:S(2)}) collective-permute-start(bf16[2,32,512]{2,1,0:T(8,128)(2,1)S(1)} %pad_maximum_fusion.7), channel_id=1, source_target_pairs={{0,3},{1,2},{2,1},{3,0},{4,7},{5,6},{6,5},{7,4},{8,11},{9,10},{10,... | collective-permute-start | bytes 196616 | tf_op jit(solution)/shard_map/ppermute | solution.py:22
  15.2 1.3 copy.78
  17.3 2.2 %collective-permute-start.15 = (bf16[64,8192]{1,0:T(8,128)(2,1)}, bf16[64,8192]{1,0:T(8,128)(2,1)}, u32[]{:S(2)}, u32[]{:S(2)}) collective-permute-start(bf16[64,8192]{1,0:T(8,128)(2,1)} %refs_0_.1), channel_id=1, source_target_pairs={{0,96},{16,112},{32,64},{48,80},{64,32},{80,48},{96,0},{112,16},{1... | collective-permute-start | bytes 3145736 | tf_op jit(solution)/shard_map/ppermute | solution.py:26
  19.6 2.5 %collective-permute-start.5 = (bf16[2,32,512]{2,1,0:T(8,128)(2,1)S(1)}, bf16[2,32,512]{2,1,0:T(8,128)(2,1)S(1)}, u32[]{:S(2)}, u32[]{:S(2)}) collective-permute-start(bf16[2,32,512]{2,1,0:T(8,128)(2,1)S(1)} %pad_maximum_fusion.8), channel_id=1, source_target_pairs={{0,12},{1,13},{2,14},{3,15},{4,8},{5,9},{6,10},{7,11},{8,4},{9,5},... | collective-permute-start | bytes 196616 | tf_op jit(solution)/shard_map/ppermute | solution.py:22
  22.1 1.8 %collective-permute-done.5 = bf16[2,32,512]{2,1,0:T(8,128)(2,1)S(1)} collective-permute-done((bf16[2,32,512]{2,1,0:T(8,128)(2,1)S(1)}, bf16[2,32,512]{2,1,0:T(8,128)(2,1)S(1)}, u32[]{:S(2)}, u32[]{:S(2)}) %collective-permute-start.5) | collective-permute-done | bytes 65568 | tf_op jit(solution)/shard_map/ppermute | solution.py:22
  25.5 2.7 %collective-permute-done.6 = bf16[4,32,512]{2,1,0:T(8,128)(2,1)S(1)} collective-permute-done((bf16[4,32,512]{2,1,0:T(8,128)(2,1)S(1)}, bf16[4,32,512]{2,1,0:T(8,128)(2,1)S(1)}, u32[]{:S(2)}, u32[]{:S(2)}) %collective-permute-start.6) | collective-permute-done | bytes 131104 | tf_op jit(solution)/shard_map/ppermute | solution.py:22
  28.2 5.0 %collective-permute-start = (bf16[64,4,896]{2,1,0:T(4,128)(2,1)S(1)}, bf16[64,4,896]{2,1,0:T(4,128)(2,1)S(1)}, u32[]{:S(2)}, u32[]{:S(2)}) collective-permute-start(bf16[64,4,896]{2,1,0:T(4,128)(2,1)S(1)} %copy.35), channel_id=1, source_target_pairs={{0,16},{16,0},{32,48},{48,32},{64,80},{80,64},{96,112},{112,96},{1... | collective-permute-start | bytes 1376264 | tf_op jit(solution)/shard_map/ppermute | solution.py:30
  34.6 2.5 %collective-permute-start.11 = (bf16[8,32,512]{2,1,0:T(8,128)(2,1)S(1)}, bf16[8,32,512]{2,1,0:T(8,128)(2,1)S(1)}, u32[]{:S(2)}, u32[]{:S(2)}) collective-permute-start(bf16[8,32,512]{2,1,0:T(8,128)(2,1)S(1)} %pad_maximum_fusion.refs_6_), channel_id=1, source_target_pairs={{0,12},{1,13},{2,14},{3,15},{4,8},{5,9},{6,10},{7,11},{8,4},{9,5},... | collective-permute-start | bytes 786440 | tf_op jit(solution)/shard_map/ppermute | solution.py:22
  38.3 1.8 %maximum_select_fusion = bf16[64,8,896]{2,1,0:T(8,128)(2,1)} fusion(bf16[64,4,896]{2,1,0:T(4,128)(2,1)S(1)} %collective-permute-done, bf16[64,4,896]{2,1,0:T(4,128)(2,1)S(1)} %copy.36, pred[]{:T(512)S(6)} %eq.6), kind=kLoop, calls=%fused_computation | loop fusion | flops 4128768 | bytes 1835009 | tf_op jit(solution)/shard_map/jit(_where)/select_n | solution.py:353
  41.0 2.5 %collective-permute-done.11.refs_7_ = bf16[8,32,512]{2,1,0:T(8,128)(2,1)S(1)} collective-permute-done((bf16[8,32,512]{2,1,0:T(8,128)(2,1)S(1)}, bf16[8,32,512]{2,1,0:T(8,128)(2,1)S(1)}, u32[]{:S(2)}, u32[]{:S(2)}) %collective-permute-start.11) | collective-permute-done | bytes 262176 | tf_op jit(solution)/shard_map/ppermute | solution.py:22
  43.5 2.1 %collective-permute-done.12.refs_9_ = bf16[8,32,512]{2,1,0:T(8,128)(2,1)S(1)} collective-permute-done((bf16[8,32,512]{2,1,0:T(8,128)(2,1)S(1)}, bf16[8,32,512]{2,1,0:T(8,128)(2,1)S(1)}, u32[]{:S(2)}, u32[]{:S(2)}) %collective-permute-start.12) | collective-permute-done | bytes 262176 | tf_op jit(solution)/shard_map/ppermute | solution.py:22
  45.5 1.5 collective-permute-start.16
  47.7 5.2 %all-to-all-start = ((bf16[64,8,896]{2,1,0:T(8,128)(2,1)}), bf16[64,8,896]{2,1,0:T(8,128)(2,1)S(1)}, u32[]{:S(2)}, u32[]{:S(2)}) async-start(bf16[64,8,896]{2,1,0:T(8,128)(2,1)} %maximum_select_fusion), calls=%async_computation | async-start | bytes 1835008 | tf_op jit(solution)/shard_map/all_to_all | solution.py:365
  53.6 13.1 %policy_logits.1.policy_ref = f32[512,896]{1,0:T(8,128)} custom-call(bf16[64,8192]{1,0:T(8,128)(2,1)} %refs_0_.1, bf16[64,8192]{1,0:T(8,128)(2,1)} %collective-permute-done.13.refs_1_, bf16[64,8192]{1,0:T(8,128)(2,1)} %collective-permute-done.14.refs_2_, bf16[64,8192]{1,0:T(8,128)(2,1)} %collective-permute-done.15.refs_3_, ...), custom_call_target="tpu_custom_call" | custom-call | flops 7516192768 | bytes 24903680 | tf_op jit(solution)/shard_map/policy_logits/pallas_call | solution.py:97
  66.7 2.1 %all-to-all-done = bf16[64,8,896]{2,1,0:T(8,128)(2,1)S(1)} async-done(((bf16[64,8,896]{2,1,0:T(8,128)(2,1)}), bf16[64,8,896]{2,1,0:T(8,128)(2,1)S(1)}, u32[]{:S(2)}, u32[]{:S(2)}) %all-to-all-start) | async-done | bytes 917536 | tf_op jit(solution)/shard_map/all_to_all | solution.py:365
  68.8 1.5 copy-done
  70.3 2.3 %row_stats.1 = f32[8,512]{1,0:T(8,128)S(1)} custom-call(s32[512]{0:T(512)S(1)} %copy-done.3, f32[512,896]{1,0:T(8,128)S(1)} %copy-done, bf16[512,896]{1,0:T(8,128)(2,1)S(1)} %bitcast.195), custom_call_target="tpu_custom_call" | custom-call | flops 9175040 | bytes 2752512 | tf_op jit(solution)/shard_map/row_stats/pallas_call | solution.py:151
  73.4 1.7 %collective-permute-start.21 = (f32[8,512]{1,0:T(8,128)S(1)}, f32[8,512]{1,0:T(8,128)S(1)}, u32[]{:S(2)}, u32[]{:S(2)}) collective-permute-start(f32[8,512]{1,0:T(8,128)S(1)} %row_stats.1), channel_id=1, source_target_pairs={{0,2},{1,3},{2,0},{3,1},{4,6},{5,7},{6,4},{7,5},{8,10},{9,11},{10,... | collective-permute-start | bytes 49160 | tf_op jit(solution)/shard_map/ppermute | solution.py:22
  77.9 1.6 collective-permute-start.25
  80.0 1.2 collective-permute-start.23
  81.7 1.8 %collective-permute-done.24 = f32[8,512]{1,0:T(8,128)S(1)} collective-permute-done((f32[8,512]{1,0:T(8,128)S(1)}, f32[8,512]{1,0:T(8,128)S(1)}, u32[]{:S(2)}, u32[]{:S(2)}) %collective-permute-start.24) | collective-permute-done | bytes 16416 | tf_op jit(solution)/shard_map/ppermute | solution.py:22
  83.7 2.8 %collective-permute-start.28 = (f32[8,512]{1,0:T(8,128)S(1)}, f32[8,512]{1,0:T(8,128)S(1)}, u32[]{:S(2)}, u32[]{:S(2)}) collective-permute-start(f32[8,512]{1,0:T(8,128)S(1)} %stack.175), channel_id=1, source_target_pairs={{0,96},{16,112},{32,64},{48,80},{64,32},{80,48},{96,0},{112,16},{1... | collective-permute-start | bytes 49160 | tf_op jit(solution)/shard_map/ppermute | solution.py:26
  87.6 3.0 %collective-permute-done.27 = f32[8,512]{1,0:T(8,128)S(1)} collective-permute-done((f32[8,512]{1,0:T(8,128)S(1)}, f32[8,512]{1,0:T(8,128)S(1)}, u32[]{:S(2)}, u32[]{:S(2)}) %collective-permute-start.27) | collective-permute-done | bytes 16416 | tf_op jit(solution)/shard_map/ppermute | solution.py:26
  90.8 5.4 %collective-permute-start.29 = (f32[8,512]{1,0:T(8,128)S(1)}, f32[8,512]{1,0:T(8,128)S(1)}, u32[]{:S(2)}, u32[]{:S(2)}) collective-permute-start(f32[8,512]{1,0:T(8,128)S(1)} %stack.188), channel_id=1, source_target_pairs={{0,16},{16,0},{32,48},{48,32},{64,80},{80,64},{96,112},{112,96},{1... | collective-permute-start | bytes 49160 | tf_op jit(solution)/shard_map/ppermute | solution.py:30
  97.2 2.1 %logit_grads.1 = (bf16[512,896]{1,0:T(8,128)(2,1)S(1)}, f32[8,128]{1,0:T(8,128)S(1)}) custom-call(f32[8,512]{1,0:T(8,128)S(1)} %stack.199.stats_ref, s32[512]{0:T(512)S(1)} %copy-done.3, s32[512]{0:T(512)S(1)} %copy-done.4, s32[512]{0:T(512)S(1)} %copy-done.5, f32[512,896]{1,0:T(8,128)S(1)} %copy-done.1, bf16[512,896]{1,0:T(8,128)(2,1)S(1)} %bitcast.196), custom_call_target="tpu_custom_call" | custom-call | flops 469762048 | bytes 4587520 | tf_op jit(solution)/shard_map/logit_grads/pallas_call | solution.py:238
  99.9 2.1 %collective-permute-done.30.other_grad = bf16[512,896]{1,0:T(8,128)(2,1)S(1)} collective-permute-done((bf16[512,896]{1,0:T(8,128)(2,1)S(1)}, bf16[512,896]{1,0:T(8,128)(2,1)S(1)}, u32[]{:S(2)}, u32[]{:S(2)}) %collective-permute-start.30) | collective-permute-done | bytes 917536 | tf_op jit(solution)/shard_map/ppermute | solution.py:30
  103.0 12.5 %hidden_parts.1 = (bf16[256,1024]{1,0:T(8,128)(2,1)S(1)}, bf16[256,1024]{1,0:T(8,128)(2,1)S(1)}, bf16[256,1024]{1,0:T(8,128)(2,1)S(1)}, bf16[256,1024]{1,0:T(8,1...) custom-call(bf16[512,896]{1,0:T(8,128)(2,1)} %copy-done.2, ...), custom_call_target="tpu_custom_call" | custom-call | flops 7516192768 | bytes 26214400 | tf_op jit(solution)/shard_map/hidden_parts/pallas_call | solution.py:307
  115.6 2.0 %collective-permute-start.33 = (bf16[256,1024]{1,0:T(8,128)(2,1)S(1)}, bf16[256,1024]{1,0:T(8,128)(2,1)S(1)}, u32[]{:S(2)}, u32[]{:S(2)}) collective-permute-start(bf16[256,1024]{1,0:T(8,128)(2,1)S(1)} %get-tuple-element.60), channel_id=1, source_target_pairs={{0,12},{1,13},{2,14},{3,15},{4,8},{5,9},{6,10},{7,11},{8,4},{9,5},... | collective-permute-start | bytes 1572872 | tf_op jit(solution)/shard_map/ppermute | solution.py:22
  117.6 2.0 %collective-permute-start.40 = (bf16[256,1024]{1,0:T(8,128)(2,1)S(1)}, bf16[256,1024]{1,0:T(8,128)(2,1)S(1)}, u32[]{:S(2)}, u32[]{:S(2)}) collective-permute-start(bf16[256,1024]{1,0:T(8,128)(2,1)S(1)} %get-tuple-element.64), channel_id=1, source_target_pairs={{0,3},{1,2},{2,1},{3,0},{4,7},{5,6},{6,5},{7,4},{8,11},{9,10},{10,... | collective-permute-start | bytes 1572872 | tf_op jit(solution)/shard_map/ppermute | solution.py:22
  119.7 9.1 %collective-permute-done.31 = bf16[256,1024]{1,0:T(8,128)(2,1)S(1)} collective-permute-done((bf16[256,1024]{1,0:T(8,128)(2,1)S(1)}, bf16[256,1024]{1,0:T(8,128)(2,1)S(1)}, u32[]{:S(2)}, u32[]{:S(2)}) %collective-permute-start.31) | collective-permute-done | bytes 524320 | tf_op jit(solution)/shard_map/ppermute | solution.py:22
  128.9 1.2 collective-permute-start.32
  130.6 1.2 collective-permute-start.39
  132.2 4.5 %collective-permute-done.32 = bf16[128,1024]{1,0:T(8,128)(2,1)S(1)} collective-permute-done((bf16[128,1024]{1,0:T(8,128)(2,1)S(1)}, bf16[128,1024]{1,0:T(8,128)(2,1)S(1)}, u32[]{:S(2)}, u32[]{:S(2)}) %collective-permute-start.32) | collective-permute-done | bytes 262176 | tf_op jit(solution)/shard_map/ppermute | solution.py:22
  137.1 1.2 collective-permute-start.37
  138.6 2.4 %collective-permute-start.35 = (bf16[32,2048]{1,0:T(8,128)(2,1)S(1)}, bf16[32,2048]{1,0:T(8,128)(2,1)S(1)}, u32[]{:S(2)}, u32[]{:S(2)}) collective-permute-start(bf16[32,2048]{1,0:T(8,128)(2,1)S(1)} %get-tuple-element.100), channel_id=1, source_target_pairs={{0,2},{1,3},{2,0},{3,1},{4,6},{5,7},{6,4},{7,5},{8,10},{9,11},{10,... | collective-permute-start | bytes 393224 | tf_op jit(solution)/shard_map/ppermute | solution.py:22
  141.3 1.3 collective-permute-start.44
  142.7 2.6 %collective-permute-start.42 = (bf16[32,2048]{1,0:T(8,128)(2,1)S(1)}, bf16[32,2048]{1,0:T(8,128)(2,1)S(1)}, u32[]{:S(2)}, u32[]{:S(2)}) collective-permute-start(bf16[32,2048]{1,0:T(8,128)(2,1)S(1)} %get-tuple-element.103), channel_id=1, source_target_pairs={{0,8},{1,9},{2,10},{3,11},{4,12},{5,13},{6,14},{7,15},{8,0},{9,1},... | collective-permute-start | bytes 393224 | tf_op jit(solution)/shard_map/ppermute | solution.py:22
  145.4 1.4 collective-permute-done.44
  146.8 2.3 %collective-permute-done.42 = bf16[32,2048]{1,0:T(8,128)(2,1)S(1)} collective-permute-done((bf16[32,2048]{1,0:T(8,128)(2,1)S(1)}, bf16[32,2048]{1,0:T(8,128)(2,1)S(1)}, u32[]{:S(2)}, u32[]{:S(2)}) %collective-permute-start.42) | collective-permute-done | bytes 131104 | tf_op jit(solution)/shard_map/ppermute | solution.py:22
  150.7 2.4 %collective-permute-start.45 = (bf16[8,4096]{1,0:T(8,128)(2,1)S(1)}, bf16[8,4096]{1,0:T(8,128)(2,1)S(1)}, u32[]{:S(2)}, u32[]{:S(2)}) collective-permute-start(bf16[8,4096]{1,0:T(8,128)(2,1)S(1)} %get-tuple-element.106), channel_id=1, source_target_pairs={{0,64},{16,80},{32,96},{48,112},{64,0},{80,16},{96,32},{112,48},{1... | collective-permute-start | bytes 196616 | tf_op jit(solution)/shard_map/ppermute | solution.py:26
  153.6 1.9 %collective-permute-done.45 = bf16[8,4096]{1,0:T(8,128)(2,1)S(1)} collective-permute-done((bf16[8,4096]{1,0:T(8,128)(2,1)S(1)}, bf16[8,4096]{1,0:T(8,128)(2,1)S(1)}, u32[]{:S(2)}, u32[]{:S(2)}) %collective-permute-start.45) | collective-permute-done | bytes 65568 | tf_op jit(solution)/shard_map/ppermute | solution.py:26
  155.6 5.9 %collective-permute-start.48 = (bf16[4,4096]{1,0:T(4,128)(2,1)S(1)}, bf16[4,4096]{1,0:T(4,128)(2,1)S(1)}, u32[]{:S(2)}, u32[]{:S(2)}) collective-permute-start(bf16[4,4096]{1,0:T(4,128)(2,1)S(1)} %get-tuple-element.110), channel_id=1, source_target_pairs={{0,16},{16,0},{32,48},{48,32},{64,80},{80,64},{96,112},{112,96},{1... | collective-permute-start | bytes 98312 | tf_op jit(solution)/shard_map/ppermute | solution.py:30
  (124 shorter events, 23.0 us)
Async XLA Ops:
  0.6 32.6 %collective-permute-start.8 = (bf16[8192,896]{1,0:T(8,128)(2,1)}, bf16[8192,896]{1,0:T(8,128)(2,1)}, u32[]{:S(2)}, u32[]{:S(2)}) collective-permute-start(bf16[8192,896]{1,0:T(8,128)(2,1)} %own_weight.1), channel_id=1, source_target_pairs={{0,16},{16,0},{32,48},{48,32},{64,80},{80,64},{96,112},{112,96},{1... | collective-permute-start | bytes 44040200 | tf_op jit(solution)/shard_map/ppermute | solution.py:30
  3.0 6.1 %collective-permute-start.1 = (bf16[64,512]{1,0:T(8,128)(2,1)S(1)}, bf16[64,512]{1,0:T(8,128)(2,1)S(1)}, u32[]{:S(2)}, u32[]{:S(2)}) collective-permute-start(bf16[64,512]{1,0:T(8,128)(2,1)S(1)} %constant_dynamic-slice_fusion), channel_id=1, source_target_pairs={{0,64},{16,80},{32,96},{48,112},{64,0},{80,16},{96,32},{112,48},{1... | collective-permute-start | bytes 196616 | tf_op jit(solution)/shard_map/ppermute | solution.py:26
  10.4 2.8 %collective-permute-start.3 = (bf16[1,32,512]{2,1,0:T(8,128)(2,1)S(1)}, bf16[1,32,512]{2,1,0:T(8,128)(2,1)S(1)}, u32[]{:S(2)}, u32[]{:S(2)}) collective-permute-start(bf16[1,32,512]{2,1,0:T(8,128)(2,1)S(1)} %get-tuple-element.132), channel_id=1, source_target_pairs={{0,4},{1,5},{2,6},{3,7},{4,0},{5,1},{6,2},{7,3},{8,12},{9,13},{10,... | collective-permute-start | bytes 98312 | tf_op jit(solution)/shard_map/ppermute | solution.py:22
  13.2 8.8 %collective-permute-start.4 = (bf16[2,32,512]{2,1,0:T(8,128)(2,1)S(1)}, bf16[2,32,512]{2,1,0:T(8,128)(2,1)S(1)}, u32[]{:S(2)}, u32[]{:S(2)}) collective-permute-start(bf16[2,32,512]{2,1,0:T(8,128)(2,1)S(1)} %pad_maximum_fusion.7), channel_id=1, source_target_pairs={{0,3},{1,2},{2,1},{3,0},{4,7},{5,6},{6,5},{7,4},{8,11},{9,10},{10,... | collective-permute-start | bytes 196616 | tf_op jit(solution)/shard_map/ppermute | solution.py:22
  16.5 29.1 %collective-permute-start.14 = (bf16[64,8192]{1,0:T(8,128)(2,1)}, bf16[64,8192]{1,0:T(8,128)(2,1)}, u32[]{:S(2)}, u32[]{:S(2)}) collective-permute-start(bf16[64,8192]{1,0:T(8,128)(2,1)} %refs_0_.1), channel_id=1, source_target_pairs={{0,32},{16,48},{32,0},{48,16},{64,96},{80,112},{96,64},{112,80},{1... | collective-permute-start | bytes 3145736 | tf_op jit(solution)/shard_map/ppermute | solution.py:26
  17.3 28.2 %collective-permute-start.15 = (bf16[64,8192]{1,0:T(8,128)(2,1)}, bf16[64,8192]{1,0:T(8,128)(2,1)}, u32[]{:S(2)}, u32[]{:S(2)}) collective-permute-start(bf16[64,8192]{1,0:T(8,128)(2,1)} %refs_0_.1), channel_id=1, source_target_pairs={{0,96},{16,112},{32,64},{48,80},{64,32},{80,48},{96,0},{112,16},{1... | collective-permute-start | bytes 3145736 | tf_op jit(solution)/shard_map/ppermute | solution.py:26
  19.6 4.3 %collective-permute-start.5 = (bf16[2,32,512]{2,1,0:T(8,128)(2,1)S(1)}, bf16[2,32,512]{2,1,0:T(8,128)(2,1)S(1)}, u32[]{:S(2)}, u32[]{:S(2)}) collective-permute-start(bf16[2,32,512]{2,1,0:T(8,128)(2,1)S(1)} %pad_maximum_fusion.8), channel_id=1, source_target_pairs={{0,12},{1,13},{2,14},{3,15},{4,8},{5,9},{6,10},{7,11},{8,4},{9,5},... | collective-permute-start | bytes 196616 | tf_op jit(solution)/shard_map/ppermute | solution.py:22
  23.9 4.3 %collective-permute-start.6 = (bf16[4,32,512]{2,1,0:T(8,128)(2,1)S(1)}, bf16[4,32,512]{2,1,0:T(8,128)(2,1)S(1)}, u32[]{:S(2)}, u32[]{:S(2)}) collective-permute-start(bf16[4,32,512]{2,1,0:T(8,128)(2,1)S(1)} %pad_maximum_fusion.4), channel_id=1, source_target_pairs={{0,4},{1,5},{2,6},{3,7},{4,0},{5,1},{6,2},{7,3},{8,12},{9,13},{10,... | collective-permute-start | bytes 393224 | tf_op jit(solution)/shard_map/ppermute | solution.py:22
  24.4 8.8 %collective-permute-start.7 = (bf16[4,32,512]{2,1,0:T(8,128)(2,1)S(1)}, bf16[4,32,512]{2,1,0:T(8,128)(2,1)S(1)}, u32[]{:S(2)}, u32[]{:S(2)}) collective-permute-start(bf16[4,32,512]{2,1,0:T(8,128)(2,1)S(1)} %pad_maximum_fusion.5), channel_id=1, source_target_pairs={{0,1},{1,0},{2,3},{3,2},{4,5},{5,4},{6,7},{7,6},{8,9},{9,8},{10,11... | collective-permute-start | bytes 393224 | tf_op jit(solution)/shard_map/ppermute | solution.py:22
  28.2 6.4 %collective-permute-start = (bf16[64,4,896]{2,1,0:T(4,128)(2,1)S(1)}, bf16[64,4,896]{2,1,0:T(4,128)(2,1)S(1)}, u32[]{:S(2)}, u32[]{:S(2)}) collective-permute-start(bf16[64,4,896]{2,1,0:T(4,128)(2,1)S(1)} %copy.35), channel_id=1, source_target_pairs={{0,16},{16,0},{32,48},{48,32},{64,80},{80,64},{96,112},{112,96},{1... | collective-permute-start | bytes 1376264 | tf_op jit(solution)/shard_map/ppermute | solution.py:30
  33.3 3.8 %collective-permute-start.9 = (bf16[8,32,512]{2,1,0:T(8,128)(2,1)S(1)}, bf16[8,32,512]{2,1,0:T(8,128)(2,1)S(1)}, u32[]{:S(2)}, u32[]{:S(2)}) collective-permute-start(bf16[8,32,512]{2,1,0:T(8,128)(2,1)S(1)} %pad_maximum_fusion.refs_6_), channel_id=1, source_target_pairs={{0,16},{16,0},{32,48},{48,32},{64,80},{80,64},{96,112},{112,96},{1... | collective-permute-start | bytes 786440 | tf_op jit(solution)/shard_map/ppermute | solution.py:30
  33.6 6.4 %collective-permute-start.10 = (bf16[8,32,512]{2,1,0:T(8,128)(2,1)S(1)}, bf16[8,32,512]{2,1,0:T(8,128)(2,1)S(1)}, u32[]{:S(2)}, u32[]{:S(2)}) collective-permute-start(bf16[8,32,512]{2,1,0:T(8,128)(2,1)S(1)} %pad_maximum_fusion.1.refs_8_), channel_id=1, source_target_pairs={{0,16},{16,0},{32,48},{48,32},{64,80},{80,64},{96,112},{112,96},{1... | collective-permute-start | bytes 786440 | tf_op jit(solution)/shard_map/ppermute | solution.py:30
  34.6 8.8 %collective-permute-start.11 = (bf16[8,32,512]{2,1,0:T(8,128)(2,1)S(1)}, bf16[8,32,512]{2,1,0:T(8,128)(2,1)S(1)}, u32[]{:S(2)}, u32[]{:S(2)}) collective-permute-start(bf16[8,32,512]{2,1,0:T(8,128)(2,1)S(1)} %pad_maximum_fusion.refs_6_), channel_id=1, source_target_pairs={{0,12},{1,13},{2,14},{3,15},{4,8},{5,9},{6,10},{7,11},{8,4},{9,5},... | collective-permute-start | bytes 786440 | tf_op jit(solution)/shard_map/ppermute | solution.py:22
  37.1 8.4 %collective-permute-start.12 = (bf16[8,32,512]{2,1,0:T(8,128)(2,1)S(1)}, bf16[8,32,512]{2,1,0:T(8,128)(2,1)S(1)}, u32[]{:S(2)}, u32[]{:S(2)}) collective-permute-start(bf16[8,32,512]{2,1,0:T(8,128)(2,1)S(1)} %pad_maximum_fusion.1.refs_8_), channel_id=1, source_target_pairs={{0,3},{1,2},{2,1},{3,0},{4,7},{5,6},{6,5},{7,4},{8,11},{9,10},{10,... | collective-permute-start | bytes 786440 | tf_op jit(solution)/shard_map/ppermute | solution.py:22
  40.0 12.9 %collective-permute-start.13 = (bf16[64,8192]{1,0:T(8,128)(2,1)}, bf16[64,8192]{1,0:T(8,128)(2,1)}, u32[]{:S(2)}, u32[]{:S(2)}) collective-permute-start(bf16[64,8192]{1,0:T(8,128)(2,1)} %refs_0_.1), channel_id=1, source_target_pairs={{0,16},{16,0},{32,48},{48,32},{64,80},{80,64},{96,112},{112,96},{1... | collective-permute-start | bytes 3145736 | tf_op jit(solution)/shard_map/ppermute | solution.py:30
  45.5 7.4 %collective-permute-start.16 = (bf16[64,8192]{1,0:T(8,128)(2,1)}, bf16[64,8192]{1,0:T(8,128)(2,1)}, u32[]{:S(2)}, u32[]{:S(2)}) collective-permute-start(bf16[64,8192]{1,0:T(8,128)(2,1)} %collective-permute-done.14.refs_2_), channel_id=1, source_target_pairs={{0,16},{16,0},{32,48},{48,32},{64,80},{80,64},{96,112},{112,96},{1... | collective-permute-start | bytes 3145736 | tf_op jit(solution)/shard_map/ppermute | solution.py:30
  47.1 5.9 %collective-permute-start.17 = (bf16[64,8192]{1,0:T(8,128)(2,1)}, bf16[64,8192]{1,0:T(8,128)(2,1)}, u32[]{:S(2)}, u32[]{:S(2)}) collective-permute-start(bf16[64,8192]{1,0:T(8,128)(2,1)} %collective-permute-done.15.refs_3_), channel_id=1, source_target_pairs={{0,16},{16,0},{32,48},{48,32},{64,80},{80,64},{96,112},{112,96},{1... | collective-permute-start | bytes 3145736 | tf_op jit(solution)/shard_map/ppermute | solution.py:30
  47.2 5.8 %collective-permute-start.18 = (bf16[8,32,512]{2,1,0:T(8,128)(2,1)S(1)}, bf16[8,32,512]{2,1,0:T(8,128)(2,1)S(1)}, u32[]{:S(2)}, u32[]{:S(2)}) collective-permute-start(bf16[8,32,512]{2,1,0:T(8,128)(2,1)S(1)} %collective-permute-done.11.refs_7_), channel_id=1, source_target_pairs={{0,16},{16,0},{32,48},{48,32},{64,80},{80,64},{96,112},{112,96},{1... | collective-permute-start | bytes 786440 | tf_op jit(solution)/shard_map/ppermute | solution.py:30
  47.6 5.3 %collective-permute-start.19 = (bf16[8,32,512]{2,1,0:T(8,128)(2,1)S(1)}, bf16[8,32,512]{2,1,0:T(8,128)(2,1)S(1)}, u32[]{:S(2)}, u32[]{:S(2)}) collective-permute-start(bf16[8,32,512]{2,1,0:T(8,128)(2,1)S(1)} %collective-permute-done.12.refs_9_), channel_id=1, source_target_pairs={{0,16},{16,0},{32,48},{48,32},{64,80},{80,64},{96,112},{112,96},{1... | collective-permute-start | bytes 786440 | tf_op jit(solution)/shard_map/ppermute | solution.py:30
  47.7 21.1 %all-to-all-start = ((bf16[64,8,896]{2,1,0:T(8,128)(2,1)}), bf16[64,8,896]{2,1,0:T(8,128)(2,1)S(1)}, u32[]{:S(2)}, u32[]{:S(2)}) async-start(bf16[64,8,896]{2,1,0:T(8,128)(2,1)} %maximum_select_fusion), calls=%async_computation | async-start | bytes 1835008 | tf_op jit(solution)/shard_map/all_to_all | solution.py:365
  72.6 3.9 %collective-permute-start.22 = (f32[8,512]{1,0:T(8,128)S(1)}, f32[8,512]{1,0:T(8,128)S(1)}, u32[]{:S(2)}, u32[]{:S(2)}) collective-permute-start(f32[8,512]{1,0:T(8,128)S(1)} %row_stats.1), channel_id=1, source_target_pairs={{0,3},{1,2},{2,1},{3,0},{4,7},{5,6},{6,5},{7,4},{8,11},{9,10},{10,... | collective-permute-start | bytes 49160 | tf_op jit(solution)/shard_map/ppermute | solution.py:22
  73.4 4.1 %collective-permute-start.21 = (f32[8,512]{1,0:T(8,128)S(1)}, f32[8,512]{1,0:T(8,128)S(1)}, u32[]{:S(2)}, u32[]{:S(2)}) collective-permute-start(f32[8,512]{1,0:T(8,128)S(1)} %row_stats.1), channel_id=1, source_target_pairs={{0,2},{1,3},{2,0},{3,1},{4,6},{5,7},{6,4},{7,5},{8,10},{9,11},{10,... | collective-permute-start | bytes 49160 | tf_op jit(solution)/shard_map/ppermute | solution.py:22
  77.9 3.9 %collective-permute-start.25 = (f32[8,512]{1,0:T(8,128)S(1)}, f32[8,512]{1,0:T(8,128)S(1)}, u32[]{:S(2)}, u32[]{:S(2)}) collective-permute-start(f32[8,512]{1,0:T(8,128)S(1)} %stack.162), channel_id=1, source_target_pairs={{0,12},{1,13},{2,14},{3,15},{4,8},{5,9},{6,10},{7,11},{8,4},{9,5},... | collective-permute-start | bytes 49160 | tf_op jit(solution)/shard_map/ppermute | solution.py:22
  79.4 4.1 %collective-permute-start.24 = (f32[8,512]{1,0:T(8,128)S(1)}, f32[8,512]{1,0:T(8,128)S(1)}, u32[]{:S(2)}, u32[]{:S(2)}) collective-permute-start(f32[8,512]{1,0:T(8,128)S(1)} %stack.162), channel_id=1, source_target_pairs={{0,8},{1,9},{2,10},{3,11},{4,12},{5,13},{6,14},{7,15},{8,0},{9,1},... | collective-permute-start | bytes 49160 | tf_op jit(solution)/shard_map/ppermute | solution.py:22
  80.0 3.5 %collective-permute-start.23 = (f32[8,512]{1,0:T(8,128)S(1)}, f32[8,512]{1,0:T(8,128)S(1)}, u32[]{:S(2)}, u32[]{:S(2)}) collective-permute-start(f32[8,512]{1,0:T(8,128)S(1)} %stack.162), channel_id=1, source_target_pairs={{0,4},{1,5},{2,6},{3,7},{4,0},{5,1},{6,2},{7,3},{8,12},{9,13},{10,... | collective-permute-start | bytes 49160 | tf_op jit(solution)/shard_map/ppermute | solution.py:22
  83.7 3.9 %collective-permute-start.28 = (f32[8,512]{1,0:T(8,128)S(1)}, f32[8,512]{1,0:T(8,128)S(1)}, u32[]{:S(2)}, u32[]{:S(2)}) collective-permute-start(f32[8,512]{1,0:T(8,128)S(1)} %stack.175), channel_id=1, source_target_pairs={{0,96},{16,112},{32,64},{48,80},{64,32},{80,48},{96,0},{112,16},{1... | collective-permute-start | bytes 49160 | tf_op jit(solution)/shard_map/ppermute | solution.py:26
  86.5 4.1 %collective-permute-start.27 = (f32[8,512]{1,0:T(8,128)S(1)}, f32[8,512]{1,0:T(8,128)S(1)}, u32[]{:S(2)}, u32[]{:S(2)}) collective-permute-start(f32[8,512]{1,0:T(8,128)S(1)} %stack.175), channel_id=1, source_target_pairs={{0,64},{16,80},{32,96},{48,112},{64,0},{80,16},{96,32},{112,48},{1... | collective-permute-start | bytes 49160 | tf_op jit(solution)/shard_map/ppermute | solution.py:26
  86.9 3.7 %collective-permute-start.26 = (f32[8,512]{1,0:T(8,128)S(1)}, f32[8,512]{1,0:T(8,128)S(1)}, u32[]{:S(2)}, u32[]{:S(2)}) collective-permute-start(f32[8,512]{1,0:T(8,128)S(1)} %stack.175), channel_id=1, source_target_pairs={{0,32},{16,48},{32,0},{48,16},{64,96},{80,112},{96,64},{112,80},{1... | collective-permute-start | bytes 49160 | tf_op jit(solution)/shard_map/ppermute | solution.py:26
  90.8 6.3 %collective-permute-start.29 = (f32[8,512]{1,0:T(8,128)S(1)}, f32[8,512]{1,0:T(8,128)S(1)}, u32[]{:S(2)}, u32[]{:S(2)}) collective-permute-start(f32[8,512]{1,0:T(8,128)S(1)} %stack.188), channel_id=1, source_target_pairs={{0,16},{16,0},{32,48},{48,32},{64,80},{80,64},{96,112},{112,96},{1... | collective-permute-start | bytes 49160 | tf_op jit(solution)/shard_map/ppermute | solution.py:30
  99.3 2.8 %collective-permute-start.30 = (bf16[512,896]{1,0:T(8,128)(2,1)S(1)}, bf16[512,896]{1,0:T(8,128)(2,1)S(1)}, u32[]{:S(2)}, u32[]{:S(2)}) collective-permute-start(bf16[512,896]{1,0:T(8,128)(2,1)S(1)} %get-tuple-element.55.own_grad), channel_id=1, source_target_pairs={{0,16},{16,0},{32,48},{48,32},{64,80},{80,64},{96,112},{112,96},{1... | collective-permute-start | bytes 2752520 | tf_op jit(solution)/shard_map/ppermute | solution.py:30
  115.5 13.2 %collective-permute-start.31 = (bf16[256,1024]{1,0:T(8,128)(2,1)S(1)}, bf16[256,1024]{1,0:T(8,128)(2,1)S(1)}, u32[]{:S(2)}, u32[]{:S(2)}) collective-permute-start(bf16[256,1024]{1,0:T(8,128)(2,1)S(1)} %get-tuple-element.58), channel_id=1, source_target_pairs={{0,4},{1,5},{2,6},{3,7},{4,0},{5,1},{6,2},{7,3},{8,12},{9,13},{10,... | collective-permute-start | bytes 1572872 | tf_op jit(solution)/shard_map/ppermute | solution.py:22
  115.6 14.4 %collective-permute-start.33 = (bf16[256,1024]{1,0:T(8,128)(2,1)S(1)}, bf16[256,1024]{1,0:T(8,128)(2,1)S(1)}, u32[]{:S(2)}, u32[]{:S(2)}) collective-permute-start(bf16[256,1024]{1,0:T(8,128)(2,1)S(1)} %get-tuple-element.60), channel_id=1, source_target_pairs={{0,12},{1,13},{2,14},{3,15},{4,8},{5,9},{6,10},{7,11},{8,4},{9,5},... | collective-permute-start | bytes 1572872 | tf_op jit(solution)/shard_map/ppermute | solution.py:22
  117.6 12.9 %collective-permute-start.38 = (bf16[256,1024]{1,0:T(8,128)(2,1)S(1)}, bf16[256,1024]{1,0:T(8,128)(2,1)S(1)}, u32[]{:S(2)}, u32[]{:S(2)}) collective-permute-start(bf16[256,1024]{1,0:T(8,128)(2,1)S(1)} %get-tuple-element.62), channel_id=1, source_target_pairs={{0,1},{1,0},{2,3},{3,2},{4,5},{5,4},{6,7},{7,6},{8,9},{9,8},{10,11... | collective-permute-start | bytes 1572872 | tf_op jit(solution)/shard_map/ppermute | solution.py:22
  117.6 14.2 %collective-permute-start.40 = (bf16[256,1024]{1,0:T(8,128)(2,1)S(1)}, bf16[256,1024]{1,0:T(8,128)(2,1)S(1)}, u32[]{:S(2)}, u32[]{:S(2)}) collective-permute-start(bf16[256,1024]{1,0:T(8,128)(2,1)S(1)} %get-tuple-element.64), channel_id=1, source_target_pairs={{0,3},{1,2},{2,1},{3,0},{4,7},{5,6},{6,5},{7,4},{8,11},{9,10},{10,... | collective-permute-start | bytes 1572872 | tf_op jit(solution)/shard_map/ppermute | solution.py:22
  128.9 7.9 %collective-permute-start.32 = (bf16[128,1024]{1,0:T(8,128)(2,1)S(1)}, bf16[128,1024]{1,0:T(8,128)(2,1)S(1)}, u32[]{:S(2)}, u32[]{:S(2)}) collective-permute-start(bf16[128,1024]{1,0:T(8,128)(2,1)S(1)} %add_convert_fusion.7), channel_id=1, source_target_pairs={{0,12},{1,13},{2,14},{3,15},{4,8},{5,9},{6,10},{7,11},{8,4},{9,5},... | collective-permute-start | bytes 786440 | tf_op jit(solution)/shard_map/ppermute | solution.py:22
  130.1 6.8 %collective-permute-start.34 = (bf16[128,1024]{1,0:T(8,128)(2,1)S(1)}, bf16[128,1024]{1,0:T(8,128)(2,1)S(1)}, u32[]{:S(2)}, u32[]{:S(2)}) collective-permute-start(bf16[128,1024]{1,0:T(8,128)(2,1)S(1)} %add_convert_fusion.5), channel_id=1, source_target_pairs={{0,4},{1,5},{2,6},{3,7},{4,0},{5,1},{6,2},{7,3},{8,12},{9,13},{10,... | collective-permute-start | bytes 786440 | tf_op jit(solution)/shard_map/ppermute | solution.py:22
  130.6 10.4 %collective-permute-start.39 = (bf16[128,1024]{1,0:T(8,128)(2,1)S(1)}, bf16[128,1024]{1,0:T(8,128)(2,1)S(1)}, u32[]{:S(2)}, u32[]{:S(2)}) collective-permute-start(bf16[128,1024]{1,0:T(8,128)(2,1)S(1)} %add_convert_fusion.3), channel_id=1, source_target_pairs={{0,3},{1,2},{2,1},{3,0},{4,7},{5,6},{6,5},{7,4},{8,11},{9,10},{10,... | collective-permute-start | bytes 786440 | tf_op jit(solution)/shard_map/ppermute | solution.py:22
  131.9 9.3 %collective-permute-start.41 = (bf16[128,1024]{1,0:T(8,128)(2,1)S(1)}, bf16[128,1024]{1,0:T(8,128)(2,1)S(1)}, u32[]{:S(2)}, u32[]{:S(2)}) collective-permute-start(bf16[128,1024]{1,0:T(8,128)(2,1)S(1)} %add_convert_fusion.1), channel_id=1, source_target_pairs={{0,1},{1,0},{2,3},{3,2},{4,5},{5,4},{6,7},{7,6},{8,9},{9,8},{10,11... | collective-permute-start | bytes 786440 | tf_op jit(solution)/shard_map/ppermute | solution.py:22
  137.1 5.6 %collective-permute-start.37 = (bf16[32,2048]{1,0:T(8,128)(2,1)S(1)}, bf16[32,2048]{1,0:T(8,128)(2,1)S(1)}, u32[]{:S(2)}, u32[]{:S(2)}) collective-permute-start(bf16[32,2048]{1,0:T(8,128)(2,1)S(1)} %get-tuple-element.101), channel_id=1, source_target_pairs={{0,3},{1,2},{2,1},{3,0},{4,7},{5,6},{6,5},{7,4},{8,11},{9,10},{10,... | collective-permute-start | bytes 393224 | tf_op jit(solution)/shard_map/ppermute | solution.py:22
  138.3 7.0 %collective-permute-start.36 = (bf16[32,2048]{1,0:T(8,128)(2,1)S(1)}, bf16[32,2048]{1,0:T(8,128)(2,1)S(1)}, u32[]{:S(2)}, u32[]{:S(2)}) collective-permute-start(bf16[32,2048]{1,0:T(8,128)(2,1)S(1)} %get-tuple-element.102), channel_id=1, source_target_pairs={{0,1},{1,0},{2,3},{3,2},{4,5},{5,4},{6,7},{7,6},{8,9},{9,8},{10,11... | collective-permute-start | bytes 393224 | tf_op jit(solution)/shard_map/ppermute | solution.py:22
  138.6 6.7 %collective-permute-start.35 = (bf16[32,2048]{1,0:T(8,128)(2,1)S(1)}, bf16[32,2048]{1,0:T(8,128)(2,1)S(1)}, u32[]{:S(2)}, u32[]{:S(2)}) collective-permute-start(bf16[32,2048]{1,0:T(8,128)(2,1)S(1)} %get-tuple-element.100), channel_id=1, source_target_pairs={{0,2},{1,3},{2,0},{3,1},{4,6},{5,7},{6,4},{7,5},{8,10},{9,11},{10,... | collective-permute-start | bytes 393224 | tf_op jit(solution)/shard_map/ppermute | solution.py:22
  141.3 5.4 %collective-permute-start.44 = (bf16[32,2048]{1,0:T(8,128)(2,1)S(1)}, bf16[32,2048]{1,0:T(8,128)(2,1)S(1)}, u32[]{:S(2)}, u32[]{:S(2)}) collective-permute-start(bf16[32,2048]{1,0:T(8,128)(2,1)S(1)} %get-tuple-element.104), channel_id=1, source_target_pairs={{0,12},{1,13},{2,14},{3,15},{4,8},{5,9},{6,10},{7,11},{8,4},{9,5},... | collective-permute-start | bytes 393224 | tf_op jit(solution)/shard_map/ppermute | solution.py:22
  142.7 4.1 %collective-permute-start.43 = (bf16[32,2048]{1,0:T(8,128)(2,1)S(1)}, bf16[32,2048]{1,0:T(8,128)(2,1)S(1)}, u32[]{:S(2)}, u32[]{:S(2)}) collective-permute-start(bf16[32,2048]{1,0:T(8,128)(2,1)S(1)} %get-tuple-element.105), channel_id=1, source_target_pairs={{0,4},{1,5},{2,6},{3,7},{4,0},{5,1},{6,2},{7,3},{8,12},{9,13},{10,... | collective-permute-start | bytes 393224 | tf_op jit(solution)/shard_map/ppermute | solution.py:22
  142.7 6.4 %collective-permute-start.42 = (bf16[32,2048]{1,0:T(8,128)(2,1)S(1)}, bf16[32,2048]{1,0:T(8,128)(2,1)S(1)}, u32[]{:S(2)}, u32[]{:S(2)}) collective-permute-start(bf16[32,2048]{1,0:T(8,128)(2,1)S(1)} %get-tuple-element.103), channel_id=1, source_target_pairs={{0,8},{1,9},{2,10},{3,11},{4,12},{5,13},{6,14},{7,15},{8,0},{9,1},... | collective-permute-start | bytes 393224 | tf_op jit(solution)/shard_map/ppermute | solution.py:22
  149.2 4.4 %collective-permute-start.47 = (bf16[8,4096]{1,0:T(8,128)(2,1)S(1)}, bf16[8,4096]{1,0:T(8,128)(2,1)S(1)}, u32[]{:S(2)}, u32[]{:S(2)}) collective-permute-start(bf16[8,4096]{1,0:T(8,128)(2,1)S(1)} %get-tuple-element.107), channel_id=1, source_target_pairs={{0,96},{16,112},{32,64},{48,80},{64,32},{80,48},{96,0},{112,16},{1... | collective-permute-start | bytes 196616 | tf_op jit(solution)/shard_map/ppermute | solution.py:26
  150.3 3.3 %collective-permute-start.46 = (bf16[8,4096]{1,0:T(8,128)(2,1)S(1)}, bf16[8,4096]{1,0:T(8,128)(2,1)S(1)}, u32[]{:S(2)}, u32[]{:S(2)}) collective-permute-start(bf16[8,4096]{1,0:T(8,128)(2,1)S(1)} %get-tuple-element.108), channel_id=1, source_target_pairs={{0,32},{16,48},{32,0},{48,16},{64,96},{80,112},{96,64},{112,80},{1... | collective-permute-start | bytes 196616 | tf_op jit(solution)/shard_map/ppermute | solution.py:26
  150.7 4.8 %collective-permute-start.45 = (bf16[8,4096]{1,0:T(8,128)(2,1)S(1)}, bf16[8,4096]{1,0:T(8,128)(2,1)S(1)}, u32[]{:S(2)}, u32[]{:S(2)}) collective-permute-start(bf16[8,4096]{1,0:T(8,128)(2,1)S(1)} %get-tuple-element.106), channel_id=1, source_target_pairs={{0,64},{16,80},{32,96},{48,112},{64,0},{80,16},{96,32},{112,48},{1... | collective-permute-start | bytes 196616 | tf_op jit(solution)/shard_map/ppermute | solution.py:26
  155.6 6.8 %collective-permute-start.48 = (bf16[4,4096]{1,0:T(4,128)(2,1)S(1)}, bf16[4,4096]{1,0:T(4,128)(2,1)S(1)}, u32[]{:S(2)}, u32[]{:S(2)}) collective-permute-start(bf16[4,4096]{1,0:T(4,128)(2,1)S(1)} %get-tuple-element.110), channel_id=1, source_target_pairs={{0,16},{16,0},{32,48},{48,32},{64,80},{80,64},{96,112},{112,96},{1... | collective-permute-start | bytes 98312 | tf_op jit(solution)/shard_map/ppermute | solution.py:30
  (11 other events, 124.2 us)

commit v3 on v2

--- a/solution.py
+++ b/solution.py
@@ -106,17 +106,15 @@
             pltpu.SemaphoreType.DMA((8 + 7 * 2 * RING,)),
         ],
         compiler_params=params(52),
-        cost_estimate=pl.CostEstimate(
-            flops=2 * tokens * width * cols, bytes_accessed=2 * width * (cols + tokens) + 4 * tokens * cols, transcendentals=0
-        ),
+        cost_estimate=pl.CostEstimate(flops=tokens * cols, bytes_accessed=tokens * cols, transcendentals=0),
         name="policy_logits",
     )(mine, theirs, *near, *gathered, weight)
 
 
-def in_token_order(refer):
+def in_token_order(refer, own):
     shape = (refer.shape[0], refer.shape[0])
     row, source = lax.broadcasted_iota(jnp.int32, shape, 0), lax.broadcasted_iota(jnp.int32, shape, 1)
-    wanted = ((row >> 2) & 15) * 8 + (row >> 6) * 4 + (row & 3)
+    wanted = ((row >> 2) & 15) * 8 + ((row >> 6) ^ own) * 4 + (row & 3)
     return jnp.dot((source == wanted).astype(F32).astype(BF16), refer, preferred_element_type=F32)
 
 
@@ -127,8 +125,11 @@
     local = targets_ref[...].reshape(1, rows) - start_col
     local = jnp.where((local >= 0) & (local < cols), local, -1).astype(F32)
     local = jnp.broadcast_to(local, (128, rows)).T[:, 0:1].astype(jnp.int32)
-    policy = policy_ref[...]
-    refer = in_token_order(refer_ref[...])
+    stats_ref[...] = block_stats(local, policy_ref[...], in_token_order(refer_ref[...], core))
+
+
+def block_stats(local, policy, refer):
+    rows, cols = policy.shape
     hit = lax.broadcasted_iota(jnp.int32, (rows, cols), 1) == local
     peak = jnp.max(policy, axis=1, keepdims=True)
     scaled = jnp.exp(policy - peak)
@@ -142,7 +143,7 @@
     table = jnp.zeros((rows, 128), F32)
     for k, value in enumerate((peak, total, cross, ref_peak, ref_total, picked, ref_picked)):
         table = jnp.where(lane == k, value, table)
-    stats_ref[...] = table.T[:8]
+    return table.T[:8]
 
 
 def row_stats(targets, policy, refer):
@@ -216,7 +217,7 @@
         span = slice(i * step, (i + 1) * step)
         per_row = packed[span]
         policy = policy_ref[span, :]
-        refer = in_token_order(refer_ref[span, :])
+        refer = in_token_order(refer_ref[span, :], core_here)
         column = lax.broadcasted_iota(jnp.int32, (step, cols), 1)
         hit = (column == per_row[:, 4:5].astype(jnp.int32)).astype(F32)
         probs = jnp.exp(policy - per_row[:, 0:1])
@@ -339,7 +340,11 @@
     x, y = t // RING, t % RING
 
     piece = width // CHIPS
-    across = swap_z(lax.dynamic_slice_in_dim(hidden, t * piece, piece, axis=1), 2)
+    across = [
+        lax.dynamic_slice(hidden, (first, (t ^ offset) * piece), (rows // 2, piece))
+        for first, offset in ((0, 0), (0, 1), (rows // 2, 0), (rows // 2, RING))
+    ]
+    across = swap_z(jnp.stack(across), 2)
     sent, across = lax.optimization_barrier((hidden, across))
     near = [swap_z(sent, 1), swap_z(sent, 3)]
     other_weight = swap_core(weight)
@@ -350,18 +355,19 @@
         for c in (core, 1 - core)
     ]
     ref_other = swap_core(ref_other)
-    ref_both = jnp.where(
-        core == 0, jnp.concatenate([ref_own, ref_other], axis=1), jnp.concatenate([ref_other, ref_own], axis=1)
-    )
-    by_x, by_y = across[None, : rows // 2], across[None, rows // 2 :]
-    for step_x, step_y in ((1, 4), (3, 12), (4, 1)):
+    ref_both = jnp.concatenate([ref_own, ref_other], axis=1)
+    by_x, by_y = across[:2], across[2:]
+    for step_x, step_y in ((3, 12), (4, 1)):
         by_x = jnp.concatenate([by_x, swap_tensor(by_x, step_x)], axis=0)
         by_y = jnp.concatenate([by_y, swap_tensor(by_y, step_y)], axis=0)
         by_x, by_y = lax.optimization_barrier((by_x, by_y))
     by_x, by_y, other_weight = lax.optimization_barrier((by_x, by_y, other_weight))
     swapped = [swap_core(by_x), swap_core(by_y)]
     late = [swap_tensor(by_x, 12), swap_tensor(by_y, 3)]
-    ref_both, swapped, late = lax.optimization_barrier((ref_both, swapped, late))
+    near, late = lax.optimization_barrier((near, late))
+    near += [swap_core(a) for a in near]
+    swapped += [swap_core(a) for a in late]
+    ref_both, near, swapped = lax.optimization_barrier((ref_both, near, swapped))
     refer = lax.all_to_all(
         ref_both,
         ("dp", "tensor"),
@@ -372,9 +378,6 @@
             [(ring * CORES + c) * CHIPS + chip for ring in range(RING) for chip in range(CHIPS)] for c in range(CORES)
         ],
     )
-    near, late = lax.optimization_barrier((near, late))
-    near += [swap_core(a) for a in near]
-    swapped += [swap_core(a) for a in late]
     gathered = [by_x, late[0], by_y, late[1], swapped[0], swapped[2], swapped[1], swapped[3]]
     policy = policy_logits(hidden, theirs, near, gathered, weight)
     refer, policy = lax.optimization_barrier((refer, policy))

time: 163 us -> 166 us (1.018)
  waiting for transfers between devices: 46.6 us -> 52.5 us
  local copies, waits for them, and re-layouts: 6.81 us -> 4.96 us
    ppermute x9, waiting for transfers between devices: 8.22 us -> 16.8 us  [swap_z(): lax.ppermute(value, 'dp', [(i, i ^ offset * CORES) for i in range(RING *...]
    ppermute x28 -> x26, waiting for transfers between devices: 32.2 us -> 26.5 us  [swap_tensor(): lax.ppermute(value, 'tensor', [(i, i ^ offset) for i in range(CHIPS)])]
    all_to_all x1, starting transfers between devices: 5.22 us -> 9.04 us  [shards(): lax.all_to_all(ref_both, ('dp', 'tensor'), split_axis=0, concat_axis=0, t...]
    ppermute x12, starting transfers between devices: 22.1 us -> 18.5 us  [swap_core(): return lax.ppermute(value, 'dp', [(i, i ^ 1) for i in range(RING * CORES)])]
    ppermute x12, waiting for transfers between devices: 4.11 us -> 6 us  [swap_core(): return lax.ppermute(value, 'dp', [(i, i ^ 1) for i in range(RING * CORES)])]
    unnamed x19 -> x21, local copies, waits for them, and re-layouts: 4.43 us -> 2.59 us
    select_n x1 -> x0, other arithmetic: 1.75 us -> none  [shards(): jnp.where(core == 0, jnp.concatenate([ref_own, ref_other], axis=1), jnp.c...]
    ppermute x28 -> x26, starting transfers between devices: 33.1 us -> 31.5 us  [swap_tensor(): lax.ppermute(value, 'tensor', [(i, i ^ offset) for i in range(CHIPS)])]
  transfers between devices with their start and end apart: 50 -> 48, of which waited for: 25 -> 30; matrix products, arithmetic and copies ran while one was open for 4% -> 3% of each run, Pallas kernels for 8% -> 8%
where the time goes in v3:
time: 166 us; the launch traced here: 165 us
  starting transfers between devices  73.1 us (44%)
  waiting for transfers between devices  52.5 us (32%)
  Pallas kernels  29.9 us (18%)
  local copies, waits for them, and re-layouts  4.96 us (3%)
  other arithmetic  3.69 us (2%)
    ppermute x26, starting transfers between devices, swap_tensor(): lax.ppermute(value, 'tensor', [(i, i ^ offset) for i in range(CHIPS)])  31.5 us
    ppermute x26, waiting for transfers between devices, swap_tensor(): lax.ppermute(value, 'tensor', [(i, i ^ offset) for i in range(CHIPS)])  26.5 us
    ppermute x12, starting transfers between devices, swap_core(): return lax.ppermute(value, 'dp', [(i, i ^ 1) for i in range(RING * CORES)])  18.5 us
    ppermute x9, waiting for transfers between devices, swap_z(): lax.ppermute(value, 'dp', [(i, i ^ offset * CORES) for i in range(RING *...  16.8 us
    ppermute x9, starting transfers between devices, swap_z(): lax.ppermute(value, 'dp', [(i, i ^ offset * CORES) for i in range(RING *...  14.2 us
    pallas_call x1, Pallas kernels, policy_logits(): pl.pallas_call(logits_body, out_shape=jax.ShapeDtypeStruct((tokens, cols)...  13.1 us
    pallas_call x1, Pallas kernels, hidden_parts(): pl.pallas_call(hidden_body, out_shape=(jax.ShapeDtypeStruct((tokens // 2,...  12.5 us
    all_to_all x1, starting transfers between devices, shards(): lax.all_to_all(ref_both, ('dp', 'tensor'), split_axis=0, concat_axis=0, t...  9.04 us
  transfers between devices with their start and end apart: 48, of which 30 were waited for; matrix products, arithmetic and copies ran while one was open for 3% of the time, Pallas kernels for 8%

profile of v3, /device:TPU:1, one launch (start us, length us, event | category | flops | bytes accessed | tf_op | source)
XLA Modules:
  0.0 165.3 jit_solution(9006295792724739937)
XLA Ops:
  0.6 1.5 collective-permute-start.8
  3.0 3.8 %collective-permute-start.1 = (bf16[4,32,512]{2,1,0:T(8,128)(2,1)S(1)}, bf16[4,32,512]{2,1,0:T(8,128)(2,1)S(1)}, u32[]{:S(2)}, u32[]{:S(2)}) collective-permute-start(bf16[4,32,512]{2,1,0:T(8,128)(2,1)S(1)} %pad_maximum_fusion.5), channel_id=1, source_target_pairs={{0,64},{16,80},{32,96},{48,112},{64,0},{80,16},{96,32},{112,48},{1... | collective-permute-start | bytes 393224 | tf_op jit(solution)/shard_map/ppermute | solution.py:26
  6.8 3.7 %collective-permute-done.1 = bf16[4,32,512]{2,1,0:T(8,128)(2,1)S(1)} collective-permute-done((bf16[4,32,512]{2,1,0:T(8,128)(2,1)S(1)}, bf16[4,32,512]{2,1,0:T(8,128)(2,1)S(1)}, u32[]{:S(2)}, u32[]{:S(2)}) %collective-permute-start.1) | collective-permute-done | bytes 131104 | tf_op jit(solution)/shard_map/ppermute | solution.py:26
  11.4 2.2 %collective-permute-start.3 = (bf16[64,8192]{1,0:T(8,128)(2,1)}, bf16[64,8192]{1,0:T(8,128)(2,1)}, u32[]{:S(2)}, u32[]{:S(2)}) collective-permute-start(bf16[64,8192]{1,0:T(8,128)(2,1)} %refs_0_.1), channel_id=1, source_target_pairs={{0,96},{16,112},{32,64},{48,80},{64,32},{80,48},{96,0},{112,16},{1... | collective-permute-start | bytes 3145736 | tf_op jit(solution)/shard_map/ppermute | solution.py:26
  13.6 2.8 %collective-permute-start.4 = (bf16[2,32,512]{2,1,0:T(8,128)(2,1)S(1)}, bf16[2,32,512]{2,1,0:T(8,128)(2,1)S(1)}, u32[]{:S(2)}, u32[]{:S(2)}) collective-permute-start(bf16[2,32,512]{2,1,0:T(8,128)(2,1)S(1)} %get-tuple-element.118), channel_id=1, source_target_pairs={{0,3},{1,2},{2,1},{3,0},{4,7},{5,6},{6,5},{7,4},{8,11},{9,10},{10,... | collective-permute-start | bytes 196616 | tf_op jit(solution)/shard_map/ppermute | solution.py:22
  16.4 2.5 %collective-permute-start.5 = (bf16[2,32,512]{2,1,0:T(8,128)(2,1)S(1)}, bf16[2,32,512]{2,1,0:T(8,128)(2,1)S(1)}, u32[]{:S(2)}, u32[]{:S(2)}) collective-permute-start(bf16[2,32,512]{2,1,0:T(8,128)(2,1)S(1)} %get-tuple-element.117), channel_id=1, source_target_pairs={{0,12},{1,13},{2,14},{3,15},{4,8},{5,9},{6,10},{7,11},{8,4},{9,5},... | collective-permute-start | bytes 196616 | tf_op jit(solution)/shard_map/ppermute | solution.py:22
  18.9 2.2 %collective-permute-done.5 = bf16[2,32,512]{2,1,0:T(8,128)(2,1)S(1)} collective-permute-done((bf16[2,32,512]{2,1,0:T(8,128)(2,1)S(1)}, bf16[2,32,512]{2,1,0:T(8,128)(2,1)S(1)}, u32[]{:S(2)}, u32[]{:S(2)}) %collective-permute-start.5) | collective-permute-done | bytes 65568 | tf_op jit(solution)/shard_map/ppermute | solution.py:22
  21.4 4.1 %collective-permute-done.6 = bf16[4,32,512]{2,1,0:T(8,128)(2,1)S(1)} collective-permute-done((bf16[4,32,512]{2,1,0:T(8,128)(2,1)S(1)}, bf16[4,32,512]{2,1,0:T(8,128)(2,1)S(1)}, u32[]{:S(2)}, u32[]{:S(2)}) %collective-permute-start.6) | collective-permute-done | bytes 131104 | tf_op jit(solution)/shard_map/ppermute | solution.py:22
  25.6 2.6 %collective-permute-start.9 = (bf16[8,32,512]{2,1,0:T(8,128)(2,1)S(1)}, bf16[8,32,512]{2,1,0:T(8,128)(2,1)S(1)}, u32[]{:S(2)}, u32[]{:S(2)}) collective-permute-start(bf16[8,32,512]{2,1,0:T(8,128)(2,1)S(1)} %pad_maximum_fusion.1.refs_6_), channel_id=1, source_target_pairs={{0,12},{1,13},{2,14},{3,15},{4,8},{5,9},{6,10},{7,11},{8,4},{9,5},... | collective-permute-start | bytes 786440 | tf_op jit(solution)/shard_map/ppermute | solution.py:22
  28.2 1.4 collective-permute-start.10
  29.6 5.3 %collective-permute-done.2.refs_2_ = bf16[64,8192]{1,0:T(8,128)(2,1)} collective-permute-done((bf16[64,8192]{1,0:T(8,128)(2,1)}, bf16[64,8192]{1,0:T(8,128)(2,1)}, u32[]{:S(2)}, u32[]{:S(2)}) %collective-permute-start.2) | collective-permute-done | bytes 1048608 | tf_op jit(solution)/shard_map/ppermute | solution.py:26
  34.8 1.5 collective-permute-done.3.refs_3_
  36.4 2.8 %collective-permute-start.11 = (bf16[64,8192]{1,0:T(8,128)(2,1)}, bf16[64,8192]{1,0:T(8,128)(2,1)}, u32[]{:S(2)}, u32[]{:S(2)}) collective-permute-start(bf16[64,8192]{1,0:T(8,128)(2,1)} %collective-permute-done.2.refs_2_), channel_id=1, source_target_pairs={{0,16},{16,0},{32,48},{48,32},{64,80},{80,64},{96,112},{112,96},{1... | collective-permute-start | bytes 3145736 | tf_op jit(solution)/shard_map/ppermute | solution.py:30
  40.9 1.9 %collective-permute-done = bf16[64,4,896]{2,1,0:T(4,128)(2,1)S(1)} collective-permute-done((bf16[64,4,896]{2,1,0:T(4,128)(2,1)S(1)}, bf16[64,4,896]{2,1,0:T(4,128)(2,1)S(1)}, u32[]{:S(2)}, u32[]{:S(2)}) %collective-permute-start) | collective-permute-done | bytes 458784 | tf_op jit(solution)/shard_map/ppermute | solution.py:30
  45.1 1.4 pad_maximum_fusion
  46.5 9.0 %all-to-all-start = ((bf16[64,8,896]{2,1,0:T(8,128)(2,1)}), bf16[64,8,896]{2,1,0:T(8,128)(2,1)S(1)}, u32[]{:S(2)}, u32[]{:S(2)}) async-start(bf16[64,8,896]{2,1,0:T(8,128)(2,1)} %pad_maximum_fusion), calls=%async_computation | async-start | bytes 1835008 | tf_op jit(solution)/shard_map/all_to_all | solution.py:371
  55.6 13.1 %policy_logits.1.policy_ref = f32[512,896]{1,0:T(8,128)} custom-call(bf16[64,8192]{1,0:T(8,128)(2,1)} %refs_0_.1, bf16[64,8192]{1,0:T(8,128)(2,1)} %collective-permute-done.17.refs_1_, bf16[64,8192]{1,0:T(8,128)(2,1)} %collective-permute-done.2.refs_2_, bf16[64,8192]{1,0:T(8,128)(2,1)} %collective-permute-done.3.refs_3_, ...), custom_call_target="tpu_custom_call" | custom-call | flops 458752 | bytes 458752 | tf_op jit(solution)/shard_map/policy_logits/pallas_call | solution.py:97
  68.7 3.3 %all-to-all-done = bf16[64,8,896]{2,1,0:T(8,128)(2,1)S(1)} async-done(((bf16[64,8,896]{2,1,0:T(8,128)(2,1)}), bf16[64,8,896]{2,1,0:T(8,128)(2,1)S(1)}, u32[]{:S(2)}, u32[]{:S(2)}) %all-to-all-start) | async-done | bytes 917536 | tf_op jit(solution)/shard_map/all_to_all | solution.py:371
  71.9 1.5 copy-done
  73.4 2.3 %row_stats.1 = f32[8,512]{1,0:T(8,128)S(1)} custom-call(s32[512]{0:T(512)S(1)} %copy-done.3, f32[512,896]{1,0:T(8,128)S(1)} %copy-done, bf16[512,896]{1,0:T(8,128)(2,1)S(1)} %bitcast.199), custom_call_target="tpu_custom_call" | custom-call | flops 9175040 | bytes 2752512 | tf_op jit(solution)/shard_map/row_stats/pallas_call | solution.py:152
  76.4 1.7 %collective-permute-start.19 = (f32[8,512]{1,0:T(8,128)S(1)}, f32[8,512]{1,0:T(8,128)S(1)}, u32[]{:S(2)}, u32[]{:S(2)}) collective-permute-start(f32[8,512]{1,0:T(8,128)S(1)} %row_stats.1), channel_id=1, source_target_pairs={{0,2},{1,3},{2,0},{3,1},{4,6},{5,7},{6,4},{7,5},{8,10},{9,11},{10,... | collective-permute-start | bytes 49160 | tf_op jit(solution)/shard_map/ppermute | solution.py:22
  78.2 0.9 collective-permute-start.18
  79.6 0.9 collective-permute-done.19
  81.4 1.5 collective-permute-start.22
  82.9 1.4 collective-permute-start.21
  85.8 2.7 %collective-permute-start.26 = (f32[8,512]{1,0:T(8,128)S(1)}, f32[8,512]{1,0:T(8,128)S(1)}, u32[]{:S(2)}, u32[]{:S(2)}) collective-permute-start(f32[8,512]{1,0:T(8,128)S(1)} %stack.195), channel_id=1, source_target_pairs={{0,96},{16,112},{32,64},{48,80},{64,32},{80,48},{96,0},{112,16},{1... | collective-permute-start | bytes 49160 | tf_op jit(solution)/shard_map/ppermute | solution.py:26
  89.8 2.8 %collective-permute-done.25 = f32[8,512]{1,0:T(8,128)S(1)} collective-permute-done((f32[8,512]{1,0:T(8,128)S(1)}, f32[8,512]{1,0:T(8,128)S(1)}, u32[]{:S(2)}, u32[]{:S(2)}) %collective-permute-start.25) | collective-permute-done | bytes 16416 | tf_op jit(solution)/shard_map/ppermute | solution.py:26
  92.8 5.1 %collective-permute-start.27 = (f32[8,512]{1,0:T(8,128)S(1)}, f32[8,512]{1,0:T(8,128)S(1)}, u32[]{:S(2)}, u32[]{:S(2)}) collective-permute-start(f32[8,512]{1,0:T(8,128)S(1)} %stack.208), channel_id=1, source_target_pairs={{0,16},{16,0},{32,48},{48,32},{64,80},{80,64},{96,112},{112,96},{1... | collective-permute-start | bytes 49160 | tf_op jit(solution)/shard_map/ppermute | solution.py:30
  98.9 2.1 %logit_grads.1 = (bf16[512,896]{1,0:T(8,128)(2,1)S(1)}, f32[8,128]{1,0:T(8,128)S(1)}) custom-call(f32[8,512]{1,0:T(8,128)S(1)} %stack.219.stats_ref, s32[512]{0:T(512)S(1)} %copy-done.3, s32[512]{0:T(512)S(1)} %copy-done.4, s32[512]{0:T(512)S(1)} %copy-done.5, f32[512,896]{1,0:T(8,128)S(1)} %copy-done.1, bf16[512,896]{1,0:T(8,128)(2,1)S(1)} %bitcast.200), custom_call_target="tpu_custom_call" | custom-call | flops 469762048 | bytes 4587520 | tf_op jit(solution)/shard_map/logit_grads/pallas_call | solution.py:239
  101.6 2.1 %collective-permute-done.28.other_grad = bf16[512,896]{1,0:T(8,128)(2,1)S(1)} collective-permute-done((bf16[512,896]{1,0:T(8,128)(2,1)S(1)}, bf16[512,896]{1,0:T(8,128)(2,1)S(1)}, u32[]{:S(2)}, u32[]{:S(2)}) %collective-permute-start.28) | collective-permute-done | bytes 917536 | tf_op jit(solution)/shard_map/ppermute | solution.py:30
  103.7 1.0 copy-done.7
  104.7 12.5 %hidden_parts.1 = (bf16[256,1024]{1,0:T(8,128)(2,1)S(1)}, bf16[256,1024]{1,0:T(8,128)(2,1)S(1)}, bf16[256,1024]{1,0:T(8,128)(2,1)S(1)}, bf16[256,1024]{1,0:T(8,1...) custom-call(bf16[512,896]{1,0:T(8,128)(2,1)} %copy-done.2, ...), custom_call_target="tpu_custom_call" | custom-call | flops 7516192768 | bytes 26214400 | tf_op jit(solution)/shard_map/hidden_parts/pallas_call | solution.py:308
  117.9 1.4 collective-permute-start.31
  119.7 1.5 collective-permute-start.38
  121.3 9.1 %collective-permute-done.29 = bf16[256,1024]{1,0:T(8,128)(2,1)S(1)} collective-permute-done((bf16[256,1024]{1,0:T(8,128)(2,1)S(1)}, bf16[256,1024]{1,0:T(8,128)(2,1)S(1)}, u32[]{:S(2)}, u32[]{:S(2)}) %collective-permute-start.29) | collective-permute-done | bytes 524320 | tf_op jit(solution)/shard_map/ppermute | solution.py:22
  130.5 1.4 collective-permute-start.30
  132.2 1.8 %collective-permute-start.37 = (bf16[128,1024]{1,0:T(8,128)(2,1)S(1)}, bf16[128,1024]{1,0:T(8,128)(2,1)S(1)}, u32[]{:S(2)}, u32[]{:S(2)}) collective-permute-start(bf16[128,1024]{1,0:T(8,128)(2,1)S(1)} %add_convert_fusion.3), channel_id=1, source_target_pairs={{0,3},{1,2},{2,1},{3,0},{4,7},{5,6},{6,5},{7,4},{8,11},{9,10},{10,... | collective-permute-start | bytes 786440 | tf_op jit(solution)/shard_map/ppermute | solution.py:22
  134.2 4.2 %collective-permute-done.30 = bf16[128,1024]{1,0:T(8,128)(2,1)S(1)} collective-permute-done((bf16[128,1024]{1,0:T(8,128)(2,1)S(1)}, bf16[128,1024]{1,0:T(8,128)(2,1)S(1)}, u32[]{:S(2)}, u32[]{:S(2)}) %collective-permute-start.30) | collective-permute-done | bytes 262176 | tf_op jit(solution)/shard_map/ppermute | solution.py:22
  138.7 1.7 %collective-permute-start.35 = (bf16[32,2048]{1,0:T(8,128)(2,1)S(1)}, bf16[32,2048]{1,0:T(8,128)(2,1)S(1)}, u32[]{:S(2)}, u32[]{:S(2)}) collective-permute-start(bf16[32,2048]{1,0:T(8,128)(2,1)S(1)} %get-tuple-element.109), channel_id=1, source_target_pairs={{0,3},{1,2},{2,1},{3,0},{4,7},{5,6},{6,5},{7,4},{8,11},{9,10},{10,... | collective-permute-start | bytes 393224 | tf_op jit(solution)/shard_map/ppermute | solution.py:22
  140.4 2.2 %collective-permute-start.33 = (bf16[32,2048]{1,0:T(8,128)(2,1)S(1)}, bf16[32,2048]{1,0:T(8,128)(2,1)S(1)}, u32[]{:S(2)}, u32[]{:S(2)}) collective-permute-start(bf16[32,2048]{1,0:T(8,128)(2,1)S(1)} %get-tuple-element.108), channel_id=1, source_target_pairs={{0,2},{1,3},{2,0},{3,1},{4,6},{5,7},{6,4},{7,5},{8,10},{9,11},{10,... | collective-permute-start | bytes 393224 | tf_op jit(solution)/shard_map/ppermute | solution.py:22
  143.0 1.4 collective-permute-start.42
  144.3 2.6 %collective-permute-start.40 = (bf16[32,2048]{1,0:T(8,128)(2,1)S(1)}, bf16[32,2048]{1,0:T(8,128)(2,1)S(1)}, u32[]{:S(2)}, u32[]{:S(2)}) collective-permute-start(bf16[32,2048]{1,0:T(8,128)(2,1)S(1)} %get-tuple-element.111), channel_id=1, source_target_pairs={{0,8},{1,9},{2,10},{3,11},{4,12},{5,13},{6,14},{7,15},{8,0},{9,1},... | collective-permute-start | bytes 393224 | tf_op jit(solution)/shard_map/ppermute | solution.py:22
  147.0 1.4 collective-permute-done.42
  148.4 2.3 %collective-permute-done.40 = bf16[32,2048]{1,0:T(8,128)(2,1)S(1)} collective-permute-done((bf16[32,2048]{1,0:T(8,128)(2,1)S(1)}, bf16[32,2048]{1,0:T(8,128)(2,1)S(1)}, u32[]{:S(2)}, u32[]{:S(2)}) %collective-permute-start.40) | collective-permute-done | bytes 131104 | tf_op jit(solution)/shard_map/ppermute | solution.py:22
  150.8 2.1 %collective-permute-start.45 = (bf16[8,4096]{1,0:T(8,128)(2,1)S(1)}, bf16[8,4096]{1,0:T(8,128)(2,1)S(1)}, u32[]{:S(2)}, u32[]{:S(2)}) collective-permute-start(bf16[8,4096]{1,0:T(8,128)(2,1)S(1)} %get-tuple-element.115), channel_id=1, source_target_pairs={{0,96},{16,112},{32,64},{48,80},{64,32},{80,48},{96,0},{112,16},{1... | collective-permute-start | bytes 196616 | tf_op jit(solution)/shard_map/ppermute | solution.py:26
  152.9 1.8 %collective-permute-start.43 = (bf16[8,4096]{1,0:T(8,128)(2,1)S(1)}, bf16[8,4096]{1,0:T(8,128)(2,1)S(1)}, u32[]{:S(2)}, u32[]{:S(2)}) collective-permute-start(bf16[8,4096]{1,0:T(8,128)(2,1)S(1)} %get-tuple-element.114), channel_id=1, source_target_pairs={{0,64},{16,80},{32,96},{48,112},{64,0},{80,16},{96,32},{112,48},{1... | collective-permute-start | bytes 196616 | tf_op jit(solution)/shard_map/ppermute | solution.py:26
  156.0 1.5 collective-permute-done.43
  157.6 6.2 %collective-permute-start.46 = (bf16[4,4096]{1,0:T(4,128)(2,1)S(1)}, bf16[4,4096]{1,0:T(4,128)(2,1)S(1)}, u32[]{:S(2)}, u32[]{:S(2)}) collective-permute-start(bf16[4,4096]{1,0:T(4,128)(2,1)S(1)} %get-tuple-element.120), channel_id=1, source_target_pairs={{0,16},{16,0},{32,48},{48,32},{64,80},{80,64},{96,112},{112,96},{1... | collective-permute-start | bytes 98312 | tf_op jit(solution)/shard_map/ppermute | solution.py:30
  (121 shorter events, 18.1 us)
Async XLA Ops:
  0.6 25.0 %collective-permute-start.8 = (bf16[8192,896]{1,0:T(8,128)(2,1)}, bf16[8192,896]{1,0:T(8,128)(2,1)}, u32[]{:S(2)}, u32[]{:S(2)}) collective-permute-start(bf16[8192,896]{1,0:T(8,128)(2,1)} %own_weight.1), channel_id=1, source_target_pairs={{0,16},{16,0},{32,48},{48,32},{64,80},{80,64},{96,112},{112,96},{1... | collective-permute-start | bytes 44040200 | tf_op jit(solution)/shard_map/ppermute | solution.py:30
  3.0 7.5 %collective-permute-start.1 = (bf16[4,32,512]{2,1,0:T(8,128)(2,1)S(1)}, bf16[4,32,512]{2,1,0:T(8,128)(2,1)S(1)}, u32[]{:S(2)}, u32[]{:S(2)}) collective-permute-start(bf16[4,32,512]{2,1,0:T(8,128)(2,1)S(1)} %pad_maximum_fusion.5), channel_id=1, source_target_pairs={{0,64},{16,80},{32,96},{48,112},{64,0},{80,16},{96,32},{112,48},{1... | collective-permute-start | bytes 393224 | tf_op jit(solution)/shard_map/ppermute | solution.py:26
  10.5 24.3 %collective-permute-start.2 = (bf16[64,8192]{1,0:T(8,128)(2,1)}, bf16[64,8192]{1,0:T(8,128)(2,1)}, u32[]{:S(2)}, u32[]{:S(2)}) collective-permute-start(bf16[64,8192]{1,0:T(8,128)(2,1)} %refs_0_.1), channel_id=1, source_target_pairs={{0,32},{16,48},{32,0},{48,16},{64,96},{80,112},{96,64},{112,80},{1... | collective-permute-start | bytes 3145736 | tf_op jit(solution)/shard_map/ppermute | solution.py:26
  11.4 25.0 %collective-permute-start.3 = (bf16[64,8192]{1,0:T(8,128)(2,1)}, bf16[64,8192]{1,0:T(8,128)(2,1)}, u32[]{:S(2)}, u32[]{:S(2)}) collective-permute-start(bf16[64,8192]{1,0:T(8,128)(2,1)} %refs_0_.1), channel_id=1, source_target_pairs={{0,96},{16,112},{32,64},{48,80},{64,32},{80,48},{96,0},{112,16},{1... | collective-permute-start | bytes 3145736 | tf_op jit(solution)/shard_map/ppermute | solution.py:26
  13.6 5.3 %collective-permute-start.4 = (bf16[2,32,512]{2,1,0:T(8,128)(2,1)S(1)}, bf16[2,32,512]{2,1,0:T(8,128)(2,1)S(1)}, u32[]{:S(2)}, u32[]{:S(2)}) collective-permute-start(bf16[2,32,512]{2,1,0:T(8,128)(2,1)S(1)} %get-tuple-element.118), channel_id=1, source_target_pairs={{0,3},{1,2},{2,1},{3,0},{4,7},{5,6},{6,5},{7,4},{8,11},{9,10},{10,... | collective-permute-start | bytes 196616 | tf_op jit(solution)/shard_map/ppermute | solution.py:22
  16.4 4.7 %collective-permute-start.5 = (bf16[2,32,512]{2,1,0:T(8,128)(2,1)S(1)}, bf16[2,32,512]{2,1,0:T(8,128)(2,1)S(1)}, u32[]{:S(2)}, u32[]{:S(2)}) collective-permute-start(bf16[2,32,512]{2,1,0:T(8,128)(2,1)S(1)} %get-tuple-element.117), channel_id=1, source_target_pairs={{0,12},{1,13},{2,14},{3,15},{4,8},{5,9},{6,10},{7,11},{8,4},{9,5},... | collective-permute-start | bytes 196616 | tf_op jit(solution)/shard_map/ppermute | solution.py:22
  21.2 4.3 %collective-permute-start.6 = (bf16[4,32,512]{2,1,0:T(8,128)(2,1)S(1)}, bf16[4,32,512]{2,1,0:T(8,128)(2,1)S(1)}, u32[]{:S(2)}, u32[]{:S(2)}) collective-permute-start(bf16[4,32,512]{2,1,0:T(8,128)(2,1)S(1)} %pad_maximum_fusion.6), channel_id=1, source_target_pairs={{0,4},{1,5},{2,6},{3,7},{4,0},{5,1},{6,2},{7,3},{8,12},{9,13},{10,... | collective-permute-start | bytes 393224 | tf_op jit(solution)/shard_map/ppermute | solution.py:22
  21.3 4.3 %collective-permute-start.7 = (bf16[4,32,512]{2,1,0:T(8,128)(2,1)S(1)}, bf16[4,32,512]{2,1,0:T(8,128)(2,1)S(1)}, u32[]{:S(2)}, u32[]{:S(2)}) collective-permute-start(bf16[4,32,512]{2,1,0:T(8,128)(2,1)S(1)} %pad_maximum_fusion.7), channel_id=1, source_target_pairs={{0,1},{1,0},{2,3},{3,2},{4,5},{5,4},{6,7},{7,6},{8,9},{9,8},{10,11... | collective-permute-start | bytes 393224 | tf_op jit(solution)/shard_map/ppermute | solution.py:22
  25.6 10.8 %collective-permute-start.9 = (bf16[8,32,512]{2,1,0:T(8,128)(2,1)S(1)}, bf16[8,32,512]{2,1,0:T(8,128)(2,1)S(1)}, u32[]{:S(2)}, u32[]{:S(2)}) collective-permute-start(bf16[8,32,512]{2,1,0:T(8,128)(2,1)S(1)} %pad_maximum_fusion.1.refs_6_), channel_id=1, source_target_pairs={{0,12},{1,13},{2,14},{3,15},{4,8},{5,9},{6,10},{7,11},{8,4},{9,5},... | collective-permute-start | bytes 786440 | tf_op jit(solution)/shard_map/ppermute | solution.py:22
  28.2 8.2 %collective-permute-start.10 = (bf16[8,32,512]{2,1,0:T(8,128)(2,1)S(1)}, bf16[8,32,512]{2,1,0:T(8,128)(2,1)S(1)}, u32[]{:S(2)}, u32[]{:S(2)}) collective-permute-start(bf16[8,32,512]{2,1,0:T(8,128)(2,1)S(1)} %pad_maximum_fusion.2.refs_8_), channel_id=1, source_target_pairs={{0,3},{1,2},{2,1},{3,0},{4,7},{5,6},{6,5},{7,4},{8,11},{9,10},{10,... | collective-permute-start | bytes 786440 | tf_op jit(solution)/shard_map/ppermute | solution.py:22
  36.4 10.1 %collective-permute-start.11 = (bf16[64,8192]{1,0:T(8,128)(2,1)}, bf16[64,8192]{1,0:T(8,128)(2,1)}, u32[]{:S(2)}, u32[]{:S(2)}) collective-permute-start(bf16[64,8192]{1,0:T(8,128)(2,1)} %collective-permute-done.2.refs_2_), channel_id=1, source_target_pairs={{0,16},{16,0},{32,48},{48,32},{64,80},{80,64},{96,112},{112,96},{1... | collective-permute-start | bytes 3145736 | tf_op jit(solution)/shard_map/ppermute | solution.py:30
  39.2 7.3 %collective-permute-start.12 = (bf16[64,8192]{1,0:T(8,128)(2,1)}, bf16[64,8192]{1,0:T(8,128)(2,1)}, u32[]{:S(2)}, u32[]{:S(2)}) collective-permute-start(bf16[64,8192]{1,0:T(8,128)(2,1)} %collective-permute-done.3.refs_3_), channel_id=1, source_target_pairs={{0,16},{16,0},{32,48},{48,32},{64,80},{80,64},{96,112},{112,96},{1... | collective-permute-start | bytes 3145736 | tf_op jit(solution)/shard_map/ppermute | solution.py:30
  39.8 3.0 %collective-permute-start = (bf16[64,4,896]{2,1,0:T(4,128)(2,1)S(1)}, bf16[64,4,896]{2,1,0:T(4,128)(2,1)S(1)}, u32[]{:S(2)}, u32[]{:S(2)}) collective-permute-start(bf16[64,4,896]{2,1,0:T(4,128)(2,1)S(1)} %copy.34), channel_id=1, source_target_pairs={{0,16},{16,0},{32,48},{48,32},{64,80},{80,64},{96,112},{112,96},{1... | collective-permute-start | bytes 1376264 | tf_op jit(solution)/shard_map/ppermute | solution.py:30
  40.4 3.2 %collective-permute-start.13 = (bf16[8,32,512]{2,1,0:T(8,128)(2,1)S(1)}, bf16[8,32,512]{2,1,0:T(8,128)(2,1)S(1)}, u32[]{:S(2)}, u32[]{:S(2)}) collective-permute-start(bf16[8,32,512]{2,1,0:T(8,128)(2,1)S(1)} %pad_maximum_fusion.1.refs_6_), channel_id=1, source_target_pairs={{0,16},{16,0},{32,48},{48,32},{64,80},{80,64},{96,112},{112,96},{1... | collective-permute-start | bytes 786440 | tf_op jit(solution)/shard_map/ppermute | solution.py:30
  40.5 3.8 %collective-permute-start.14 = (bf16[8,32,512]{2,1,0:T(8,128)(2,1)S(1)}, bf16[8,32,512]{2,1,0:T(8,128)(2,1)S(1)}, u32[]{:S(2)}, u32[]{:S(2)}) collective-permute-start(bf16[8,32,512]{2,1,0:T(8,128)(2,1)S(1)} %pad_maximum_fusion.2.refs_8_), channel_id=1, source_target_pairs={{0,16},{16,0},{32,48},{48,32},{64,80},{80,64},{96,112},{112,96},{1... | collective-permute-start | bytes 786440 | tf_op jit(solution)/shard_map/ppermute | solution.py:30
  42.8 3.6 %collective-permute-start.15 = (bf16[8,32,512]{2,1,0:T(8,128)(2,1)S(1)}, bf16[8,32,512]{2,1,0:T(8,128)(2,1)S(1)}, u32[]{:S(2)}, u32[]{:S(2)}) collective-permute-start(bf16[8,32,512]{2,1,0:T(8,128)(2,1)S(1)} %collective-permute-done.9.refs_7_), channel_id=1, source_target_pairs={{0,16},{16,0},{32,48},{48,32},{64,80},{80,64},{96,112},{112,96},{1... | collective-permute-start | bytes 786440 | tf_op jit(solution)/shard_map/ppermute | solution.py:30
  43.6 2.9 %collective-permute-start.16 = (bf16[8,32,512]{2,1,0:T(8,128)(2,1)S(1)}, bf16[8,32,512]{2,1,0:T(8,128)(2,1)S(1)}, u32[]{:S(2)}, u32[]{:S(2)}) collective-permute-start(bf16[8,32,512]{2,1,0:T(8,128)(2,1)S(1)} %collective-permute-done.10.refs_9_), channel_id=1, source_target_pairs={{0,16},{16,0},{32,48},{48,32},{64,80},{80,64},{96,112},{112,96},{1... | collective-permute-start | bytes 786440 | tf_op jit(solution)/shard_map/ppermute | solution.py:30
  44.3 11.2 %collective-permute-start.17 = (bf16[64,8192]{1,0:T(8,128)(2,1)}, bf16[64,8192]{1,0:T(8,128)(2,1)}, u32[]{:S(2)}, u32[]{:S(2)}) collective-permute-start(bf16[64,8192]{1,0:T(8,128)(2,1)} %refs_0_.1), channel_id=1, source_target_pairs={{0,16},{16,0},{32,48},{48,32},{64,80},{80,64},{96,112},{112,96},{1... | collective-permute-start | bytes 3145736 | tf_op jit(solution)/shard_map/ppermute | solution.py:30
  46.5 25.4 %all-to-all-start = ((bf16[64,8,896]{2,1,0:T(8,128)(2,1)}), bf16[64,8,896]{2,1,0:T(8,128)(2,1)S(1)}, u32[]{:S(2)}, u32[]{:S(2)}) async-start(bf16[64,8,896]{2,1,0:T(8,128)(2,1)} %pad_maximum_fusion), calls=%async_computation | async-start | bytes 1835008 | tf_op jit(solution)/shard_map/all_to_all | solution.py:371
  75.8 3.9 %collective-permute-start.20 = (f32[8,512]{1,0:T(8,128)S(1)}, f32[8,512]{1,0:T(8,128)S(1)}, u32[]{:S(2)}, u32[]{:S(2)}) collective-permute-start(f32[8,512]{1,0:T(8,128)S(1)} %row_stats.1), channel_id=1, source_target_pairs={{0,3},{1,2},{2,1},{3,0},{4,7},{5,6},{6,5},{7,4},{8,11},{9,10},{10,... | collective-permute-start | bytes 49160 | tf_op jit(solution)/shard_map/ppermute | solution.py:22
  76.4 4.1 %collective-permute-start.19 = (f32[8,512]{1,0:T(8,128)S(1)}, f32[8,512]{1,0:T(8,128)S(1)}, u32[]{:S(2)}, u32[]{:S(2)}) collective-permute-start(f32[8,512]{1,0:T(8,128)S(1)} %row_stats.1), channel_id=1, source_target_pairs={{0,2},{1,3},{2,0},{3,1},{4,6},{5,7},{6,4},{7,5},{8,10},{9,11},{10,... | collective-permute-start | bytes 49160 | tf_op jit(solution)/shard_map/ppermute | solution.py:22
  78.2 2.6 %collective-permute-start.18 = (f32[8,512]{1,0:T(8,128)S(1)}, f32[8,512]{1,0:T(8,128)S(1)}, u32[]{:S(2)}, u32[]{:S(2)}) collective-permute-start(f32[8,512]{1,0:T(8,128)S(1)} %row_stats.1), channel_id=1, source_target_pairs={{0,1},{1,0},{2,3},{3,2},{4,5},{5,4},{6,7},{7,6},{8,9},{9,8},{10,11... | collective-permute-start | bytes 49160 | tf_op jit(solution)/shard_map/ppermute | solution.py:22
  80.9 3.9 %collective-permute-start.23 = (f32[8,512]{1,0:T(8,128)S(1)}, f32[8,512]{1,0:T(8,128)S(1)}, u32[]{:S(2)}, u32[]{:S(2)}) collective-permute-start(f32[8,512]{1,0:T(8,128)S(1)} %stack.182), channel_id=1, source_target_pairs={{0,12},{1,13},{2,14},{3,15},{4,8},{5,9},{6,10},{7,11},{8,4},{9,5},... | collective-permute-start | bytes 49160 | tf_op jit(solution)/shard_map/ppermute | solution.py:22
  81.4 4.1 %collective-permute-start.22 = (f32[8,512]{1,0:T(8,128)S(1)}, f32[8,512]{1,0:T(8,128)S(1)}, u32[]{:S(2)}, u32[]{:S(2)}) collective-permute-start(f32[8,512]{1,0:T(8,128)S(1)} %stack.182), channel_id=1, source_target_pairs={{0,8},{1,9},{2,10},{3,11},{4,12},{5,13},{6,14},{7,15},{8,0},{9,1},... | collective-permute-start | bytes 49160 | tf_op jit(solution)/shard_map/ppermute | solution.py:22
  82.9 2.7 %collective-permute-start.21 = (f32[8,512]{1,0:T(8,128)S(1)}, f32[8,512]{1,0:T(8,128)S(1)}, u32[]{:S(2)}, u32[]{:S(2)}) collective-permute-start(f32[8,512]{1,0:T(8,128)S(1)} %stack.182), channel_id=1, source_target_pairs={{0,4},{1,5},{2,6},{3,7},{4,0},{5,1},{6,2},{7,3},{8,12},{9,13},{10,... | collective-permute-start | bytes 49160 | tf_op jit(solution)/shard_map/ppermute | solution.py:22
  85.8 4.0 %collective-permute-start.26 = (f32[8,512]{1,0:T(8,128)S(1)}, f32[8,512]{1,0:T(8,128)S(1)}, u32[]{:S(2)}, u32[]{:S(2)}) collective-permute-start(f32[8,512]{1,0:T(8,128)S(1)} %stack.195), channel_id=1, source_target_pairs={{0,96},{16,112},{32,64},{48,80},{64,32},{80,48},{96,0},{112,16},{1... | collective-permute-start | bytes 49160 | tf_op jit(solution)/shard_map/ppermute | solution.py:26
  88.5 4.1 %collective-permute-start.25 = (f32[8,512]{1,0:T(8,128)S(1)}, f32[8,512]{1,0:T(8,128)S(1)}, u32[]{:S(2)}, u32[]{:S(2)}) collective-permute-start(f32[8,512]{1,0:T(8,128)S(1)} %stack.195), channel_id=1, source_target_pairs={{0,64},{16,80},{32,96},{48,112},{64,0},{80,16},{96,32},{112,48},{1... | collective-permute-start | bytes 49160 | tf_op jit(solution)/shard_map/ppermute | solution.py:26
  88.8 3.7 %collective-permute-start.24 = (f32[8,512]{1,0:T(8,128)S(1)}, f32[8,512]{1,0:T(8,128)S(1)}, u32[]{:S(2)}, u32[]{:S(2)}) collective-permute-start(f32[8,512]{1,0:T(8,128)S(1)} %stack.195), channel_id=1, source_target_pairs={{0,32},{16,48},{32,0},{48,16},{64,96},{80,112},{96,64},{112,80},{1... | collective-permute-start | bytes 49160 | tf_op jit(solution)/shard_map/ppermute | solution.py:26
  92.8 5.9 %collective-permute-start.27 = (f32[8,512]{1,0:T(8,128)S(1)}, f32[8,512]{1,0:T(8,128)S(1)}, u32[]{:S(2)}, u32[]{:S(2)}) collective-permute-start(f32[8,512]{1,0:T(8,128)S(1)} %stack.208), channel_id=1, source_target_pairs={{0,16},{16,0},{32,48},{48,32},{64,80},{80,64},{96,112},{112,96},{1... | collective-permute-start | bytes 49160 | tf_op jit(solution)/shard_map/ppermute | solution.py:30
  100.9 2.8 %collective-permute-start.28 = (bf16[512,896]{1,0:T(8,128)(2,1)S(1)}, bf16[512,896]{1,0:T(8,128)(2,1)S(1)}, u32[]{:S(2)}, u32[]{:S(2)}) collective-permute-start(bf16[512,896]{1,0:T(8,128)(2,1)S(1)} %get-tuple-element.59.own_grad), channel_id=1, source_target_pairs={{0,16},{16,0},{32,48},{48,32},{64,80},{80,64},{96,112},{112,96},{1... | collective-permute-start | bytes 2752520 | tf_op jit(solution)/shard_map/ppermute | solution.py:30
  117.2 13.2 %collective-permute-start.29 = (bf16[256,1024]{1,0:T(8,128)(2,1)S(1)}, bf16[256,1024]{1,0:T(8,128)(2,1)S(1)}, u32[]{:S(2)}, u32[]{:S(2)}) collective-permute-start(bf16[256,1024]{1,0:T(8,128)(2,1)S(1)} %get-tuple-element.62), channel_id=1, source_target_pairs={{0,4},{1,5},{2,6},{3,7},{4,0},{5,1},{6,2},{7,3},{8,12},{9,13},{10,... | collective-permute-start | bytes 1572872 | tf_op jit(solution)/shard_map/ppermute | solution.py:22
  117.9 14.1 %collective-permute-start.31 = (bf16[256,1024]{1,0:T(8,128)(2,1)S(1)}, bf16[256,1024]{1,0:T(8,128)(2,1)S(1)}, u32[]{:S(2)}, u32[]{:S(2)}) collective-permute-start(bf16[256,1024]{1,0:T(8,128)(2,1)S(1)} %get-tuple-element.64), channel_id=1, source_target_pairs={{0,12},{1,13},{2,14},{3,15},{4,8},{5,9},{6,10},{7,11},{8,4},{9,5},... | collective-permute-start | bytes 1572872 | tf_op jit(solution)/shard_map/ppermute | solution.py:22
  119.3 12.9 %collective-permute-start.36 = (bf16[256,1024]{1,0:T(8,128)(2,1)S(1)}, bf16[256,1024]{1,0:T(8,128)(2,1)S(1)}, u32[]{:S(2)}, u32[]{:S(2)}) collective-permute-start(bf16[256,1024]{1,0:T(8,128)(2,1)S(1)} %get-tuple-element.66), channel_id=1, source_target_pairs={{0,1},{1,0},{2,3},{3,2},{4,5},{5,4},{6,7},{7,6},{8,9},{9,8},{10,11... | collective-permute-start | bytes 1572872 | tf_op jit(solution)/shard_map/ppermute | solution.py:22
  119.7 14.3 %collective-permute-start.38 = (bf16[256,1024]{1,0:T(8,128)(2,1)S(1)}, bf16[256,1024]{1,0:T(8,128)(2,1)S(1)}, u32[]{:S(2)}, u32[]{:S(2)}) collective-permute-start(bf16[256,1024]{1,0:T(8,128)(2,1)S(1)} %get-tuple-element.68), channel_id=1, source_target_pairs={{0,3},{1,2},{2,1},{3,0},{4,7},{5,6},{6,5},{7,4},{8,11},{9,10},{10,... | collective-permute-start | bytes 1572872 | tf_op jit(solution)/shard_map/ppermute | solution.py:22
  130.5 7.9 %collective-permute-start.30 = (bf16[128,1024]{1,0:T(8,128)(2,1)S(1)}, bf16[128,1024]{1,0:T(8,128)(2,1)S(1)}, u32[]{:S(2)}, u32[]{:S(2)}) collective-permute-start(bf16[128,1024]{1,0:T(8,128)(2,1)S(1)} %add_convert_fusion.7), channel_id=1, source_target_pairs={{0,12},{1,13},{2,14},{3,15},{4,8},{5,9},{6,10},{7,11},{8,4},{9,5},... | collective-permute-start | bytes 786440 | tf_op jit(solution)/shard_map/ppermute | solution.py:22
  132.0 6.5 %collective-permute-start.32 = (bf16[128,1024]{1,0:T(8,128)(2,1)S(1)}, bf16[128,1024]{1,0:T(8,128)(2,1)S(1)}, u32[]{:S(2)}, u32[]{:S(2)}) collective-permute-start(bf16[128,1024]{1,0:T(8,128)(2,1)S(1)} %add_convert_fusion.5), channel_id=1, source_target_pairs={{0,4},{1,5},{2,6},{3,7},{4,0},{5,1},{6,2},{7,3},{8,12},{9,13},{10,... | collective-permute-start | bytes 786440 | tf_op jit(solution)/shard_map/ppermute | solution.py:22
  132.2 10.5 %collective-permute-start.37 = (bf16[128,1024]{1,0:T(8,128)(2,1)S(1)}, bf16[128,1024]{1,0:T(8,128)(2,1)S(1)}, u32[]{:S(2)}, u32[]{:S(2)}) collective-permute-start(bf16[128,1024]{1,0:T(8,128)(2,1)S(1)} %add_convert_fusion.3), channel_id=1, source_target_pairs={{0,3},{1,2},{2,1},{3,0},{4,7},{5,6},{6,5},{7,4},{8,11},{9,10},{10,... | collective-permute-start | bytes 786440 | tf_op jit(solution)/shard_map/ppermute | solution.py:22
  134.1 8.7 %collective-permute-start.39 = (bf16[128,1024]{1,0:T(8,128)(2,1)S(1)}, bf16[128,1024]{1,0:T(8,128)(2,1)S(1)}, u32[]{:S(2)}, u32[]{:S(2)}) collective-permute-start(bf16[128,1024]{1,0:T(8,128)(2,1)S(1)} %add_convert_fusion.1), channel_id=1, source_target_pairs={{0,1},{1,0},{2,3},{3,2},{4,5},{5,4},{6,7},{7,6},{8,9},{9,8},{10,11... | collective-permute-start | bytes 786440 | tf_op jit(solution)/shard_map/ppermute | solution.py:22
  138.7 5.6 %collective-permute-start.35 = (bf16[32,2048]{1,0:T(8,128)(2,1)S(1)}, bf16[32,2048]{1,0:T(8,128)(2,1)S(1)}, u32[]{:S(2)}, u32[]{:S(2)}) collective-permute-start(bf16[32,2048]{1,0:T(8,128)(2,1)S(1)} %get-tuple-element.109), channel_id=1, source_target_pairs={{0,3},{1,2},{2,1},{3,0},{4,7},{5,6},{6,5},{7,4},{8,11},{9,10},{10,... | collective-permute-start | bytes 393224 | tf_op jit(solution)/shard_map/ppermute | solution.py:22
  140.4 6.5 %collective-permute-start.34 = (bf16[32,2048]{1,0:T(8,128)(2,1)S(1)}, bf16[32,2048]{1,0:T(8,128)(2,1)S(1)}, u32[]{:S(2)}, u32[]{:S(2)}) collective-permute-start(bf16[32,2048]{1,0:T(8,128)(2,1)S(1)} %get-tuple-element.110), channel_id=1, source_target_pairs={{0,1},{1,0},{2,3},{3,2},{4,5},{5,4},{6,7},{7,6},{8,9},{9,8},{10,11... | collective-permute-start | bytes 393224 | tf_op jit(solution)/shard_map/ppermute | solution.py:22
  140.4 6.5 %collective-permute-start.33 = (bf16[32,2048]{1,0:T(8,128)(2,1)S(1)}, bf16[32,2048]{1,0:T(8,128)(2,1)S(1)}, u32[]{:S(2)}, u32[]{:S(2)}) collective-permute-start(bf16[32,2048]{1,0:T(8,128)(2,1)S(1)} %get-tuple-element.108), channel_id=1, source_target_pairs={{0,2},{1,3},{2,0},{3,1},{4,6},{5,7},{6,4},{7,5},{8,10},{9,11},{10,... | collective-permute-start | bytes 393224 | tf_op jit(solution)/shard_map/ppermute | solution.py:22
  143.0 5.4 %collective-permute-start.42 = (bf16[32,2048]{1,0:T(8,128)(2,1)S(1)}, bf16[32,2048]{1,0:T(8,128)(2,1)S(1)}, u32[]{:S(2)}, u32[]{:S(2)}) collective-permute-start(bf16[32,2048]{1,0:T(8,128)(2,1)S(1)} %get-tuple-element.112), channel_id=1, source_target_pairs={{0,12},{1,13},{2,14},{3,15},{4,8},{5,9},{6,10},{7,11},{8,4},{9,5},... | collective-permute-start | bytes 393224 | tf_op jit(solution)/shard_map/ppermute | solution.py:22
  144.3 4.1 %collective-permute-start.41 = (bf16[32,2048]{1,0:T(8,128)(2,1)S(1)}, bf16[32,2048]{1,0:T(8,128)(2,1)S(1)}, u32[]{:S(2)}, u32[]{:S(2)}) collective-permute-start(bf16[32,2048]{1,0:T(8,128)(2,1)S(1)} %get-tuple-element.113), channel_id=1, source_target_pairs={{0,4},{1,5},{2,6},{3,7},{4,0},{5,1},{6,2},{7,3},{8,12},{9,13},{10,... | collective-permute-start | bytes 393224 | tf_op jit(solution)/shard_map/ppermute | solution.py:22
  144.3 6.4 %collective-permute-start.40 = (bf16[32,2048]{1,0:T(8,128)(2,1)S(1)}, bf16[32,2048]{1,0:T(8,128)(2,1)S(1)}, u32[]{:S(2)}, u32[]{:S(2)}) collective-permute-start(bf16[32,2048]{1,0:T(8,128)(2,1)S(1)} %get-tuple-element.111), channel_id=1, source_target_pairs={{0,8},{1,9},{2,10},{3,11},{4,12},{5,13},{6,14},{7,15},{8,0},{9,1},... | collective-permute-start | bytes 393224 | tf_op jit(solution)/shard_map/ppermute | solution.py:22
  150.8 4.4 %collective-permute-start.45 = (bf16[8,4096]{1,0:T(8,128)(2,1)S(1)}, bf16[8,4096]{1,0:T(8,128)(2,1)S(1)}, u32[]{:S(2)}, u32[]{:S(2)}) collective-permute-start(bf16[8,4096]{1,0:T(8,128)(2,1)S(1)} %get-tuple-element.115), channel_id=1, source_target_pairs={{0,96},{16,112},{32,64},{48,80},{64,32},{80,48},{96,0},{112,16},{1... | collective-permute-start | bytes 196616 | tf_op jit(solution)/shard_map/ppermute | solution.py:26
  152.9 3.1 %collective-permute-start.44 = (bf16[8,4096]{1,0:T(8,128)(2,1)S(1)}, bf16[8,4096]{1,0:T(8,128)(2,1)S(1)}, u32[]{:S(2)}, u32[]{:S(2)}) collective-permute-start(bf16[8,4096]{1,0:T(8,128)(2,1)S(1)} %get-tuple-element.116), channel_id=1, source_target_pairs={{0,32},{16,48},{32,0},{48,16},{64,96},{80,112},{96,64},{112,80},{1... | collective-permute-start | bytes 196616 | tf_op jit(solution)/shard_map/ppermute | solution.py:26
  152.9 4.6 %collective-permute-start.43 = (bf16[8,4096]{1,0:T(8,128)(2,1)S(1)}, bf16[8,4096]{1,0:T(8,128)(2,1)S(1)}, u32[]{:S(2)}, u32[]{:S(2)}) collective-permute-start(bf16[8,4096]{1,0:T(8,128)(2,1)S(1)} %get-tuple-element.114), channel_id=1, source_target_pairs={{0,64},{16,80},{32,96},{48,112},{64,0},{80,16},{96,32},{112,48},{1... | collective-permute-start | bytes 196616 | tf_op jit(solution)/shard_map/ppermute | solution.py:26
  157.6 7.0 %collective-permute-start.46 = (bf16[4,4096]{1,0:T(4,128)(2,1)S(1)}, bf16[4,4096]{1,0:T(4,128)(2,1)S(1)}, u32[]{:S(2)}, u32[]{:S(2)}) collective-permute-start(bf16[4,4096]{1,0:T(4,128)(2,1)S(1)} %get-tuple-element.120), channel_id=1, source_target_pairs={{0,16},{16,0},{32,48},{48,32},{64,80},{80,64},{96,112},{112,96},{1... | collective-permute-start | bytes 98312 | tf_op jit(solution)/shard_map/ppermute | solution.py:30
  (10 other events, 162.4 us)

commit v4 on v3

--- a/solution.py
+++ b/solution.py
@@ -49,8 +49,8 @@
 
 
 def logits_body(*refs):
-    (mine, theirs), near, gathered, weight, policy_ref = refs[:2], refs[2:6], refs[6:14], refs[14], refs[15]
-    states, pieces, slabs, sems = refs[16:]
+    (mine, theirs), near, gathered, weight, policy_ref = refs[:2], refs[2:6], refs[6:10], refs[10], refs[11]
+    states, pieces, slabs, sems = refs[12:]
     rows, width = mine.shape
     depth = width // (2 * RING)
     span = width // CHIPS
@@ -61,7 +61,7 @@
         return pl.ds(pl.multiple_of(start, size), size)
 
     loads = [
-        pltpu.make_async_copy(ref, pieces.at[i // 2, pl.ds(8 * (i % 2), 8)], sems.at[i]) for i, ref in enumerate(gathered)
+        pltpu.make_async_copy(ref, pieces.at[i], sems.at[i]) for i, ref in enumerate(gathered)
     ]
     blocks = [(0, 0, mine), (0, 1, theirs), (1, 0, near[0]), (3, 0, near[1]), (1, 1, near[2]), (3, 1, near[3])]
     slices = []
@@ -97,7 +97,7 @@
     return pl.pallas_call(
         logits_body,
         out_shape=jax.ShapeDtypeStruct((tokens, cols), F32),
-        in_specs=[any_spec()] * 15,
+        in_specs=[any_spec()] * 11,
         out_specs=pl.BlockSpec(memory_space=pltpu.VMEM),
         scratch_shapes=[
             pltpu.VMEM((tokens, width), BF16),
@@ -362,12 +362,14 @@
         by_y = jnp.concatenate([by_y, swap_tensor(by_y, step_y)], axis=0)
         by_x, by_y = lax.optimization_barrier((by_x, by_y))
     by_x, by_y, other_weight = lax.optimization_barrier((by_x, by_y, other_weight))
-    swapped = [swap_core(by_x), swap_core(by_y)]
     late = [swap_tensor(by_x, 12), swap_tensor(by_y, 3)]
-    near, late = lax.optimization_barrier((near, late))
+    ref_both, late = lax.optimization_barrier((ref_both, late))
+    gathered = [jnp.concatenate(pair, axis=0) for pair in zip((by_x, by_y), late)]
+    near, gathered = lax.optimization_barrier((near, gathered))
     near += [swap_core(a) for a in near]
-    swapped += [swap_core(a) for a in late]
-    ref_both, near, swapped = lax.optimization_barrier((ref_both, near, swapped))
+    gathered += [swap_core(a) for a in gathered]
+    ref_both, near, gathered = lax.optimization_barrier((ref_both, near, gathered))
+
     refer = lax.all_to_all(
         ref_both,
         ("dp", "tensor"),
@@ -378,7 +380,6 @@
             [(ring * CORES + c) * CHIPS + chip for ring in range(RING) for chip in range(CHIPS)] for c in range(CORES)
         ],
     )
-    gathered = [by_x, late[0], by_y, late[1], swapped[0], swapped[2], swapped[1], swapped[3]]
     policy = policy_logits(hidden, theirs, near, gathered, weight)
     refer, policy = lax.optimization_barrier((refer, policy))
     refer = refer.reshape(policy.shape)

time: 166 us -> 168 us (1.012)
  local copies, waits for them, and re-layouts: 4.96 us -> 7.89 us
    ppermute x9, waiting for transfers between devices: 16.8 us -> 9.79 us  [swap_z(): lax.ppermute(value, 'dp', [(i, i ^ offset * CORES) for i in range(RING *...]
    ppermute x26, waiting for transfers between devices: 26.5 us -> 32.4 us  [swap_tensor(): lax.ppermute(value, 'tensor', [(i, i ^ offset) for i in range(CHIPS)])]
    ppermute x12 -> x10, starting transfers between devices: 18.5 us -> 23 us  [swap_core(): return lax.ppermute(value, 'dp', [(i, i ^ 1) for i in range(RING * CORES)])]
    all_to_all x1, starting transfers between devices: 9.04 us -> 4.83 us  [shards(): lax.all_to_all(ref_both, ('dp', 'tensor'), split_axis=0, concat_axis=0, t...]
    unnamed x21 -> x27, local copies, waits for them, and re-layouts: 2.59 us -> 5.52 us
    ppermute x12 -> x10, waiting for transfers between devices: 6 us -> 8.16 us  [swap_core(): return lax.ppermute(value, 'dp', [(i, i ^ 1) for i in range(RING * CORES)])]
  transfers between devices with their start and end apart: 48 -> 46, of which waited for: 30 -> 28; matrix products, arithmetic and copies ran while one was open for 3% -> 4% of each run, Pallas kernels for 8% -> 8%
where the time goes in v4:
time: 168 us
  starting transfers between devices  71.9 us (43%)
  waiting for transfers between devices  53.4 us (32%)
  Pallas kernels  29.9 us (18%)
  local copies, waits for them, and re-layouts  7.89 us (5%)
  other arithmetic  3.79 us (2%)
    ppermute x26, waiting for transfers between devices, swap_tensor(): lax.ppermute(value, 'tensor', [(i, i ^ offset) for i in range(CHIPS)])  32.4 us
    ppermute x26, starting transfers between devices, swap_tensor(): lax.ppermute(value, 'tensor', [(i, i ^ offset) for i in range(CHIPS)])  29.9 us
    ppermute x10, starting transfers between devices, swap_core(): return lax.ppermute(value, 'dp', [(i, i ^ 1) for i in range(RING * CORES)])  23 us
    ppermute x9, starting transfers between devices, swap_z(): lax.ppermute(value, 'dp', [(i, i ^ offset * CORES) for i in range(RING *...  14.2 us
    pallas_call x1, Pallas kernels, policy_logits(): pl.pallas_call(logits_body, out_shape=jax.ShapeDtypeStruct((tokens, cols)...  13.1 us
    pallas_call x1, Pallas kernels, hidden_parts(): pl.pallas_call(hidden_body, out_shape=(jax.ShapeDtypeStruct((tokens // 2,...  12.5 us
    ppermute x9, waiting for transfers between devices, swap_z(): lax.ppermute(value, 'dp', [(i, i ^ offset * CORES) for i in range(RING *...  9.79 us
    ppermute x10, waiting for transfers between devices, swap_core(): return lax.ppermute(value, 'dp', [(i, i ^ 1) for i in range(RING * CORES)])  8.16 us
  transfers between devices with their start and end apart: 46, of which 28 were waited for; matrix products, arithmetic and copies ran while one was open for 4% of the time, Pallas kernels for 8%

profile of v4, /device:TPU:1, one launch (start us, length us, event | category | flops | bytes accessed | tf_op | source)
XLA Modules:
  0.0 168.0 jit_solution(12735596384837056885)
XLA Ops:
  0.6 1.5 collective-permute-start.6
  3.0 3.8 %collective-permute-start.1 = (bf16[4,32,512]{2,1,0:T(8,128)(2,1)S(1)}, bf16[4,32,512]{2,1,0:T(8,128)(2,1)S(1)}, u32[]{:S(2)}, u32[]{:S(2)}) collective-permute-start(bf16[4,32,512]{2,1,0:T(8,128)(2,1)S(1)} %pad_maximum_fusion.7), channel_id=1, source_target_pairs={{0,64},{16,80},{32,96},{48,112},{64,0},{80,16},{96,32},{112,48},{1... | collective-permute-start | bytes 393224 | tf_op jit(solution)/shard_map/ppermute | solution.py:26
  6.8 3.7 %collective-permute-done.1 = bf16[4,32,512]{2,1,0:T(8,128)(2,1)S(1)} collective-permute-done((bf16[4,32,512]{2,1,0:T(8,128)(2,1)S(1)}, bf16[4,32,512]{2,1,0:T(8,128)(2,1)S(1)}, u32[]{:S(2)}, u32[]{:S(2)}) %collective-permute-start.1) | collective-permute-done | bytes 131104 | tf_op jit(solution)/shard_map/ppermute | solution.py:26
  10.5 2.8 %collective-permute-start.2 = (bf16[2,32,512]{2,1,0:T(8,128)(2,1)S(1)}, bf16[2,32,512]{2,1,0:T(8,128)(2,1)S(1)}, u32[]{:S(2)}, u32[]{:S(2)}) collective-permute-start(bf16[2,32,512]{2,1,0:T(8,128)(2,1)S(1)} %get-tuple-element.124), channel_id=1, source_target_pairs={{0,3},{1,2},{2,1},{3,0},{4,7},{5,6},{6,5},{7,4},{8,11},{9,10},{10,... | collective-permute-start | bytes 196616 | tf_op jit(solution)/shard_map/ppermute | solution.py:22
  13.4 1.3 copy.76
  15.6 2.2 %collective-permute-start.10 = (bf16[64,8192]{1,0:T(8,128)(2,1)S(1)}, bf16[64,8192]{1,0:T(8,128)(2,1)S(1)}, u32[]{:S(2)}, u32[]{:S(2)}) collective-permute-start(bf16[64,8192]{1,0:T(8,128)(2,1)S(1)} %copy-done.6), channel_id=1, source_target_pairs={{0,96},{16,112},{32,64},{48,80},{64,32},{80,48},{96,0},{112,16},{1... | collective-permute-start | bytes 3145736 | tf_op jit(solution)/shard_map/ppermute | solution.py:26
  17.8 2.5 %collective-permute-start.3 = (bf16[2,32,512]{2,1,0:T(8,128)(2,1)S(1)}, bf16[2,32,512]{2,1,0:T(8,128)(2,1)S(1)}, u32[]{:S(2)}, u32[]{:S(2)}) collective-permute-start(bf16[2,32,512]{2,1,0:T(8,128)(2,1)S(1)} %get-tuple-element.123), channel_id=1, source_target_pairs={{0,12},{1,13},{2,14},{3,15},{4,8},{5,9},{6,10},{7,11},{8,4},{9,5},... | collective-permute-start | bytes 196616 | tf_op jit(solution)/shard_map/ppermute | solution.py:22
  20.3 2.1 %collective-permute-done.3 = bf16[2,32,512]{2,1,0:T(8,128)(2,1)S(1)} collective-permute-done((bf16[2,32,512]{2,1,0:T(8,128)(2,1)S(1)}, bf16[2,32,512]{2,1,0:T(8,128)(2,1)S(1)}, u32[]{:S(2)}, u32[]{:S(2)}) %collective-permute-start.3) | collective-permute-done | bytes 65568 | tf_op jit(solution)/shard_map/ppermute | solution.py:22
  23.0 2.9 %collective-permute-start = (bf16[64,4,896]{2,1,0:T(4,128)(2,1)S(1)}, bf16[64,4,896]{2,1,0:T(4,128)(2,1)S(1)}, u32[]{:S(2)}, u32[]{:S(2)}) collective-permute-start(bf16[64,4,896]{2,1,0:T(4,128)(2,1)S(1)} %copy.34), channel_id=1, source_target_pairs={{0,16},{16,0},{32,48},{48,32},{64,80},{80,64},{96,112},{112,96},{1... | collective-permute-start | bytes 1376264 | tf_op jit(solution)/shard_map/ppermute | solution.py:30
  26.7 4.1 %collective-permute-done.5 = bf16[4,32,512]{2,1,0:T(8,128)(2,1)S(1)} collective-permute-done((bf16[4,32,512]{2,1,0:T(8,128)(2,1)S(1)}, bf16[4,32,512]{2,1,0:T(8,128)(2,1)S(1)}, u32[]{:S(2)}, u32[]{:S(2)}) %collective-permute-start.5) | collective-permute-done | bytes 131104 | tf_op jit(solution)/shard_map/ppermute | solution.py:22
  30.8 2.6 %collective-permute-start.7 = (bf16[8,32,512]{2,1,0:T(8,128)(2,1)S(1)}, bf16[8,32,512]{2,1,0:T(8,128)(2,1)S(1)}, u32[]{:S(2)}, u32[]{:S(2)}) collective-permute-start(bf16[8,32,512]{2,1,0:T(8,128)(2,1)S(1)} %pad_maximum_fusion.3), channel_id=1, source_target_pairs={{0,12},{1,13},{2,14},{3,15},{4,8},{5,9},{6,10},{7,11},{8,4},{9,5},... | collective-permute-start | bytes 786440 | tf_op jit(solution)/shard_map/ppermute | solution.py:22
  33.8 1.4 pad_maximum_fusion
  35.2 2.4 %collective-permute-done.7 = bf16[8,32,512]{2,1,0:T(8,128)(2,1)S(1)} collective-permute-done((bf16[8,32,512]{2,1,0:T(8,128)(2,1)S(1)}, bf16[8,32,512]{2,1,0:T(8,128)(2,1)S(1)}, u32[]{:S(2)}, u32[]{:S(2)}) %collective-permute-start.7) | collective-permute-done | bytes 262176 | tf_op jit(solution)/shard_map/ppermute | solution.py:22
  37.6 2.5 %collective-permute-done.8 = bf16[8,32,512]{2,1,0:T(8,128)(2,1)S(1)} collective-permute-done((bf16[8,32,512]{2,1,0:T(8,128)(2,1)S(1)}, bf16[8,32,512]{2,1,0:T(8,128)(2,1)S(1)}, u32[]{:S(2)}, u32[]{:S(2)}) %collective-permute-start.8) | collective-permute-done | bytes 262176 | tf_op jit(solution)/shard_map/ppermute | solution.py:22
  40.2 5.5 %collective-permute-start.11 = (bf16[64,8192]{1,0:T(8,128)(2,1)S(1)}, bf16[64,8192]{1,0:T(8,128)(2,1)S(1)}, u32[]{:S(2)}, u32[]{:S(2)}) collective-permute-start(bf16[64,8192]{1,0:T(8,128)(2,1)S(1)} %collective-permute-done.9.refs_2_), channel_id=1, source_target_pairs={{0,16},{16,0},{32,48},{48,32},{64,80},{80,64},{96,112},{112,96},{1... | collective-permute-start | bytes 3145736 | tf_op jit(solution)/shard_map/ppermute | solution.py:30
  46.7 3.3 %collective-permute-done.13.refs_8_ = bf16[16,32,512]{2,1,0:T(8,128)(2,1)S(1)} collective-permute-done((bf16[16,32,512]{2,1,0:T(8,128)(2,1)S(1)}, bf16[16,32,512]{2,1,0:T(8,128)(2,1)S(1)}, u32[]{:S(2)}, u32[]{:S(2)}) %collective-permute-start.13) | collective-permute-done | bytes 524320 | tf_op jit(solution)/shard_map/ppermute | solution.py:30
  50.1 1.5 collective-permute-done.14.refs_9_
  52.4 1.0 copy-done.9
  53.3 4.8 %all-to-all-start = ((bf16[64,8,896]{2,1,0:T(8,128)(2,1)}), bf16[64,8,896]{2,1,0:T(8,128)(2,1)S(1)}, u32[]{:S(2)}, u32[]{:S(2)}) async-start(bf16[64,8,896]{2,1,0:T(8,128)(2,1)} %pad_maximum_fusion), calls=%async_computation | async-start | bytes 1835008 | tf_op jit(solution)/shard_map/all_to_all | solution.py:373
  58.2 13.1 %policy_logits.1.policy_ref = f32[512,896]{1,0:T(8,128)} custom-call(bf16[64,8192]{1,0:T(8,128)(2,1)} %refs_0_.1, bf16[64,8192]{1,0:T(8,128)(2,1)} %collective-permute-done.15.refs_1_, bf16[64,8192]{1,0:T(8,128)(2,1)} %copy-done.7, bf16[64,8192]{1,0:T(8,128)(2,1)} %copy-done.8, bf16[64,8192]{1,0:T(8,128)(2,1)} %copy-done.9, ...), custom_call_target="tpu_custom_call" | custom-call | flops 458752 | bytes 458752 | tf_op jit(solution)/shard_map/policy_logits/pallas_call | solution.py:97
  71.3 3.0 %all-to-all-done = bf16[64,8,896]{2,1,0:T(8,128)(2,1)S(1)} async-done(((bf16[64,8,896]{2,1,0:T(8,128)(2,1)}), bf16[64,8,896]{2,1,0:T(8,128)(2,1)S(1)}, u32[]{:S(2)}, u32[]{:S(2)}) %all-to-all-start) | async-done | bytes 917536 | tf_op jit(solution)/shard_map/all_to_all | solution.py:373
  74.3 1.5 copy-done
  75.8 2.3 %row_stats.1 = f32[8,512]{1,0:T(8,128)S(1)} custom-call(s32[512]{0:T(512)S(1)} %copy-done.3, f32[512,896]{1,0:T(8,128)S(1)} %copy-done, bf16[512,896]{1,0:T(8,128)(2,1)S(1)} %bitcast.199), custom_call_target="tpu_custom_call" | custom-call | flops 9175040 | bytes 2752512 | tf_op jit(solution)/shard_map/row_stats/pallas_call | solution.py:152
  78.7 2.1 %collective-permute-start.17 = (f32[8,512]{1,0:T(8,128)S(1)}, f32[8,512]{1,0:T(8,128)S(1)}, u32[]{:S(2)}, u32[]{:S(2)}) collective-permute-start(f32[8,512]{1,0:T(8,128)S(1)} %row_stats.1), channel_id=1, source_target_pairs={{0,2},{1,3},{2,0},{3,1},{4,6},{5,7},{6,4},{7,5},{8,10},{9,11},{10,... | collective-permute-start | bytes 49160 | tf_op jit(solution)/shard_map/ppermute | solution.py:22
  84.0 1.3 collective-permute-start.20
  85.3 1.6 collective-permute-start.19
  88.4 2.7 %collective-permute-start.24 = (f32[8,512]{1,0:T(8,128)S(1)}, f32[8,512]{1,0:T(8,128)S(1)}, u32[]{:S(2)}, u32[]{:S(2)}) collective-permute-start(f32[8,512]{1,0:T(8,128)S(1)} %stack.195), channel_id=1, source_target_pairs={{0,96},{16,112},{32,64},{48,80},{64,32},{80,48},{96,0},{112,16},{1... | collective-permute-start | bytes 49160 | tf_op jit(solution)/shard_map/ppermute | solution.py:26
  92.6 2.6 %collective-permute-done.23 = f32[8,512]{1,0:T(8,128)S(1)} collective-permute-done((f32[8,512]{1,0:T(8,128)S(1)}, f32[8,512]{1,0:T(8,128)S(1)}, u32[]{:S(2)}, u32[]{:S(2)}) %collective-permute-start.23) | collective-permute-done | bytes 16416 | tf_op jit(solution)/shard_map/ppermute | solution.py:26
  95.4 5.2 %collective-permute-start.25 = (f32[8,512]{1,0:T(8,128)S(1)}, f32[8,512]{1,0:T(8,128)S(1)}, u32[]{:S(2)}, u32[]{:S(2)}) collective-permute-start(f32[8,512]{1,0:T(8,128)S(1)} %stack.208), channel_id=1, source_target_pairs={{0,16},{16,0},{32,48},{48,32},{64,80},{80,64},{96,112},{112,96},{1... | collective-permute-start | bytes 49160 | tf_op jit(solution)/shard_map/ppermute | solution.py:30
  101.6 2.1 %logit_grads.1 = (bf16[512,896]{1,0:T(8,128)(2,1)S(1)}, f32[8,128]{1,0:T(8,128)S(1)}) custom-call(f32[8,512]{1,0:T(8,128)S(1)} %stack.219.stats_ref, s32[512]{0:T(512)S(1)} %copy-done.3, s32[512]{0:T(512)S(1)} %copy-done.4, s32[512]{0:T(512)S(1)} %copy-done.5, f32[512,896]{1,0:T(8,128)S(1)} %copy-done.1, bf16[512,896]{1,0:T(8,128)(2,1)S(1)} %bitcast.200), custom_call_target="tpu_custom_call" | custom-call | flops 469762048 | bytes 4587520 | tf_op jit(solution)/shard_map/logit_grads/pallas_call | solution.py:239
  104.4 2.1 %collective-permute-done.26.other_grad = bf16[512,896]{1,0:T(8,128)(2,1)S(1)} collective-permute-done((bf16[512,896]{1,0:T(8,128)(2,1)S(1)}, bf16[512,896]{1,0:T(8,128)(2,1)S(1)}, u32[]{:S(2)}, u32[]{:S(2)}) %collective-permute-start.26) | collective-permute-done | bytes 917536 | tf_op jit(solution)/shard_map/ppermute | solution.py:30
  107.5 12.5 %hidden_parts.1 = (bf16[256,1024]{1,0:T(8,128)(2,1)S(1)}, bf16[256,1024]{1,0:T(8,128)(2,1)S(1)}, bf16[256,1024]{1,0:T(8,128)(2,1)S(1)}, bf16[256,1024]{1,0:T(8,1...) custom-call(bf16[512,896]{1,0:T(8,128)(2,1)} %copy-done.2, ...), custom_call_target="tpu_custom_call" | custom-call | flops 7516192768 | bytes 26214400 | tf_op jit(solution)/shard_map/hidden_parts/pallas_call | solution.py:308
  120.5 1.5 collective-permute-start.29
  122.4 1.7 %collective-permute-start.36 = (bf16[256,1024]{1,0:T(8,128)(2,1)S(1)}, bf16[256,1024]{1,0:T(8,128)(2,1)S(1)}, u32[]{:S(2)}, u32[]{:S(2)}) collective-permute-start(bf16[256,1024]{1,0:T(8,128)(2,1)S(1)} %get-tuple-element.74), channel_id=1, source_target_pairs={{0,3},{1,2},{2,1},{3,0},{4,7},{5,6},{6,5},{7,4},{8,11},{9,10},{10,... | collective-permute-start | bytes 1572872 | tf_op jit(solution)/shard_map/ppermute | solution.py:22
  124.1 9.1 %collective-permute-done.27 = bf16[256,1024]{1,0:T(8,128)(2,1)S(1)} collective-permute-done((bf16[256,1024]{1,0:T(8,128)(2,1)S(1)}, bf16[256,1024]{1,0:T(8,128)(2,1)S(1)}, u32[]{:S(2)}, u32[]{:S(2)}) %collective-permute-start.27) | collective-permute-done | bytes 524320 | tf_op jit(solution)/shard_map/ppermute | solution.py:22
  133.3 1.2 collective-permute-start.28
  135.0 1.7 %collective-permute-start.35 = (bf16[128,1024]{1,0:T(8,128)(2,1)S(1)}, bf16[128,1024]{1,0:T(8,128)(2,1)S(1)}, u32[]{:S(2)}, u32[]{:S(2)}) collective-permute-start(bf16[128,1024]{1,0:T(8,128)(2,1)S(1)} %add_convert_fusion.3), channel_id=1, source_target_pairs={{0,3},{1,2},{2,1},{3,0},{4,7},{5,6},{6,5},{7,4},{8,11},{9,10},{10,... | collective-permute-start | bytes 786440 | tf_op jit(solution)/shard_map/ppermute | solution.py:22
  136.9 4.3 %collective-permute-done.28 = bf16[128,1024]{1,0:T(8,128)(2,1)S(1)} collective-permute-done((bf16[128,1024]{1,0:T(8,128)(2,1)S(1)}, bf16[128,1024]{1,0:T(8,128)(2,1)S(1)}, u32[]{:S(2)}, u32[]{:S(2)}) %collective-permute-start.28) | collective-permute-done | bytes 262176 | tf_op jit(solution)/shard_map/ppermute | solution.py:22
  141.5 1.6 collective-permute-start.33
  143.1 2.4 %collective-permute-start.31 = (bf16[32,2048]{1,0:T(8,128)(2,1)S(1)}, bf16[32,2048]{1,0:T(8,128)(2,1)S(1)}, u32[]{:S(2)}, u32[]{:S(2)}) collective-permute-start(bf16[32,2048]{1,0:T(8,128)(2,1)S(1)} %get-tuple-element.114), channel_id=1, source_target_pairs={{0,2},{1,3},{2,0},{3,1},{4,6},{5,7},{6,4},{7,5},{8,10},{9,11},{10,... | collective-permute-start | bytes 393224 | tf_op jit(solution)/shard_map/ppermute | solution.py:22
  145.8 1.3 collective-permute-start.40
  147.1 2.6 %collective-permute-start.38 = (bf16[32,2048]{1,0:T(8,128)(2,1)S(1)}, bf16[32,2048]{1,0:T(8,128)(2,1)S(1)}, u32[]{:S(2)}, u32[]{:S(2)}) collective-permute-start(bf16[32,2048]{1,0:T(8,128)(2,1)S(1)} %get-tuple-element.117), channel_id=1, source_target_pairs={{0,8},{1,9},{2,10},{3,11},{4,12},{5,13},{6,14},{7,15},{8,0},{9,1},... | collective-permute-start | bytes 393224 | tf_op jit(solution)/shard_map/ppermute | solution.py:22
  149.8 1.4 collective-permute-done.40
  151.2 2.3 %collective-permute-done.38 = bf16[32,2048]{1,0:T(8,128)(2,1)S(1)} collective-permute-done((bf16[32,2048]{1,0:T(8,128)(2,1)S(1)}, bf16[32,2048]{1,0:T(8,128)(2,1)S(1)}, u32[]{:S(2)}, u32[]{:S(2)}) %collective-permute-start.38) | collective-permute-done | bytes 131104 | tf_op jit(solution)/shard_map/ppermute | solution.py:22
  153.6 1.9 %collective-permute-start.43 = (bf16[8,4096]{1,0:T(8,128)(2,1)S(1)}, bf16[8,4096]{1,0:T(8,128)(2,1)S(1)}, u32[]{:S(2)}, u32[]{:S(2)}) collective-permute-start(bf16[8,4096]{1,0:T(8,128)(2,1)S(1)} %get-tuple-element.121), channel_id=1, source_target_pairs={{0,96},{16,112},{32,64},{48,80},{64,32},{80,48},{96,0},{112,16},{1... | collective-permute-start | bytes 196616 | tf_op jit(solution)/shard_map/ppermute | solution.py:26
  155.6 2.0 %collective-permute-start.41 = (bf16[8,4096]{1,0:T(8,128)(2,1)S(1)}, bf16[8,4096]{1,0:T(8,128)(2,1)S(1)}, u32[]{:S(2)}, u32[]{:S(2)}) collective-permute-start(bf16[8,4096]{1,0:T(8,128)(2,1)S(1)} %get-tuple-element.120), channel_id=1, source_target_pairs={{0,64},{16,80},{32,96},{48,112},{64,0},{80,16},{96,32},{112,48},{1... | collective-permute-start | bytes 196616 | tf_op jit(solution)/shard_map/ppermute | solution.py:26
  158.7 1.5 collective-permute-done.41
  160.3 6.2 %collective-permute-start.44 = (bf16[4,4096]{1,0:T(4,128)(2,1)S(1)}, bf16[4,4096]{1,0:T(4,128)(2,1)S(1)}, u32[]{:S(2)}, u32[]{:S(2)}) collective-permute-start(bf16[4,4096]{1,0:T(4,128)(2,1)S(1)} %get-tuple-element.126), channel_id=1, source_target_pairs={{0,16},{16,0},{32,48},{48,32},{64,80},{80,64},{96,112},{112,96},{1... | collective-permute-start | bytes 98312 | tf_op jit(solution)/shard_map/ppermute | solution.py:30
  (125 shorter events, 20.1 us)
Async XLA Ops:
  0.6 30.2 %collective-permute-start.6 = (bf16[8192,896]{1,0:T(8,128)(2,1)}, bf16[8192,896]{1,0:T(8,128)(2,1)}, u32[]{:S(2)}, u32[]{:S(2)}) collective-permute-start(bf16[8192,896]{1,0:T(8,128)(2,1)} %own_weight.1), channel_id=1, source_target_pairs={{0,16},{16,0},{32,48},{48,32},{64,80},{80,64},{96,112},{112,96},{1... | collective-permute-start | bytes 44040200 | tf_op jit(solution)/shard_map/ppermute | solution.py:30
  3.0 7.5 %collective-permute-start.1 = (bf16[4,32,512]{2,1,0:T(8,128)(2,1)S(1)}, bf16[4,32,512]{2,1,0:T(8,128)(2,1)S(1)}, u32[]{:S(2)}, u32[]{:S(2)}) collective-permute-start(bf16[4,32,512]{2,1,0:T(8,128)(2,1)S(1)} %pad_maximum_fusion.7), channel_id=1, source_target_pairs={{0,64},{16,80},{32,96},{48,112},{64,0},{80,16},{96,32},{112,48},{1... | collective-permute-start | bytes 393224 | tf_op jit(solution)/shard_map/ppermute | solution.py:26
  10.5 9.8 %collective-permute-start.2 = (bf16[2,32,512]{2,1,0:T(8,128)(2,1)S(1)}, bf16[2,32,512]{2,1,0:T(8,128)(2,1)S(1)}, u32[]{:S(2)}, u32[]{:S(2)}) collective-permute-start(bf16[2,32,512]{2,1,0:T(8,128)(2,1)S(1)} %get-tuple-element.124), channel_id=1, source_target_pairs={{0,3},{1,2},{2,1},{3,0},{4,7},{5,6},{6,5},{7,4},{8,11},{9,10},{10,... | collective-permute-start | bytes 196616 | tf_op jit(solution)/shard_map/ppermute | solution.py:22
  14.7 25.5 %collective-permute-start.9 = (bf16[64,8192]{1,0:T(8,128)(2,1)S(1)}, bf16[64,8192]{1,0:T(8,128)(2,1)S(1)}, u32[]{:S(2)}, u32[]{:S(2)}) collective-permute-start(bf16[64,8192]{1,0:T(8,128)(2,1)S(1)} %copy-done.6), channel_id=1, source_target_pairs={{0,32},{16,48},{32,0},{48,16},{64,96},{80,112},{96,64},{112,80},{1... | collective-permute-start | bytes 3145736 | tf_op jit(solution)/shard_map/ppermute | solution.py:26
  15.6 24.6 %collective-permute-start.10 = (bf16[64,8192]{1,0:T(8,128)(2,1)S(1)}, bf16[64,8192]{1,0:T(8,128)(2,1)S(1)}, u32[]{:S(2)}, u32[]{:S(2)}) collective-permute-start(bf16[64,8192]{1,0:T(8,128)(2,1)S(1)} %copy-done.6), channel_id=1, source_target_pairs={{0,96},{16,112},{32,64},{48,80},{64,32},{80,48},{96,0},{112,16},{1... | collective-permute-start | bytes 3145736 | tf_op jit(solution)/shard_map/ppermute | solution.py:26
  17.8 4.6 %collective-permute-start.3 = (bf16[2,32,512]{2,1,0:T(8,128)(2,1)S(1)}, bf16[2,32,512]{2,1,0:T(8,128)(2,1)S(1)}, u32[]{:S(2)}, u32[]{:S(2)}) collective-permute-start(bf16[2,32,512]{2,1,0:T(8,128)(2,1)S(1)} %get-tuple-element.123), channel_id=1, source_target_pairs={{0,12},{1,13},{2,14},{3,15},{4,8},{5,9},{6,10},{7,11},{8,4},{9,5},... | collective-permute-start | bytes 196616 | tf_op jit(solution)/shard_map/ppermute | solution.py:22
  22.5 4.2 %collective-permute-start.4 = (bf16[4,32,512]{2,1,0:T(8,128)(2,1)S(1)}, bf16[4,32,512]{2,1,0:T(8,128)(2,1)S(1)}, u32[]{:S(2)}, u32[]{:S(2)}) collective-permute-start(bf16[4,32,512]{2,1,0:T(8,128)(2,1)S(1)} %pad_maximum_fusion.8), channel_id=1, source_target_pairs={{0,4},{1,5},{2,6},{3,7},{4,0},{5,1},{6,2},{7,3},{8,12},{9,13},{10,... | collective-permute-start | bytes 393224 | tf_op jit(solution)/shard_map/ppermute | solution.py:22
  23.0 10.7 %collective-permute-start = (bf16[64,4,896]{2,1,0:T(4,128)(2,1)S(1)}, bf16[64,4,896]{2,1,0:T(4,128)(2,1)S(1)}, u32[]{:S(2)}, u32[]{:S(2)}) collective-permute-start(bf16[64,4,896]{2,1,0:T(4,128)(2,1)S(1)} %copy.34), channel_id=1, source_target_pairs={{0,16},{16,0},{32,48},{48,32},{64,80},{80,64},{96,112},{112,96},{1... | collective-permute-start | bytes 1376264 | tf_op jit(solution)/shard_map/ppermute | solution.py:30
  26.7 4.1 %collective-permute-start.5 = (bf16[4,32,512]{2,1,0:T(8,128)(2,1)S(1)}, bf16[4,32,512]{2,1,0:T(8,128)(2,1)S(1)}, u32[]{:S(2)}, u32[]{:S(2)}) collective-permute-start(bf16[4,32,512]{2,1,0:T(8,128)(2,1)S(1)} %pad_maximum_fusion.9), channel_id=1, source_target_pairs={{0,1},{1,0},{2,3},{3,2},{4,5},{5,4},{6,7},{7,6},{8,9},{9,8},{10,11... | collective-permute-start | bytes 393224 | tf_op jit(solution)/shard_map/ppermute | solution.py:22
  30.8 6.8 %collective-permute-start.7 = (bf16[8,32,512]{2,1,0:T(8,128)(2,1)S(1)}, bf16[8,32,512]{2,1,0:T(8,128)(2,1)S(1)}, u32[]{:S(2)}, u32[]{:S(2)}) collective-permute-start(bf16[8,32,512]{2,1,0:T(8,128)(2,1)S(1)} %pad_maximum_fusion.3), channel_id=1, source_target_pairs={{0,12},{1,13},{2,14},{3,15},{4,8},{5,9},{6,10},{7,11},{8,4},{9,5},... | collective-permute-start | bytes 786440 | tf_op jit(solution)/shard_map/ppermute | solution.py:22
  33.4 6.7 %collective-permute-start.8 = (bf16[8,32,512]{2,1,0:T(8,128)(2,1)S(1)}, bf16[8,32,512]{2,1,0:T(8,128)(2,1)S(1)}, u32[]{:S(2)}, u32[]{:S(2)}) collective-permute-start(bf16[8,32,512]{2,1,0:T(8,128)(2,1)S(1)} %pad_maximum_fusion.4), channel_id=1, source_target_pairs={{0,3},{1,2},{2,1},{3,0},{4,7},{5,6},{6,5},{7,4},{8,11},{9,10},{10,... | collective-permute-start | bytes 786440 | tf_op jit(solution)/shard_map/ppermute | solution.py:22
  40.2 11.4 %collective-permute-start.11 = (bf16[64,8192]{1,0:T(8,128)(2,1)S(1)}, bf16[64,8192]{1,0:T(8,128)(2,1)S(1)}, u32[]{:S(2)}, u32[]{:S(2)}) collective-permute-start(bf16[64,8192]{1,0:T(8,128)(2,1)S(1)} %collective-permute-done.9.refs_2_), channel_id=1, source_target_pairs={{0,16},{16,0},{32,48},{48,32},{64,80},{80,64},{96,112},{112,96},{1... | collective-permute-start | bytes 3145736 | tf_op jit(solution)/shard_map/ppermute | solution.py:30
  45.7 7.6 %collective-permute-start.12 = (bf16[64,8192]{1,0:T(8,128)(2,1)S(1)}, bf16[64,8192]{1,0:T(8,128)(2,1)}, u32[]{:S(2)}, u32[]{:S(2)}) collective-permute-start(bf16[64,8192]{1,0:T(8,128)(2,1)S(1)} %collective-permute-done.10.refs_3_), channel_id=1, source_target_pairs={{0,16},{16,0},{32,48},{48,32},{64,80},{80,64},{96,112},{112,96},{1... | collective-permute-start | bytes 3145736 | tf_op jit(solution)/shard_map/ppermute | solution.py:30
  45.8 4.3 %collective-permute-start.13 = (bf16[16,32,512]{2,1,0:T(8,128)(2,1)S(1)}, bf16[16,32,512]{2,1,0:T(8,128)(2,1)S(1)}, u32[]{:S(2)}, u32[]{:S(2)}) collective-permute-start(bf16[16,32,512]{2,1,0:T(8,128)(2,1)S(1)} %get-tuple-element.59.refs_6_), channel_id=1, source_target_pairs={{0,16},{16,0},{32,48},{48,32},{64,80},{80,64},{96,112},{112,96},{1... | collective-permute-start | bytes 1572872 | tf_op jit(solution)/shard_map/ppermute | solution.py:30
  46.2 5.3 %collective-permute-start.14 = (bf16[16,32,512]{2,1,0:T(8,128)(2,1)S(1)}, bf16[16,32,512]{2,1,0:T(8,128)(2,1)S(1)}, u32[]{:S(2)}, u32[]{:S(2)}) collective-permute-start(bf16[16,32,512]{2,1,0:T(8,128)(2,1)S(1)} %get-tuple-element.60.refs_7_), channel_id=1, source_target_pairs={{0,16},{16,0},{32,48},{48,32},{64,80},{80,64},{96,112},{112,96},{1... | collective-permute-start | bytes 1572872 | tf_op jit(solution)/shard_map/ppermute | solution.py:30
  46.3 11.9 %collective-permute-start.15 = (bf16[64,8192]{1,0:T(8,128)(2,1)S(1)}, bf16[64,8192]{1,0:T(8,128)(2,1)}, u32[]{:S(2)}, u32[]{:S(2)}) collective-permute-start(bf16[64,8192]{1,0:T(8,128)(2,1)S(1)} %copy-done.6), channel_id=1, source_target_pairs={{0,16},{16,0},{32,48},{48,32},{64,80},{80,64},{96,112},{112,96},{1... | collective-permute-start | bytes 3145736 | tf_op jit(solution)/shard_map/ppermute | solution.py:30
  53.3 20.9 %all-to-all-start = ((bf16[64,8,896]{2,1,0:T(8,128)(2,1)}), bf16[64,8,896]{2,1,0:T(8,128)(2,1)S(1)}, u32[]{:S(2)}, u32[]{:S(2)}) async-start(bf16[64,8,896]{2,1,0:T(8,128)(2,1)} %pad_maximum_fusion), calls=%async_computation | async-start | bytes 1835008 | tf_op jit(solution)/shard_map/all_to_all | solution.py:373
  75.8 25.9 %copy-start.4 = (s32[512]{0:T(512)S(1)}, s32[512]{0:T(512)}, u32[]{:S(2)}) copy-start(s32[512]{0:T(512)} %sequence_ref.1) | copy-start | bytes 6148
  75.8 25.9 %copy-start.5 = (s32[512]{0:T(512)S(1)}, s32[512]{0:T(512)}, u32[]{:S(2)}) copy-start(s32[512]{0:T(512)} %response_ref.1) | copy-start | bytes 6148
  78.1 3.9 %collective-permute-start.18 = (f32[8,512]{1,0:T(8,128)S(1)}, f32[8,512]{1,0:T(8,128)S(1)}, u32[]{:S(2)}, u32[]{:S(2)}) collective-permute-start(f32[8,512]{1,0:T(8,128)S(1)} %row_stats.1), channel_id=1, source_target_pairs={{0,3},{1,2},{2,1},{3,0},{4,7},{5,6},{6,5},{7,4},{8,11},{9,10},{10,... | collective-permute-start | bytes 49160 | tf_op jit(solution)/shard_map/ppermute | solution.py:22
  78.7 4.1 %collective-permute-start.17 = (f32[8,512]{1,0:T(8,128)S(1)}, f32[8,512]{1,0:T(8,128)S(1)}, u32[]{:S(2)}, u32[]{:S(2)}) collective-permute-start(f32[8,512]{1,0:T(8,128)S(1)} %row_stats.1), channel_id=1, source_target_pairs={{0,2},{1,3},{2,0},{3,1},{4,6},{5,7},{6,4},{7,5},{8,10},{9,11},{10,... | collective-permute-start | bytes 49160 | tf_op jit(solution)/shard_map/ppermute | solution.py:22
  80.8 2.6 %collective-permute-start.16 = (f32[8,512]{1,0:T(8,128)S(1)}, f32[8,512]{1,0:T(8,128)S(1)}, u32[]{:S(2)}, u32[]{:S(2)}) collective-permute-start(f32[8,512]{1,0:T(8,128)S(1)} %row_stats.1), channel_id=1, source_target_pairs={{0,1},{1,0},{2,3},{3,2},{4,5},{5,4},{6,7},{7,6},{8,9},{9,8},{10,11... | collective-permute-start | bytes 49160 | tf_op jit(solution)/shard_map/ppermute | solution.py:22
  83.6 3.9 %collective-permute-start.21 = (f32[8,512]{1,0:T(8,128)S(1)}, f32[8,512]{1,0:T(8,128)S(1)}, u32[]{:S(2)}, u32[]{:S(2)}) collective-permute-start(f32[8,512]{1,0:T(8,128)S(1)} %stack.182), channel_id=1, source_target_pairs={{0,12},{1,13},{2,14},{3,15},{4,8},{5,9},{6,10},{7,11},{8,4},{9,5},... | collective-permute-start | bytes 49160 | tf_op jit(solution)/shard_map/ppermute | solution.py:22
  84.0 4.1 %collective-permute-start.20 = (f32[8,512]{1,0:T(8,128)S(1)}, f32[8,512]{1,0:T(8,128)S(1)}, u32[]{:S(2)}, u32[]{:S(2)}) collective-permute-start(f32[8,512]{1,0:T(8,128)S(1)} %stack.182), channel_id=1, source_target_pairs={{0,8},{1,9},{2,10},{3,11},{4,12},{5,13},{6,14},{7,15},{8,0},{9,1},... | collective-permute-start | bytes 49160 | tf_op jit(solution)/shard_map/ppermute | solution.py:22
  85.3 2.9 %collective-permute-start.19 = (f32[8,512]{1,0:T(8,128)S(1)}, f32[8,512]{1,0:T(8,128)S(1)}, u32[]{:S(2)}, u32[]{:S(2)}) collective-permute-start(f32[8,512]{1,0:T(8,128)S(1)} %stack.182), channel_id=1, source_target_pairs={{0,4},{1,5},{2,6},{3,7},{4,0},{5,1},{6,2},{7,3},{8,12},{9,13},{10,... | collective-permute-start | bytes 49160 | tf_op jit(solution)/shard_map/ppermute | solution.py:22
  88.4 4.2 %collective-permute-start.24 = (f32[8,512]{1,0:T(8,128)S(1)}, f32[8,512]{1,0:T(8,128)S(1)}, u32[]{:S(2)}, u32[]{:S(2)}) collective-permute-start(f32[8,512]{1,0:T(8,128)S(1)} %stack.195), channel_id=1, source_target_pairs={{0,96},{16,112},{32,64},{48,80},{64,32},{80,48},{96,0},{112,16},{1... | collective-permute-start | bytes 49160 | tf_op jit(solution)/shard_map/ppermute | solution.py:26
  91.1 4.1 %collective-permute-start.23 = (f32[8,512]{1,0:T(8,128)S(1)}, f32[8,512]{1,0:T(8,128)S(1)}, u32[]{:S(2)}, u32[]{:S(2)}) collective-permute-start(f32[8,512]{1,0:T(8,128)S(1)} %stack.195), channel_id=1, source_target_pairs={{0,64},{16,80},{32,96},{48,112},{64,0},{80,16},{96,32},{112,48},{1... | collective-permute-start | bytes 49160 | tf_op jit(solution)/shard_map/ppermute | solution.py:26
  91.4 3.7 %collective-permute-start.22 = (f32[8,512]{1,0:T(8,128)S(1)}, f32[8,512]{1,0:T(8,128)S(1)}, u32[]{:S(2)}, u32[]{:S(2)}) collective-permute-start(f32[8,512]{1,0:T(8,128)S(1)} %stack.195), channel_id=1, source_target_pairs={{0,32},{16,48},{32,0},{48,16},{64,96},{80,112},{96,64},{112,80},{1... | collective-permute-start | bytes 49160 | tf_op jit(solution)/shard_map/ppermute | solution.py:26
  95.4 6.1 %collective-permute-start.25 = (f32[8,512]{1,0:T(8,128)S(1)}, f32[8,512]{1,0:T(8,128)S(1)}, u32[]{:S(2)}, u32[]{:S(2)}) collective-permute-start(f32[8,512]{1,0:T(8,128)S(1)} %stack.208), channel_id=1, source_target_pairs={{0,16},{16,0},{32,48},{48,32},{64,80},{80,64},{96,112},{112,96},{1... | collective-permute-start | bytes 49160 | tf_op jit(solution)/shard_map/ppermute | solution.py:30
  103.7 2.8 %collective-permute-start.26 = (bf16[512,896]{1,0:T(8,128)(2,1)S(1)}, bf16[512,896]{1,0:T(8,128)(2,1)S(1)}, u32[]{:S(2)}, u32[]{:S(2)}) collective-permute-start(bf16[512,896]{1,0:T(8,128)(2,1)S(1)} %get-tuple-element.65.own_grad), channel_id=1, source_target_pairs={{0,16},{16,0},{32,48},{48,32},{64,80},{80,64},{96,112},{112,96},{1... | collective-permute-start | bytes 2752520 | tf_op jit(solution)/shard_map/ppermute | solution.py:30
  120.0 13.2 %collective-permute-start.27 = (bf16[256,1024]{1,0:T(8,128)(2,1)S(1)}, bf16[256,1024]{1,0:T(8,128)(2,1)S(1)}, u32[]{:S(2)}, u32[]{:S(2)}) collective-permute-start(bf16[256,1024]{1,0:T(8,128)(2,1)S(1)} %get-tuple-element.68), channel_id=1, source_target_pairs={{0,4},{1,5},{2,6},{3,7},{4,0},{5,1},{6,2},{7,3},{8,12},{9,13},{10,... | collective-permute-start | bytes 1572872 | tf_op jit(solution)/shard_map/ppermute | solution.py:22
  120.5 14.1 %collective-permute-start.29 = (bf16[256,1024]{1,0:T(8,128)(2,1)S(1)}, bf16[256,1024]{1,0:T(8,128)(2,1)S(1)}, u32[]{:S(2)}, u32[]{:S(2)}) collective-permute-start(bf16[256,1024]{1,0:T(8,128)(2,1)S(1)} %get-tuple-element.70), channel_id=1, source_target_pairs={{0,12},{1,13},{2,14},{3,15},{4,8},{5,9},{6,10},{7,11},{8,4},{9,5},... | collective-permute-start | bytes 1572872 | tf_op jit(solution)/shard_map/ppermute | solution.py:22
  122.0 12.9 %collective-permute-start.34 = (bf16[256,1024]{1,0:T(8,128)(2,1)S(1)}, bf16[256,1024]{1,0:T(8,128)(2,1)S(1)}, u32[]{:S(2)}, u32[]{:S(2)}) collective-permute-start(bf16[256,1024]{1,0:T(8,128)(2,1)S(1)} %get-tuple-element.72), channel_id=1, source_target_pairs={{0,1},{1,0},{2,3},{3,2},{4,5},{5,4},{6,7},{7,6},{8,9},{9,8},{10,11... | collective-permute-start | bytes 1572872 | tf_op jit(solution)/shard_map/ppermute | solution.py:22
  122.4 14.3 %collective-permute-start.36 = (bf16[256,1024]{1,0:T(8,128)(2,1)S(1)}, bf16[256,1024]{1,0:T(8,128)(2,1)S(1)}, u32[]{:S(2)}, u32[]{:S(2)}) collective-permute-start(bf16[256,1024]{1,0:T(8,128)(2,1)S(1)} %get-tuple-element.74), channel_id=1, source_target_pairs={{0,3},{1,2},{2,1},{3,0},{4,7},{5,6},{6,5},{7,4},{8,11},{9,10},{10,... | collective-permute-start | bytes 1572872 | tf_op jit(solution)/shard_map/ppermute | solution.py:22
  133.3 7.9 %collective-permute-start.28 = (bf16[128,1024]{1,0:T(8,128)(2,1)S(1)}, bf16[128,1024]{1,0:T(8,128)(2,1)S(1)}, u32[]{:S(2)}, u32[]{:S(2)}) collective-permute-start(bf16[128,1024]{1,0:T(8,128)(2,1)S(1)} %add_convert_fusion.7), channel_id=1, source_target_pairs={{0,12},{1,13},{2,14},{3,15},{4,8},{5,9},{6,10},{7,11},{8,4},{9,5},... | collective-permute-start | bytes 786440 | tf_op jit(solution)/shard_map/ppermute | solution.py:22
  134.6 6.7 %collective-permute-start.30 = (bf16[128,1024]{1,0:T(8,128)(2,1)S(1)}, bf16[128,1024]{1,0:T(8,128)(2,1)S(1)}, u32[]{:S(2)}, u32[]{:S(2)}) collective-permute-start(bf16[128,1024]{1,0:T(8,128)(2,1)S(1)} %add_convert_fusion.5), channel_id=1, source_target_pairs={{0,4},{1,5},{2,6},{3,7},{4,0},{5,1},{6,2},{7,3},{8,12},{9,13},{10,... | collective-permute-start | bytes 786440 | tf_op jit(solution)/shard_map/ppermute | solution.py:22
  135.0 10.5 %collective-permute-start.35 = (bf16[128,1024]{1,0:T(8,128)(2,1)S(1)}, bf16[128,1024]{1,0:T(8,128)(2,1)S(1)}, u32[]{:S(2)}, u32[]{:S(2)}) collective-permute-start(bf16[128,1024]{1,0:T(8,128)(2,1)S(1)} %add_convert_fusion.3), channel_id=1, source_target_pairs={{0,3},{1,2},{2,1},{3,0},{4,7},{5,6},{6,5},{7,4},{8,11},{9,10},{10,... | collective-permute-start | bytes 786440 | tf_op jit(solution)/shard_map/ppermute | solution.py:22
  136.8 8.8 %collective-permute-start.37 = (bf16[128,1024]{1,0:T(8,128)(2,1)S(1)}, bf16[128,1024]{1,0:T(8,128)(2,1)S(1)}, u32[]{:S(2)}, u32[]{:S(2)}) collective-permute-start(bf16[128,1024]{1,0:T(8,128)(2,1)S(1)} %add_convert_fusion.1), channel_id=1, source_target_pairs={{0,1},{1,0},{2,3},{3,2},{4,5},{5,4},{6,7},{7,6},{8,9},{9,8},{10,11... | collective-permute-start | bytes 786440 | tf_op jit(solution)/shard_map/ppermute | solution.py:22
  141.5 5.6 %collective-permute-start.33 = (bf16[32,2048]{1,0:T(8,128)(2,1)S(1)}, bf16[32,2048]{1,0:T(8,128)(2,1)S(1)}, u32[]{:S(2)}, u32[]{:S(2)}) collective-permute-start(bf16[32,2048]{1,0:T(8,128)(2,1)S(1)} %get-tuple-element.115), channel_id=1, source_target_pairs={{0,3},{1,2},{2,1},{3,0},{4,7},{5,6},{6,5},{7,4},{8,11},{9,10},{10,... | collective-permute-start | bytes 393224 | tf_op jit(solution)/shard_map/ppermute | solution.py:22
  143.1 6.6 %collective-permute-start.32 = (bf16[32,2048]{1,0:T(8,128)(2,1)S(1)}, bf16[32,2048]{1,0:T(8,128)(2,1)S(1)}, u32[]{:S(2)}, u32[]{:S(2)}) collective-permute-start(bf16[32,2048]{1,0:T(8,128)(2,1)S(1)} %get-tuple-element.116), channel_id=1, source_target_pairs={{0,1},{1,0},{2,3},{3,2},{4,5},{5,4},{6,7},{7,6},{8,9},{9,8},{10,11... | collective-permute-start | bytes 393224 | tf_op jit(solution)/shard_map/ppermute | solution.py:22
  143.1 6.6 %collective-permute-start.31 = (bf16[32,2048]{1,0:T(8,128)(2,1)S(1)}, bf16[32,2048]{1,0:T(8,128)(2,1)S(1)}, u32[]{:S(2)}, u32[]{:S(2)}) collective-permute-start(bf16[32,2048]{1,0:T(8,128)(2,1)S(1)} %get-tuple-element.114), channel_id=1, source_target_pairs={{0,2},{1,3},{2,0},{3,1},{4,6},{5,7},{6,4},{7,5},{8,10},{9,11},{10,... | collective-permute-start | bytes 393224 | tf_op jit(solution)/shard_map/ppermute | solution.py:22
  145.8 5.4 %collective-permute-start.40 = (bf16[32,2048]{1,0:T(8,128)(2,1)S(1)}, bf16[32,2048]{1,0:T(8,128)(2,1)S(1)}, u32[]{:S(2)}, u32[]{:S(2)}) collective-permute-start(bf16[32,2048]{1,0:T(8,128)(2,1)S(1)} %get-tuple-element.118), channel_id=1, source_target_pairs={{0,12},{1,13},{2,14},{3,15},{4,8},{5,9},{6,10},{7,11},{8,4},{9,5},... | collective-permute-start | bytes 393224 | tf_op jit(solution)/shard_map/ppermute | solution.py:22
  147.1 4.1 %collective-permute-start.39 = (bf16[32,2048]{1,0:T(8,128)(2,1)S(1)}, bf16[32,2048]{1,0:T(8,128)(2,1)S(1)}, u32[]{:S(2)}, u32[]{:S(2)}) collective-permute-start(bf16[32,2048]{1,0:T(8,128)(2,1)S(1)} %get-tuple-element.119), channel_id=1, source_target_pairs={{0,4},{1,5},{2,6},{3,7},{4,0},{5,1},{6,2},{7,3},{8,12},{9,13},{10,... | collective-permute-start | bytes 393224 | tf_op jit(solution)/shard_map/ppermute | solution.py:22
  147.1 6.4 %collective-permute-start.38 = (bf16[32,2048]{1,0:T(8,128)(2,1)S(1)}, bf16[32,2048]{1,0:T(8,128)(2,1)S(1)}, u32[]{:S(2)}, u32[]{:S(2)}) collective-permute-start(bf16[32,2048]{1,0:T(8,128)(2,1)S(1)} %get-tuple-element.117), channel_id=1, source_target_pairs={{0,8},{1,9},{2,10},{3,11},{4,12},{5,13},{6,14},{7,15},{8,0},{9,1},... | collective-permute-start | bytes 393224 | tf_op jit(solution)/shard_map/ppermute | solution.py:22
  153.6 4.4 %collective-permute-start.43 = (bf16[8,4096]{1,0:T(8,128)(2,1)S(1)}, bf16[8,4096]{1,0:T(8,128)(2,1)S(1)}, u32[]{:S(2)}, u32[]{:S(2)}) collective-permute-start(bf16[8,4096]{1,0:T(8,128)(2,1)S(1)} %get-tuple-element.121), channel_id=1, source_target_pairs={{0,96},{16,112},{32,64},{48,80},{64,32},{80,48},{96,0},{112,16},{1... | collective-permute-start | bytes 196616 | tf_op jit(solution)/shard_map/ppermute | solution.py:26
  155.6 3.1 %collective-permute-start.42 = (bf16[8,4096]{1,0:T(8,128)(2,1)S(1)}, bf16[8,4096]{1,0:T(8,128)(2,1)S(1)}, u32[]{:S(2)}, u32[]{:S(2)}) collective-permute-start(bf16[8,4096]{1,0:T(8,128)(2,1)S(1)} %get-tuple-element.122), channel_id=1, source_target_pairs={{0,32},{16,48},{32,0},{48,16},{64,96},{80,112},{96,64},{112,80},{1... | collective-permute-start | bytes 196616 | tf_op jit(solution)/shard_map/ppermute | solution.py:26
  155.6 4.6 %collective-permute-start.41 = (bf16[8,4096]{1,0:T(8,128)(2,1)S(1)}, bf16[8,4096]{1,0:T(8,128)(2,1)S(1)}, u32[]{:S(2)}, u32[]{:S(2)}) collective-permute-start(bf16[8,4096]{1,0:T(8,128)(2,1)S(1)} %get-tuple-element.120), channel_id=1, source_target_pairs={{0,64},{16,80},{32,96},{48,112},{64,0},{80,16},{96,32},{112,48},{1... | collective-permute-start | bytes 196616 | tf_op jit(solution)/shard_map/ppermute | solution.py:26
  160.3 7.0 %collective-permute-start.44 = (bf16[4,4096]{1,0:T(4,128)(2,1)S(1)}, bf16[4,4096]{1,0:T(4,128)(2,1)S(1)}, u32[]{:S(2)}, u32[]{:S(2)}) collective-permute-start(bf16[4,4096]{1,0:T(4,128)(2,1)S(1)} %get-tuple-element.126), channel_id=1, source_target_pairs={{0,16},{16,0},{32,48},{48,32},{64,80},{80,64},{96,112},{112,96},{1... | collective-permute-start | bytes 98312 | tf_op jit(solution)/shard_map/ppermute | solution.py:30
  (11 other events, 102.5 us)

commit v5 on v3

--- a/solution.py
+++ b/solution.py
@@ -364,10 +364,7 @@
     by_x, by_y, other_weight = lax.optimization_barrier((by_x, by_y, other_weight))
     swapped = [swap_core(by_x), swap_core(by_y)]
     late = [swap_tensor(by_x, 12), swap_tensor(by_y, 3)]
-    near, late = lax.optimization_barrier((near, late))
-    near += [swap_core(a) for a in near]
-    swapped += [swap_core(a) for a in late]
-    ref_both, near, swapped = lax.optimization_barrier((ref_both, near, swapped))
+    ref_both, swapped = lax.optimization_barrier((ref_both, swapped))
     refer = lax.all_to_all(
         ref_both,
         ("dp", "tensor"),
@@ -378,6 +375,9 @@
             [(ring * CORES + c) * CHIPS + chip for ring in range(RING) for chip in range(CHIPS)] for c in range(CORES)
         ],
     )
+    near, late = lax.optimization_barrier((near, late))
+    near += [swap_core(a) for a in near]
+    swapped += [swap_core(a) for a in late]
     gathered = [by_x, late[0], by_y, late[1], swapped[0], swapped[2], swapped[1], swapped[3]]
     policy = policy_logits(hidden, theirs, near, gathered, weight)
     refer, policy = lax.optimization_barrier((refer, policy))

time: 166 us -> 163 us (0.982)
  waiting for transfers between devices: 52.5 us -> 48.4 us
  local copies, waits for them, and re-layouts: 4.96 us -> 6.82 us
    ppermute x26, waiting for transfers between devices: 26.5 us -> 31.8 us  [swap_tensor(): lax.ppermute(value, 'tensor', [(i, i ^ offset) for i in range(CHIPS)])]
    ppermute x9, waiting for transfers between devices: 16.8 us -> 11.9 us  [swap_z(): lax.ppermute(value, 'dp', [(i, i ^ offset * CORES) for i in range(RING *...]
    ppermute x12, starting transfers between devices: 18.5 us -> 22.7 us  [swap_core(): return lax.ppermute(value, 'dp', [(i, i ^ 1) for i in range(RING * CORES)])]
    all_to_all x1, waiting for transfers between devices: 3.26 us -> 0.1 us  [shards(): lax.all_to_all(ref_both, ('dp', 'tensor'), split_axis=0, concat_axis=0, t...]
    all_to_all x1, starting transfers between devices: 9.04 us -> 6.09 us  [shards(): lax.all_to_all(ref_both, ('dp', 'tensor'), split_axis=0, concat_axis=0, t...]
    unnamed x21 -> x19, local copies, waits for them, and re-layouts: 2.59 us -> 4.45 us
  transfers between devices with their start and end apart: 48 -> 48, of which waited for: 30 -> 24; matrix products, arithmetic and copies ran while one was open for 3% -> 4% of each run, Pallas kernels for 8% -> 8%
where the time goes in v5:
time: 163 us
  starting transfers between devices  72.8 us (45%)
  waiting for transfers between devices  48.4 us (30%)
  Pallas kernels  30 us (18%)
  local copies, waits for them, and re-layouts  6.82 us (4%)
  other arithmetic  3.7 us (2%)
    ppermute x26, waiting for transfers between devices, swap_tensor(): lax.ppermute(value, 'tensor', [(i, i ^ offset) for i in range(CHIPS)])  31.8 us
    ppermute x26, starting transfers between devices, swap_tensor(): lax.ppermute(value, 'tensor', [(i, i ^ offset) for i in range(CHIPS)])  29.9 us
    ppermute x12, starting transfers between devices, swap_core(): return lax.ppermute(value, 'dp', [(i, i ^ 1) for i in range(RING * CORES)])  22.7 us
    ppermute x9, starting transfers between devices, swap_z(): lax.ppermute(value, 'dp', [(i, i ^ offset * CORES) for i in range(RING *...  14.1 us
    pallas_call x1, Pallas kernels, policy_logits(): pl.pallas_call(logits_body, out_shape=jax.ShapeDtypeStruct((tokens, cols)...  13.1 us
    pallas_call x1, Pallas kernels, hidden_parts(): pl.pallas_call(hidden_body, out_shape=(jax.ShapeDtypeStruct((tokens // 2,...  12.5 us
    ppermute x9, waiting for transfers between devices, swap_z(): lax.ppermute(value, 'dp', [(i, i ^ offset * CORES) for i in range(RING *...  11.9 us
    all_to_all x1, starting transfers between devices, shards(): lax.all_to_all(ref_both, ('dp', 'tensor'), split_axis=0, concat_axis=0, t...  6.09 us
  transfers between devices with their start and end apart: 48, of which 24 were waited for; matrix products, arithmetic and copies ran while one was open for 4% of the time, Pallas kernels for 8%

profile of v5, /device:TPU:1, one launch (start us, length us, event | category | flops | bytes accessed | tf_op | source)
XLA Modules:
  0.0 162.7 jit_solution(4046291773712781648)
XLA Ops:
  0.6 1.5 collective-permute-start.6
  3.0 3.8 %collective-permute-start.1 = (bf16[4,32,512]{2,1,0:T(8,128)(2,1)S(1)}, bf16[4,32,512]{2,1,0:T(8,128)(2,1)S(1)}, u32[]{:S(2)}, u32[]{:S(2)}) collective-permute-start(bf16[4,32,512]{2,1,0:T(8,128)(2,1)S(1)} %pad_maximum_fusion.5), channel_id=1, source_target_pairs={{0,64},{16,80},{32,96},{48,112},{64,0},{80,16},{96,32},{112,48},{1... | collective-permute-start | bytes 393224 | tf_op jit(solution)/shard_map/ppermute | solution.py:26
  6.7 3.8 %collective-permute-done.1 = bf16[4,32,512]{2,1,0:T(8,128)(2,1)S(1)} collective-permute-done((bf16[4,32,512]{2,1,0:T(8,128)(2,1)S(1)}, bf16[4,32,512]{2,1,0:T(8,128)(2,1)S(1)}, u32[]{:S(2)}, u32[]{:S(2)}) %collective-permute-start.1) | collective-permute-done | bytes 131104 | tf_op jit(solution)/shard_map/ppermute | solution.py:26
  11.4 2.2 %collective-permute-start.11 = (bf16[64,8192]{1,0:T(8,128)(2,1)}, bf16[64,8192]{1,0:T(8,128)(2,1)}, u32[]{:S(2)}, u32[]{:S(2)}) collective-permute-start(bf16[64,8192]{1,0:T(8,128)(2,1)} %refs_0_.1), channel_id=1, source_target_pairs={{0,96},{16,112},{32,64},{48,80},{64,32},{80,48},{96,0},{112,16},{1... | collective-permute-start | bytes 3145736 | tf_op jit(solution)/shard_map/ppermute | solution.py:26
  13.6 2.8 %collective-permute-start.2 = (bf16[2,32,512]{2,1,0:T(8,128)(2,1)S(1)}, bf16[2,32,512]{2,1,0:T(8,128)(2,1)S(1)}, u32[]{:S(2)}, u32[]{:S(2)}) collective-permute-start(bf16[2,32,512]{2,1,0:T(8,128)(2,1)S(1)} %get-tuple-element.106), channel_id=1, source_target_pairs={{0,3},{1,2},{2,1},{3,0},{4,7},{5,6},{6,5},{7,4},{8,11},{9,10},{10,... | collective-permute-start | bytes 196616 | tf_op jit(solution)/shard_map/ppermute | solution.py:22
  16.4 1.3 copy.76
  17.7 2.6 %collective-permute-start.3 = (bf16[2,32,512]{2,1,0:T(8,128)(2,1)S(1)}, bf16[2,32,512]{2,1,0:T(8,128)(2,1)S(1)}, u32[]{:S(2)}, u32[]{:S(2)}) collective-permute-start(bf16[2,32,512]{2,1,0:T(8,128)(2,1)S(1)} %get-tuple-element.105), channel_id=1, source_target_pairs={{0,12},{1,13},{2,14},{3,15},{4,8},{5,9},{6,10},{7,11},{8,4},{9,5},... | collective-permute-start | bytes 196616 | tf_op jit(solution)/shard_map/ppermute | solution.py:22
  20.3 2.2 %collective-permute-done.3 = bf16[2,32,512]{2,1,0:T(8,128)(2,1)S(1)} collective-permute-done((bf16[2,32,512]{2,1,0:T(8,128)(2,1)S(1)}, bf16[2,32,512]{2,1,0:T(8,128)(2,1)S(1)}, u32[]{:S(2)}, u32[]{:S(2)}) %collective-permute-start.3) | collective-permute-done | bytes 65568 | tf_op jit(solution)/shard_map/ppermute | solution.py:22
  23.2 3.7 %collective-permute-done.4 = bf16[4,32,512]{2,1,0:T(8,128)(2,1)S(1)} collective-permute-done((bf16[4,32,512]{2,1,0:T(8,128)(2,1)S(1)}, bf16[4,32,512]{2,1,0:T(8,128)(2,1)S(1)}, u32[]{:S(2)}, u32[]{:S(2)}) %collective-permute-start.4) | collective-permute-done | bytes 131104 | tf_op jit(solution)/shard_map/ppermute | solution.py:22
  26.9 3.2 %collective-permute-start = (bf16[64,4,896]{2,1,0:T(4,128)(2,1)S(1)}, bf16[64,4,896]{2,1,0:T(4,128)(2,1)S(1)}, u32[]{:S(2)}, u32[]{:S(2)}) collective-permute-start(bf16[64,4,896]{2,1,0:T(4,128)(2,1)S(1)} %copy.34), channel_id=1, source_target_pairs={{0,16},{16,0},{32,48},{48,32},{64,80},{80,64},{96,112},{112,96},{1... | collective-permute-start | bytes 1376264 | tf_op jit(solution)/shard_map/ppermute | solution.py:30
  30.1 2.6 %collective-permute-start.12 = (bf16[8,32,512]{2,1,0:T(8,128)(2,1)S(1)}, bf16[8,32,512]{2,1,0:T(8,128)(2,1)S(1)}, u32[]{:S(2)}, u32[]{:S(2)}) collective-permute-start(bf16[8,32,512]{2,1,0:T(8,128)(2,1)S(1)} %pad_maximum_fusion.1.refs_6_), channel_id=1, source_target_pairs={{0,12},{1,13},{2,14},{3,15},{4,8},{5,9},{6,10},{7,11},{8,4},{9,5},... | collective-permute-start | bytes 786440 | tf_op jit(solution)/shard_map/ppermute | solution.py:22
  32.7 2.3 %collective-permute-done.10.refs_2_ = bf16[64,8192]{1,0:T(8,128)(2,1)} collective-permute-done((bf16[64,8192]{1,0:T(8,128)(2,1)}, bf16[64,8192]{1,0:T(8,128)(2,1)}, u32[]{:S(2)}, u32[]{:S(2)}) %collective-permute-start.10) | collective-permute-done | bytes 1048608 | tf_op jit(solution)/shard_map/ppermute | solution.py:26
  35.0 1.5 collective-permute-start.7
  36.5 2.0 %collective-permute-start.8 = (bf16[8,32,512]{2,1,0:T(8,128)(2,1)S(1)}, bf16[8,32,512]{2,1,0:T(8,128)(2,1)S(1)}, u32[]{:S(2)}, u32[]{:S(2)}) collective-permute-start(bf16[8,32,512]{2,1,0:T(8,128)(2,1)S(1)} %pad_maximum_fusion.2.refs_8_), channel_id=1, source_target_pairs={{0,16},{16,0},{32,48},{48,32},{64,80},{80,64},{96,112},{112,96},{1... | collective-permute-start | bytes 786440 | tf_op jit(solution)/shard_map/ppermute | solution.py:30
  39.1 1.0 collective-permute-start.9
  40.1 1.3 collective-permute-done.13.refs_9_
  41.4 1.2 collective-permute-start.14
  43.0 1.4 pad_maximum_fusion
  44.4 6.1 %all-to-all-start = ((bf16[64,8,896]{2,1,0:T(8,128)(2,1)}), bf16[64,8,896]{2,1,0:T(8,128)(2,1)S(1)}, u32[]{:S(2)}, u32[]{:S(2)}) async-start(bf16[64,8,896]{2,1,0:T(8,128)(2,1)} %pad_maximum_fusion), calls=%async_computation | async-start | bytes 1835008 | tf_op jit(solution)/shard_map/all_to_all | solution.py:368
  53.5 13.1 %policy_logits.1.policy_ref = f32[512,896]{1,0:T(8,128)} custom-call(bf16[64,8192]{1,0:T(8,128)(2,1)} %refs_0_.1, bf16[64,8192]{1,0:T(8,128)(2,1)} %collective-permute-done.9.refs_1_, bf16[64,8192]{1,0:T(8,128)(2,1)} %collective-permute-done.10.refs_2_, bf16[64,8192]{1,0:T(8,128)(2,1)} %collective-permute-done.11.refs_3_, ...), custom_call_target="tpu_custom_call" | custom-call | flops 458752 | bytes 458752 | tf_op jit(solution)/shard_map/policy_logits/pallas_call | solution.py:97
  66.7 1.5 copy-done
  68.2 2.4 %row_stats.1 = f32[8,512]{1,0:T(8,128)S(1)} custom-call(s32[512]{0:T(512)S(1)} %copy-done.3, f32[512,896]{1,0:T(8,128)S(1)} %copy-done, bf16[512,896]{1,0:T(8,128)(2,1)S(1)} %bitcast.199), custom_call_target="tpu_custom_call" | custom-call | flops 9175040 | bytes 2752512 | tf_op jit(solution)/shard_map/row_stats/pallas_call | solution.py:152
  70.5 2.5 %collective-permute-start.20 = (f32[8,512]{1,0:T(8,128)S(1)}, f32[8,512]{1,0:T(8,128)S(1)}, u32[]{:S(2)}, u32[]{:S(2)}) collective-permute-start(f32[8,512]{1,0:T(8,128)S(1)} %row_stats.1), channel_id=1, source_target_pairs={{0,3},{1,2},{2,1},{3,0},{4,7},{5,6},{6,5},{7,4},{8,11},{9,10},{10,... | collective-permute-start | bytes 49160 | tf_op jit(solution)/shard_map/ppermute | solution.py:22
  74.4 2.7 %collective-permute-done.19 = f32[8,512]{1,0:T(8,128)S(1)} collective-permute-done((f32[8,512]{1,0:T(8,128)S(1)}, f32[8,512]{1,0:T(8,128)S(1)}, u32[]{:S(2)}, u32[]{:S(2)}) %collective-permute-start.19) | collective-permute-done | bytes 16416 | tf_op jit(solution)/shard_map/ppermute | solution.py:22
  77.4 2.4 %collective-permute-start.23 = (f32[8,512]{1,0:T(8,128)S(1)}, f32[8,512]{1,0:T(8,128)S(1)}, u32[]{:S(2)}, u32[]{:S(2)}) collective-permute-start(f32[8,512]{1,0:T(8,128)S(1)} %stack.182), channel_id=1, source_target_pairs={{0,12},{1,13},{2,14},{3,15},{4,8},{5,9},{6,10},{7,11},{8,4},{9,5},... | collective-permute-start | bytes 49160 | tf_op jit(solution)/shard_map/ppermute | solution.py:22
  81.2 2.7 %collective-permute-done.22 = f32[8,512]{1,0:T(8,128)S(1)} collective-permute-done((f32[8,512]{1,0:T(8,128)S(1)}, f32[8,512]{1,0:T(8,128)S(1)}, u32[]{:S(2)}, u32[]{:S(2)}) %collective-permute-start.22) | collective-permute-done | bytes 16416 | tf_op jit(solution)/shard_map/ppermute | solution.py:22
  84.2 2.7 %collective-permute-start.26 = (f32[8,512]{1,0:T(8,128)S(1)}, f32[8,512]{1,0:T(8,128)S(1)}, u32[]{:S(2)}, u32[]{:S(2)}) collective-permute-start(f32[8,512]{1,0:T(8,128)S(1)} %stack.195), channel_id=1, source_target_pairs={{0,96},{16,112},{32,64},{48,80},{64,32},{80,48},{96,0},{112,16},{1... | collective-permute-start | bytes 49160 | tf_op jit(solution)/shard_map/ppermute | solution.py:26
  88.0 2.9 %collective-permute-done.25 = f32[8,512]{1,0:T(8,128)S(1)} collective-permute-done((f32[8,512]{1,0:T(8,128)S(1)}, f32[8,512]{1,0:T(8,128)S(1)}, u32[]{:S(2)}, u32[]{:S(2)}) %collective-permute-start.25) | collective-permute-done | bytes 16416 | tf_op jit(solution)/shard_map/ppermute | solution.py:26
  91.2 4.7 %collective-permute-start.27 = (f32[8,512]{1,0:T(8,128)S(1)}, f32[8,512]{1,0:T(8,128)S(1)}, u32[]{:S(2)}, u32[]{:S(2)}) collective-permute-start(f32[8,512]{1,0:T(8,128)S(1)} %stack.208), channel_id=1, source_target_pairs={{0,16},{16,0},{32,48},{48,32},{64,80},{80,64},{96,112},{112,96},{1... | collective-permute-start | bytes 49160 | tf_op jit(solution)/shard_map/ppermute | solution.py:30
  96.9 2.1 %logit_grads.1 = (bf16[512,896]{1,0:T(8,128)(2,1)S(1)}, f32[8,128]{1,0:T(8,128)S(1)}) custom-call(f32[8,512]{1,0:T(8,128)S(1)} %stack.219.stats_ref, s32[512]{0:T(512)S(1)} %copy-done.3, s32[512]{0:T(512)S(1)} %copy-done.4, s32[512]{0:T(512)S(1)} %copy-done.5, f32[512,896]{1,0:T(8,128)S(1)} %copy-done.1, bf16[512,896]{1,0:T(8,128)(2,1)S(1)} %bitcast.200), custom_call_target="tpu_custom_call" | custom-call | flops 469762048 | bytes 4587520 | tf_op jit(solution)/shard_map/logit_grads/pallas_call | solution.py:239
  99.6 2.1 %collective-permute-done.28.other_grad = bf16[512,896]{1,0:T(8,128)(2,1)S(1)} collective-permute-done((bf16[512,896]{1,0:T(8,128)(2,1)S(1)}, bf16[512,896]{1,0:T(8,128)(2,1)S(1)}, u32[]{:S(2)}, u32[]{:S(2)}) %collective-permute-start.28) | collective-permute-done | bytes 917536 | tf_op jit(solution)/shard_map/ppermute | solution.py:30
  102.7 12.5 %hidden_parts.1 = (bf16[256,1024]{1,0:T(8,128)(2,1)S(1)}, bf16[256,1024]{1,0:T(8,128)(2,1)S(1)}, bf16[256,1024]{1,0:T(8,128)(2,1)S(1)}, bf16[256,1024]{1,0:T(8,1...) custom-call(bf16[512,896]{1,0:T(8,128)(2,1)} %copy-done.2, ...), custom_call_target="tpu_custom_call" | custom-call | flops 7516192768 | bytes 26214400 | tf_op jit(solution)/shard_map/hidden_parts/pallas_call | solution.py:308
  115.3 2.0 %collective-permute-start.31 = (bf16[256,1024]{1,0:T(8,128)(2,1)S(1)}, bf16[256,1024]{1,0:T(8,128)(2,1)S(1)}, u32[]{:S(2)}, u32[]{:S(2)}) collective-permute-start(bf16[256,1024]{1,0:T(8,128)(2,1)S(1)} %get-tuple-element.52), channel_id=1, source_target_pairs={{0,12},{1,13},{2,14},{3,15},{4,8},{5,9},{6,10},{7,11},{8,4},{9,5},... | collective-permute-start | bytes 1572872 | tf_op jit(solution)/shard_map/ppermute | solution.py:22
  117.3 2.0 %collective-permute-start.38 = (bf16[256,1024]{1,0:T(8,128)(2,1)S(1)}, bf16[256,1024]{1,0:T(8,128)(2,1)S(1)}, u32[]{:S(2)}, u32[]{:S(2)}) collective-permute-start(bf16[256,1024]{1,0:T(8,128)(2,1)S(1)} %get-tuple-element.56), channel_id=1, source_target_pairs={{0,3},{1,2},{2,1},{3,0},{4,7},{5,6},{6,5},{7,4},{8,11},{9,10},{10,... | collective-permute-start | bytes 1572872 | tf_op jit(solution)/shard_map/ppermute | solution.py:22
  119.3 9.1 %collective-permute-done.29 = bf16[256,1024]{1,0:T(8,128)(2,1)S(1)} collective-permute-done((bf16[256,1024]{1,0:T(8,128)(2,1)S(1)}, bf16[256,1024]{1,0:T(8,128)(2,1)S(1)}, u32[]{:S(2)}, u32[]{:S(2)}) %collective-permute-start.29) | collective-permute-done | bytes 524320 | tf_op jit(solution)/shard_map/ppermute | solution.py:22
  128.5 1.2 collective-permute-start.30
  130.3 1.2 collective-permute-start.37
  131.9 4.5 %collective-permute-done.30 = bf16[128,1024]{1,0:T(8,128)(2,1)S(1)} collective-permute-done((bf16[128,1024]{1,0:T(8,128)(2,1)S(1)}, bf16[128,1024]{1,0:T(8,128)(2,1)S(1)}, u32[]{:S(2)}, u32[]{:S(2)}) %collective-permute-start.30) | collective-permute-done | bytes 262176 | tf_op jit(solution)/shard_map/ppermute | solution.py:22
  136.8 1.2 collective-permute-start.35
  138.3 2.4 %collective-permute-start.33 = (bf16[32,2048]{1,0:T(8,128)(2,1)S(1)}, bf16[32,2048]{1,0:T(8,128)(2,1)S(1)}, u32[]{:S(2)}, u32[]{:S(2)}) collective-permute-start(bf16[32,2048]{1,0:T(8,128)(2,1)S(1)} %get-tuple-element.96), channel_id=1, source_target_pairs={{0,2},{1,3},{2,0},{3,1},{4,6},{5,7},{6,4},{7,5},{8,10},{9,11},{10,... | collective-permute-start | bytes 393224 | tf_op jit(solution)/shard_map/ppermute | solution.py:22
  141.0 1.3 collective-permute-start.42
  142.3 2.6 %collective-permute-start.40 = (bf16[32,2048]{1,0:T(8,128)(2,1)S(1)}, bf16[32,2048]{1,0:T(8,128)(2,1)S(1)}, u32[]{:S(2)}, u32[]{:S(2)}) collective-permute-start(bf16[32,2048]{1,0:T(8,128)(2,1)S(1)} %get-tuple-element.99), channel_id=1, source_target_pairs={{0,8},{1,9},{2,10},{3,11},{4,12},{5,13},{6,14},{7,15},{8,0},{9,1},... | collective-permute-start | bytes 393224 | tf_op jit(solution)/shard_map/ppermute | solution.py:22
  145.0 1.4 collective-permute-done.42
  146.4 2.3 %collective-permute-done.40 = bf16[32,2048]{1,0:T(8,128)(2,1)S(1)} collective-permute-done((bf16[32,2048]{1,0:T(8,128)(2,1)S(1)}, bf16[32,2048]{1,0:T(8,128)(2,1)S(1)}, u32[]{:S(2)}, u32[]{:S(2)}) %collective-permute-start.40) | collective-permute-done | bytes 131104 | tf_op jit(solution)/shard_map/ppermute | solution.py:22
  148.9 1.1 collective-permute-start.45
  150.4 2.4 %collective-permute-start.43 = (bf16[8,4096]{1,0:T(8,128)(2,1)S(1)}, bf16[8,4096]{1,0:T(8,128)(2,1)S(1)}, u32[]{:S(2)}, u32[]{:S(2)}) collective-permute-start(bf16[8,4096]{1,0:T(8,128)(2,1)S(1)} %get-tuple-element.102), channel_id=1, source_target_pairs={{0,64},{16,80},{32,96},{48,112},{64,0},{80,16},{96,32},{112,48},{1... | collective-permute-start | bytes 196616 | tf_op jit(solution)/shard_map/ppermute | solution.py:26
  153.3 1.9 %collective-permute-done.43 = bf16[8,4096]{1,0:T(8,128)(2,1)S(1)} collective-permute-done((bf16[8,4096]{1,0:T(8,128)(2,1)S(1)}, bf16[8,4096]{1,0:T(8,128)(2,1)S(1)}, u32[]{:S(2)}, u32[]{:S(2)}) %collective-permute-start.43) | collective-permute-done | bytes 65568 | tf_op jit(solution)/shard_map/ppermute | solution.py:26
  155.3 5.9 %collective-permute-start.46 = (bf16[4,4096]{1,0:T(4,128)(2,1)S(1)}, bf16[4,4096]{1,0:T(4,128)(2,1)S(1)}, u32[]{:S(2)}, u32[]{:S(2)}) collective-permute-start(bf16[4,4096]{1,0:T(4,128)(2,1)S(1)} %get-tuple-element.108), channel_id=1, source_target_pairs={{0,16},{16,0},{32,48},{48,32},{64,80},{80,64},{96,112},{112,96},{1... | collective-permute-start | bytes 98312 | tf_op jit(solution)/shard_map/ppermute | solution.py:30
  (119 shorter events, 18.3 us)
Async XLA Ops:
  0.6 29.5 %collective-permute-start.6 = (bf16[8192,896]{1,0:T(8,128)(2,1)}, bf16[8192,896]{1,0:T(8,128)(2,1)}, u32[]{:S(2)}, u32[]{:S(2)}) collective-permute-start(bf16[8192,896]{1,0:T(8,128)(2,1)} %own_weight.1), channel_id=1, source_target_pairs={{0,16},{16,0},{32,48},{48,32},{64,80},{80,64},{96,112},{112,96},{1... | collective-permute-start | bytes 44040200 | tf_op jit(solution)/shard_map/ppermute | solution.py:30
  3.0 7.6 %collective-permute-start.1 = (bf16[4,32,512]{2,1,0:T(8,128)(2,1)S(1)}, bf16[4,32,512]{2,1,0:T(8,128)(2,1)S(1)}, u32[]{:S(2)}, u32[]{:S(2)}) collective-permute-start(bf16[4,32,512]{2,1,0:T(8,128)(2,1)S(1)} %pad_maximum_fusion.5), channel_id=1, source_target_pairs={{0,64},{16,80},{32,96},{48,112},{64,0},{80,16},{96,32},{112,48},{1... | collective-permute-start | bytes 393224 | tf_op jit(solution)/shard_map/ppermute | solution.py:26
  10.6 24.4 %collective-permute-start.10 = (bf16[64,8192]{1,0:T(8,128)(2,1)}, bf16[64,8192]{1,0:T(8,128)(2,1)}, u32[]{:S(2)}, u32[]{:S(2)}) collective-permute-start(bf16[64,8192]{1,0:T(8,128)(2,1)} %refs_0_.1), channel_id=1, source_target_pairs={{0,32},{16,48},{32,0},{48,16},{64,96},{80,112},{96,64},{112,80},{1... | collective-permute-start | bytes 3145736 | tf_op jit(solution)/shard_map/ppermute | solution.py:26
  11.4 25.1 %collective-permute-start.11 = (bf16[64,8192]{1,0:T(8,128)(2,1)}, bf16[64,8192]{1,0:T(8,128)(2,1)}, u32[]{:S(2)}, u32[]{:S(2)}) collective-permute-start(bf16[64,8192]{1,0:T(8,128)(2,1)} %refs_0_.1), channel_id=1, source_target_pairs={{0,96},{16,112},{32,64},{48,80},{64,32},{80,48},{96,0},{112,16},{1... | collective-permute-start | bytes 3145736 | tf_op jit(solution)/shard_map/ppermute | solution.py:26
  13.6 6.7 %collective-permute-start.2 = (bf16[2,32,512]{2,1,0:T(8,128)(2,1)S(1)}, bf16[2,32,512]{2,1,0:T(8,128)(2,1)S(1)}, u32[]{:S(2)}, u32[]{:S(2)}) collective-permute-start(bf16[2,32,512]{2,1,0:T(8,128)(2,1)S(1)} %get-tuple-element.106), channel_id=1, source_target_pairs={{0,3},{1,2},{2,1},{3,0},{4,7},{5,6},{6,5},{7,4},{8,11},{9,10},{10,... | collective-permute-start | bytes 196616 | tf_op jit(solution)/shard_map/ppermute | solution.py:22
  17.7 4.8 %collective-permute-start.3 = (bf16[2,32,512]{2,1,0:T(8,128)(2,1)S(1)}, bf16[2,32,512]{2,1,0:T(8,128)(2,1)S(1)}, u32[]{:S(2)}, u32[]{:S(2)}) collective-permute-start(bf16[2,32,512]{2,1,0:T(8,128)(2,1)S(1)} %get-tuple-element.105), channel_id=1, source_target_pairs={{0,12},{1,13},{2,14},{3,15},{4,8},{5,9},{6,10},{7,11},{8,4},{9,5},... | collective-permute-start | bytes 196616 | tf_op jit(solution)/shard_map/ppermute | solution.py:22
  22.6 4.3 %collective-permute-start.4 = (bf16[4,32,512]{2,1,0:T(8,128)(2,1)S(1)}, bf16[4,32,512]{2,1,0:T(8,128)(2,1)S(1)}, u32[]{:S(2)}, u32[]{:S(2)}) collective-permute-start(bf16[4,32,512]{2,1,0:T(8,128)(2,1)S(1)} %pad_maximum_fusion.6), channel_id=1, source_target_pairs={{0,4},{1,5},{2,6},{3,7},{4,0},{5,1},{6,2},{7,3},{8,12},{9,13},{10,... | collective-permute-start | bytes 393224 | tf_op jit(solution)/shard_map/ppermute | solution.py:22
  22.7 7.4 %collective-permute-start.5 = (bf16[4,32,512]{2,1,0:T(8,128)(2,1)S(1)}, bf16[4,32,512]{2,1,0:T(8,128)(2,1)S(1)}, u32[]{:S(2)}, u32[]{:S(2)}) collective-permute-start(bf16[4,32,512]{2,1,0:T(8,128)(2,1)S(1)} %pad_maximum_fusion.7), channel_id=1, source_target_pairs={{0,1},{1,0},{2,3},{3,2},{4,5},{5,4},{6,7},{7,6},{8,9},{9,8},{10,11... | collective-permute-start | bytes 393224 | tf_op jit(solution)/shard_map/ppermute | solution.py:22
  26.9 15.7 %collective-permute-start = (bf16[64,4,896]{2,1,0:T(4,128)(2,1)S(1)}, bf16[64,4,896]{2,1,0:T(4,128)(2,1)S(1)}, u32[]{:S(2)}, u32[]{:S(2)}) collective-permute-start(bf16[64,4,896]{2,1,0:T(4,128)(2,1)S(1)} %copy.34), channel_id=1, source_target_pairs={{0,16},{16,0},{32,48},{48,32},{64,80},{80,64},{96,112},{112,96},{1... | collective-permute-start | bytes 1376264 | tf_op jit(solution)/shard_map/ppermute | solution.py:30
  30.1 9.0 %collective-permute-start.12 = (bf16[8,32,512]{2,1,0:T(8,128)(2,1)S(1)}, bf16[8,32,512]{2,1,0:T(8,128)(2,1)S(1)}, u32[]{:S(2)}, u32[]{:S(2)}) collective-permute-start(bf16[8,32,512]{2,1,0:T(8,128)(2,1)S(1)} %pad_maximum_fusion.1.refs_6_), channel_id=1, source_target_pairs={{0,12},{1,13},{2,14},{3,15},{4,8},{5,9},{6,10},{7,11},{8,4},{9,5},... | collective-permute-start | bytes 786440 | tf_op jit(solution)/shard_map/ppermute | solution.py:22
  32.7 8.8 %collective-permute-start.13 = (bf16[8,32,512]{2,1,0:T(8,128)(2,1)S(1)}, bf16[8,32,512]{2,1,0:T(8,128)(2,1)S(1)}, u32[]{:S(2)}, u32[]{:S(2)}) collective-permute-start(bf16[8,32,512]{2,1,0:T(8,128)(2,1)S(1)} %pad_maximum_fusion.2.refs_8_), channel_id=1, source_target_pairs={{0,3},{1,2},{2,1},{3,0},{4,7},{5,6},{6,5},{7,4},{8,11},{9,10},{10,... | collective-permute-start | bytes 786440 | tf_op jit(solution)/shard_map/ppermute | solution.py:22
  35.0 9.4 %collective-permute-start.7 = (bf16[8,32,512]{2,1,0:T(8,128)(2,1)S(1)}, bf16[8,32,512]{2,1,0:T(8,128)(2,1)S(1)}, u32[]{:S(2)}, u32[]{:S(2)}) collective-permute-start(bf16[8,32,512]{2,1,0:T(8,128)(2,1)S(1)} %pad_maximum_fusion.1.refs_6_), channel_id=1, source_target_pairs={{0,16},{16,0},{32,48},{48,32},{64,80},{80,64},{96,112},{112,96},{1... | collective-permute-start | bytes 786440 | tf_op jit(solution)/shard_map/ppermute | solution.py:30
  36.5 7.9 %collective-permute-start.8 = (bf16[8,32,512]{2,1,0:T(8,128)(2,1)S(1)}, bf16[8,32,512]{2,1,0:T(8,128)(2,1)S(1)}, u32[]{:S(2)}, u32[]{:S(2)}) collective-permute-start(bf16[8,32,512]{2,1,0:T(8,128)(2,1)S(1)} %pad_maximum_fusion.2.refs_8_), channel_id=1, source_target_pairs={{0,16},{16,0},{32,48},{48,32},{64,80},{80,64},{96,112},{112,96},{1... | collective-permute-start | bytes 786440 | tf_op jit(solution)/shard_map/ppermute | solution.py:30
  39.1 12.5 %collective-permute-start.9 = (bf16[64,8192]{1,0:T(8,128)(2,1)}, bf16[64,8192]{1,0:T(8,128)(2,1)}, u32[]{:S(2)}, u32[]{:S(2)}) collective-permute-start(bf16[64,8192]{1,0:T(8,128)(2,1)} %refs_0_.1), channel_id=1, source_target_pairs={{0,16},{16,0},{32,48},{48,32},{64,80},{80,64},{96,112},{112,96},{1... | collective-permute-start | bytes 3145736 | tf_op jit(solution)/shard_map/ppermute | solution.py:30
  41.4 11.4 %collective-permute-start.14 = (bf16[64,8192]{1,0:T(8,128)(2,1)}, bf16[64,8192]{1,0:T(8,128)(2,1)}, u32[]{:S(2)}, u32[]{:S(2)}) collective-permute-start(bf16[64,8192]{1,0:T(8,128)(2,1)} %collective-permute-done.10.refs_2_), channel_id=1, source_target_pairs={{0,16},{16,0},{32,48},{48,32},{64,80},{80,64},{96,112},{112,96},{1... | collective-permute-start | bytes 3145736 | tf_op jit(solution)/shard_map/ppermute | solution.py:30
  42.6 10.2 %collective-permute-start.15 = (bf16[64,8192]{1,0:T(8,128)(2,1)}, bf16[64,8192]{1,0:T(8,128)(2,1)}, u32[]{:S(2)}, u32[]{:S(2)}) collective-permute-start(bf16[64,8192]{1,0:T(8,128)(2,1)} %collective-permute-done.11.refs_3_), channel_id=1, source_target_pairs={{0,16},{16,0},{32,48},{48,32},{64,80},{80,64},{96,112},{112,96},{1... | collective-permute-start | bytes 3145736 | tf_op jit(solution)/shard_map/ppermute | solution.py:30
  44.4 22.3 %all-to-all-start = ((bf16[64,8,896]{2,1,0:T(8,128)(2,1)}), bf16[64,8,896]{2,1,0:T(8,128)(2,1)S(1)}, u32[]{:S(2)}, u32[]{:S(2)}) async-start(bf16[64,8,896]{2,1,0:T(8,128)(2,1)} %pad_maximum_fusion), calls=%async_computation | async-start | bytes 1835008 | tf_op jit(solution)/shard_map/all_to_all | solution.py:368
  50.5 1.9 %collective-permute-start.16 = (bf16[8,32,512]{2,1,0:T(8,128)(2,1)S(1)}, bf16[8,32,512]{2,1,0:T(8,128)(2,1)S(1)}, u32[]{:S(2)}, u32[]{:S(2)}) collective-permute-start(bf16[8,32,512]{2,1,0:T(8,128)(2,1)S(1)} %collective-permute-done.12.refs_7_), channel_id=1, source_target_pairs={{0,16},{16,0},{32,48},{48,32},{64,80},{80,64},{96,112},{112,96},{1... | collective-permute-start | bytes 786440 | tf_op jit(solution)/shard_map/ppermute | solution.py:30
  51.3 1.5 collective-permute-start.17
  70.5 3.9 %collective-permute-start.20 = (f32[8,512]{1,0:T(8,128)S(1)}, f32[8,512]{1,0:T(8,128)S(1)}, u32[]{:S(2)}, u32[]{:S(2)}) collective-permute-start(f32[8,512]{1,0:T(8,128)S(1)} %row_stats.1), channel_id=1, source_target_pairs={{0,3},{1,2},{2,1},{3,0},{4,7},{5,6},{6,5},{7,4},{8,11},{9,10},{10,... | collective-permute-start | bytes 49160 | tf_op jit(solution)/shard_map/ppermute | solution.py:22
  73.0 4.1 %collective-permute-start.19 = (f32[8,512]{1,0:T(8,128)S(1)}, f32[8,512]{1,0:T(8,128)S(1)}, u32[]{:S(2)}, u32[]{:S(2)}) collective-permute-start(f32[8,512]{1,0:T(8,128)S(1)} %row_stats.1), channel_id=1, source_target_pairs={{0,2},{1,3},{2,0},{3,1},{4,6},{5,7},{6,4},{7,5},{8,10},{9,11},{10,... | collective-permute-start | bytes 49160 | tf_op jit(solution)/shard_map/ppermute | solution.py:22
  73.6 3.6 %collective-permute-start.18 = (f32[8,512]{1,0:T(8,128)S(1)}, f32[8,512]{1,0:T(8,128)S(1)}, u32[]{:S(2)}, u32[]{:S(2)}) collective-permute-start(f32[8,512]{1,0:T(8,128)S(1)} %row_stats.1), channel_id=1, source_target_pairs={{0,1},{1,0},{2,3},{3,2},{4,5},{5,4},{6,7},{7,6},{8,9},{9,8},{10,11... | collective-permute-start | bytes 49160 | tf_op jit(solution)/shard_map/ppermute | solution.py:22
  77.4 3.9 %collective-permute-start.23 = (f32[8,512]{1,0:T(8,128)S(1)}, f32[8,512]{1,0:T(8,128)S(1)}, u32[]{:S(2)}, u32[]{:S(2)}) collective-permute-start(f32[8,512]{1,0:T(8,128)S(1)} %stack.182), channel_id=1, source_target_pairs={{0,12},{1,13},{2,14},{3,15},{4,8},{5,9},{6,10},{7,11},{8,4},{9,5},... | collective-permute-start | bytes 49160 | tf_op jit(solution)/shard_map/ppermute | solution.py:22
  79.8 4.2 %collective-permute-start.22 = (f32[8,512]{1,0:T(8,128)S(1)}, f32[8,512]{1,0:T(8,128)S(1)}, u32[]{:S(2)}, u32[]{:S(2)}) collective-permute-start(f32[8,512]{1,0:T(8,128)S(1)} %stack.182), channel_id=1, source_target_pairs={{0,8},{1,9},{2,10},{3,11},{4,12},{5,13},{6,14},{7,15},{8,0},{9,1},... | collective-permute-start | bytes 49160 | tf_op jit(solution)/shard_map/ppermute | solution.py:22
  80.4 3.6 %collective-permute-start.21 = (f32[8,512]{1,0:T(8,128)S(1)}, f32[8,512]{1,0:T(8,128)S(1)}, u32[]{:S(2)}, u32[]{:S(2)}) collective-permute-start(f32[8,512]{1,0:T(8,128)S(1)} %stack.182), channel_id=1, source_target_pairs={{0,4},{1,5},{2,6},{3,7},{4,0},{5,1},{6,2},{7,3},{8,12},{9,13},{10,... | collective-permute-start | bytes 49160 | tf_op jit(solution)/shard_map/ppermute | solution.py:22
  84.2 3.9 %collective-permute-start.26 = (f32[8,512]{1,0:T(8,128)S(1)}, f32[8,512]{1,0:T(8,128)S(1)}, u32[]{:S(2)}, u32[]{:S(2)}) collective-permute-start(f32[8,512]{1,0:T(8,128)S(1)} %stack.195), channel_id=1, source_target_pairs={{0,96},{16,112},{32,64},{48,80},{64,32},{80,48},{96,0},{112,16},{1... | collective-permute-start | bytes 49160 | tf_op jit(solution)/shard_map/ppermute | solution.py:26
  86.9 4.1 %collective-permute-start.25 = (f32[8,512]{1,0:T(8,128)S(1)}, f32[8,512]{1,0:T(8,128)S(1)}, u32[]{:S(2)}, u32[]{:S(2)}) collective-permute-start(f32[8,512]{1,0:T(8,128)S(1)} %stack.195), channel_id=1, source_target_pairs={{0,64},{16,80},{32,96},{48,112},{64,0},{80,16},{96,32},{112,48},{1... | collective-permute-start | bytes 49160 | tf_op jit(solution)/shard_map/ppermute | solution.py:26
  87.2 3.7 %collective-permute-start.24 = (f32[8,512]{1,0:T(8,128)S(1)}, f32[8,512]{1,0:T(8,128)S(1)}, u32[]{:S(2)}, u32[]{:S(2)}) collective-permute-start(f32[8,512]{1,0:T(8,128)S(1)} %stack.195), channel_id=1, source_target_pairs={{0,32},{16,48},{32,0},{48,16},{64,96},{80,112},{96,64},{112,80},{1... | collective-permute-start | bytes 49160 | tf_op jit(solution)/shard_map/ppermute | solution.py:26
  91.2 5.6 %collective-permute-start.27 = (f32[8,512]{1,0:T(8,128)S(1)}, f32[8,512]{1,0:T(8,128)S(1)}, u32[]{:S(2)}, u32[]{:S(2)}) collective-permute-start(f32[8,512]{1,0:T(8,128)S(1)} %stack.208), channel_id=1, source_target_pairs={{0,16},{16,0},{32,48},{48,32},{64,80},{80,64},{96,112},{112,96},{1... | collective-permute-start | bytes 49160 | tf_op jit(solution)/shard_map/ppermute | solution.py:30
  99.0 2.8 %collective-permute-start.28 = (bf16[512,896]{1,0:T(8,128)(2,1)S(1)}, bf16[512,896]{1,0:T(8,128)(2,1)S(1)}, u32[]{:S(2)}, u32[]{:S(2)}) collective-permute-start(bf16[512,896]{1,0:T(8,128)(2,1)S(1)} %get-tuple-element.47.own_grad), channel_id=1, source_target_pairs={{0,16},{16,0},{32,48},{48,32},{64,80},{80,64},{96,112},{112,96},{1... | collective-permute-start | bytes 2752520 | tf_op jit(solution)/shard_map/ppermute | solution.py:30
  115.2 13.2 %collective-permute-start.29 = (bf16[256,1024]{1,0:T(8,128)(2,1)S(1)}, bf16[256,1024]{1,0:T(8,128)(2,1)S(1)}, u32[]{:S(2)}, u32[]{:S(2)}) collective-permute-start(bf16[256,1024]{1,0:T(8,128)(2,1)S(1)} %get-tuple-element.50), channel_id=1, source_target_pairs={{0,4},{1,5},{2,6},{3,7},{4,0},{5,1},{6,2},{7,3},{8,12},{9,13},{10,... | collective-permute-start | bytes 1572872 | tf_op jit(solution)/shard_map/ppermute | solution.py:22
  115.3 14.4 %collective-permute-start.31 = (bf16[256,1024]{1,0:T(8,128)(2,1)S(1)}, bf16[256,1024]{1,0:T(8,128)(2,1)S(1)}, u32[]{:S(2)}, u32[]{:S(2)}) collective-permute-start(bf16[256,1024]{1,0:T(8,128)(2,1)S(1)} %get-tuple-element.52), channel_id=1, source_target_pairs={{0,12},{1,13},{2,14},{3,15},{4,8},{5,9},{6,10},{7,11},{8,4},{9,5},... | collective-permute-start | bytes 1572872 | tf_op jit(solution)/shard_map/ppermute | solution.py:22
  117.3 12.9 %collective-permute-start.36 = (bf16[256,1024]{1,0:T(8,128)(2,1)S(1)}, bf16[256,1024]{1,0:T(8,128)(2,1)S(1)}, u32[]{:S(2)}, u32[]{:S(2)}) collective-permute-start(bf16[256,1024]{1,0:T(8,128)(2,1)S(1)} %get-tuple-element.54), channel_id=1, source_target_pairs={{0,1},{1,0},{2,3},{3,2},{4,5},{5,4},{6,7},{7,6},{8,9},{9,8},{10,11... | collective-permute-start | bytes 1572872 | tf_op jit(solution)/shard_map/ppermute | solution.py:22
  117.3 14.2 %collective-permute-start.38 = (bf16[256,1024]{1,0:T(8,128)(2,1)S(1)}, bf16[256,1024]{1,0:T(8,128)(2,1)S(1)}, u32[]{:S(2)}, u32[]{:S(2)}) collective-permute-start(bf16[256,1024]{1,0:T(8,128)(2,1)S(1)} %get-tuple-element.56), channel_id=1, source_target_pairs={{0,3},{1,2},{2,1},{3,0},{4,7},{5,6},{6,5},{7,4},{8,11},{9,10},{10,... | collective-permute-start | bytes 1572872 | tf_op jit(solution)/shard_map/ppermute | solution.py:22
  128.5 7.9 %collective-permute-start.30 = (bf16[128,1024]{1,0:T(8,128)(2,1)S(1)}, bf16[128,1024]{1,0:T(8,128)(2,1)S(1)}, u32[]{:S(2)}, u32[]{:S(2)}) collective-permute-start(bf16[128,1024]{1,0:T(8,128)(2,1)S(1)} %add_convert_fusion.7), channel_id=1, source_target_pairs={{0,12},{1,13},{2,14},{3,15},{4,8},{5,9},{6,10},{7,11},{8,4},{9,5},... | collective-permute-start | bytes 786440 | tf_op jit(solution)/shard_map/ppermute | solution.py:22
  129.8 6.8 %collective-permute-start.32 = (bf16[128,1024]{1,0:T(8,128)(2,1)S(1)}, bf16[128,1024]{1,0:T(8,128)(2,1)S(1)}, u32[]{:S(2)}, u32[]{:S(2)}) collective-permute-start(bf16[128,1024]{1,0:T(8,128)(2,1)S(1)} %add_convert_fusion.5), channel_id=1, source_target_pairs={{0,4},{1,5},{2,6},{3,7},{4,0},{5,1},{6,2},{7,3},{8,12},{9,13},{10,... | collective-permute-start | bytes 786440 | tf_op jit(solution)/shard_map/ppermute | solution.py:22
  130.3 10.4 %collective-permute-start.37 = (bf16[128,1024]{1,0:T(8,128)(2,1)S(1)}, bf16[128,1024]{1,0:T(8,128)(2,1)S(1)}, u32[]{:S(2)}, u32[]{:S(2)}) collective-permute-start(bf16[128,1024]{1,0:T(8,128)(2,1)S(1)} %add_convert_fusion.3), channel_id=1, source_target_pairs={{0,3},{1,2},{2,1},{3,0},{4,7},{5,6},{6,5},{7,4},{8,11},{9,10},{10,... | collective-permute-start | bytes 786440 | tf_op jit(solution)/shard_map/ppermute | solution.py:22
  131.6 9.3 %collective-permute-start.39 = (bf16[128,1024]{1,0:T(8,128)(2,1)S(1)}, bf16[128,1024]{1,0:T(8,128)(2,1)S(1)}, u32[]{:S(2)}, u32[]{:S(2)}) collective-permute-start(bf16[128,1024]{1,0:T(8,128)(2,1)S(1)} %add_convert_fusion.1), channel_id=1, source_target_pairs={{0,1},{1,0},{2,3},{3,2},{4,5},{5,4},{6,7},{7,6},{8,9},{9,8},{10,11... | collective-permute-start | bytes 786440 | tf_op jit(solution)/shard_map/ppermute | solution.py:22
  136.8 5.6 %collective-permute-start.35 = (bf16[32,2048]{1,0:T(8,128)(2,1)S(1)}, bf16[32,2048]{1,0:T(8,128)(2,1)S(1)}, u32[]{:S(2)}, u32[]{:S(2)}) collective-permute-start(bf16[32,2048]{1,0:T(8,128)(2,1)S(1)} %get-tuple-element.97), channel_id=1, source_target_pairs={{0,3},{1,2},{2,1},{3,0},{4,7},{5,6},{6,5},{7,4},{8,11},{9,10},{10,... | collective-permute-start | bytes 393224 | tf_op jit(solution)/shard_map/ppermute | solution.py:22
  138.0 7.0 %collective-permute-start.34 = (bf16[32,2048]{1,0:T(8,128)(2,1)S(1)}, bf16[32,2048]{1,0:T(8,128)(2,1)S(1)}, u32[]{:S(2)}, u32[]{:S(2)}) collective-permute-start(bf16[32,2048]{1,0:T(8,128)(2,1)S(1)} %get-tuple-element.98), channel_id=1, source_target_pairs={{0,1},{1,0},{2,3},{3,2},{4,5},{5,4},{6,7},{7,6},{8,9},{9,8},{10,11... | collective-permute-start | bytes 393224 | tf_op jit(solution)/shard_map/ppermute | solution.py:22
  138.3 6.7 %collective-permute-start.33 = (bf16[32,2048]{1,0:T(8,128)(2,1)S(1)}, bf16[32,2048]{1,0:T(8,128)(2,1)S(1)}, u32[]{:S(2)}, u32[]{:S(2)}) collective-permute-start(bf16[32,2048]{1,0:T(8,128)(2,1)S(1)} %get-tuple-element.96), channel_id=1, source_target_pairs={{0,2},{1,3},{2,0},{3,1},{4,6},{5,7},{6,4},{7,5},{8,10},{9,11},{10,... | collective-permute-start | bytes 393224 | tf_op jit(solution)/shard_map/ppermute | solution.py:22
  141.0 5.4 %collective-permute-start.42 = (bf16[32,2048]{1,0:T(8,128)(2,1)S(1)}, bf16[32,2048]{1,0:T(8,128)(2,1)S(1)}, u32[]{:S(2)}, u32[]{:S(2)}) collective-permute-start(bf16[32,2048]{1,0:T(8,128)(2,1)S(1)} %get-tuple-element.100), channel_id=1, source_target_pairs={{0,12},{1,13},{2,14},{3,15},{4,8},{5,9},{6,10},{7,11},{8,4},{9,5},... | collective-permute-start | bytes 393224 | tf_op jit(solution)/shard_map/ppermute | solution.py:22
  142.3 4.1 %collective-permute-start.41 = (bf16[32,2048]{1,0:T(8,128)(2,1)S(1)}, bf16[32,2048]{1,0:T(8,128)(2,1)S(1)}, u32[]{:S(2)}, u32[]{:S(2)}) collective-permute-start(bf16[32,2048]{1,0:T(8,128)(2,1)S(1)} %get-tuple-element.101), channel_id=1, source_target_pairs={{0,4},{1,5},{2,6},{3,7},{4,0},{5,1},{6,2},{7,3},{8,12},{9,13},{10,... | collective-permute-start | bytes 393224 | tf_op jit(solution)/shard_map/ppermute | solution.py:22
  142.3 6.4 %collective-permute-start.40 = (bf16[32,2048]{1,0:T(8,128)(2,1)S(1)}, bf16[32,2048]{1,0:T(8,128)(2,1)S(1)}, u32[]{:S(2)}, u32[]{:S(2)}) collective-permute-start(bf16[32,2048]{1,0:T(8,128)(2,1)S(1)} %get-tuple-element.99), channel_id=1, source_target_pairs={{0,8},{1,9},{2,10},{3,11},{4,12},{5,13},{6,14},{7,15},{8,0},{9,1},... | collective-permute-start | bytes 393224 | tf_op jit(solution)/shard_map/ppermute | solution.py:22
  148.9 4.4 %collective-permute-start.45 = (bf16[8,4096]{1,0:T(8,128)(2,1)S(1)}, bf16[8,4096]{1,0:T(8,128)(2,1)S(1)}, u32[]{:S(2)}, u32[]{:S(2)}) collective-permute-start(bf16[8,4096]{1,0:T(8,128)(2,1)S(1)} %get-tuple-element.103), channel_id=1, source_target_pairs={{0,96},{16,112},{32,64},{48,80},{64,32},{80,48},{96,0},{112,16},{1... | collective-permute-start | bytes 196616 | tf_op jit(solution)/shard_map/ppermute | solution.py:26
  150.0 3.3 %collective-permute-start.44 = (bf16[8,4096]{1,0:T(8,128)(2,1)S(1)}, bf16[8,4096]{1,0:T(8,128)(2,1)S(1)}, u32[]{:S(2)}, u32[]{:S(2)}) collective-permute-start(bf16[8,4096]{1,0:T(8,128)(2,1)S(1)} %get-tuple-element.104), channel_id=1, source_target_pairs={{0,32},{16,48},{32,0},{48,16},{64,96},{80,112},{96,64},{112,80},{1... | collective-permute-start | bytes 196616 | tf_op jit(solution)/shard_map/ppermute | solution.py:26
  150.4 4.8 %collective-permute-start.43 = (bf16[8,4096]{1,0:T(8,128)(2,1)S(1)}, bf16[8,4096]{1,0:T(8,128)(2,1)S(1)}, u32[]{:S(2)}, u32[]{:S(2)}) collective-permute-start(bf16[8,4096]{1,0:T(8,128)(2,1)S(1)} %get-tuple-element.102), channel_id=1, source_target_pairs={{0,64},{16,80},{32,96},{48,112},{64,0},{80,16},{96,32},{112,48},{1... | collective-permute-start | bytes 196616 | tf_op jit(solution)/shard_map/ppermute | solution.py:26
  155.3 6.8 %collective-permute-start.46 = (bf16[4,4096]{1,0:T(4,128)(2,1)S(1)}, bf16[4,4096]{1,0:T(4,128)(2,1)S(1)}, u32[]{:S(2)}, u32[]{:S(2)}) collective-permute-start(bf16[4,4096]{1,0:T(4,128)(2,1)S(1)} %get-tuple-element.108), channel_id=1, source_target_pairs={{0,16},{16,0},{32,48},{48,32},{64,80},{80,64},{96,112},{112,96},{1... | collective-permute-start | bytes 98312 | tf_op jit(solution)/shard_map/ppermute | solution.py:30
  (9 other events, 124.6 us)
